TPU v7x, 32 devices: a whole 2x2x4 slice. The times are simulated.
32 devices in a mesh: dp: 8 (over y, x, core), tensor: 4 (over z).
Axes of the slice: x: 2, y: 2, z: 4, core: 2. Of those that a mesh axis runs over, the one named last changes fastest.
Arguments:
- hidden_in: bfloat16 [16384, 768], P(('dp', 'tensor')), may hold values from -6 to 6
- lengths: int32 [128], P('dp'), may hold values from 96 to 128, as said below
- span_start: int32 [128], P('dp'), may hold values from 1 to 63
- span_len: int32 [128], P('dp'), may hold values from 2 to 17
- mask_embed: bfloat16 [768], replicated, may hold values from -6 to 6
- w_query: bfloat16 [768, 768], P(None, 'tensor'), may hold values from -0.21875 to 0.21875
- b_query: bfloat16 [768], P('tensor'), may hold values from -3 to 3
- w_key: bfloat16 [768, 768], P(None, 'tensor'), may hold values from -0.21875 to 0.21875
- w_value: bfloat16 [768, 768], P(None, 'tensor'), may hold values from -0.21875 to 0.21875
- b_value: bfloat16 [768], P('tensor'), may hold values from -3 to 3
- w_out: bfloat16 [768, 768], P('tensor'), may hold values from -1.25 to 1.25
- b_out: bfloat16 [768], replicated, may hold values from -3 to 3
- g_attn: bfloat16 [768], replicated, may hold values from 0.25 to 1.75
- s_attn: bfloat16 [768], replicated, may hold values from -2 to 2
- w_in: bfloat16 [768, 3072], P(None, 'tensor'), may hold values from -0.21875 to 0.21875
- b_in: bfloat16 [3072], P('tensor'), may hold values from -3 to 3
- w_back: bfloat16 [3072, 768], P('tensor'), may hold values from -0.15625 to 0.15625
- b_back: bfloat16 [768], replicated, may hold values from -3 to 3
- g_ffn: bfloat16 [768], replicated, may hold values from 0.25 to 1.75
- s_ffn: bfloat16 [768], replicated, may hold values from -2 to 2
- cotangent: bfloat16 [16384, 768], P(('dp', 'tensor')), may hold values from -6 to 6
Outputs:
- layer_out: bfloat16 [16384, 768], P(('dp', 'tensor'))
- grad_input: bfloat16 [16384, 768], P(('dp', 'tensor'))
- grad_mask_embed: float32 [768], replicated
- grad_w_query: float32 [768, 768], P(None, 'tensor')
- grad_b_query: float32 [768], P('tensor')
- grad_w_key: float32 [768, 768], P(None, 'tensor')
- grad_w_value: float32 [768, 768], P(None, 'tensor')
- grad_b_value: float32 [768], P('tensor')
- grad_w_out: float32 [768, 768], P('tensor')
- grad_b_out: float32 [768], replicated
- grad_g_attn: float32 [768], replicated
- grad_s_attn: float32 [768], replicated
- grad_w_in: float32 [768, 3072], P(None, 'tensor')
- grad_b_in: float32 [3072], P('tensor')
- grad_w_back: float32 [3072, 768], P('tensor')
- grad_b_back: float32 [768], replicated
- grad_g_ffn: float32 [768], replicated
- grad_s_ffn: float32 [768], replicated
Inputs may be any that keep to these rules, and one draw needn't show every extreme that they name: `lengths`: real residues of each chain; one chain of the whole batch has all 128 positions real, and every chain's masked span lies within its real residues.
All inputs are finite; a program needn't handle non-finite values.
Results may differ from a plain program's by a relative error of at most 0.02.
Values may be sent and summed in bfloat16 or wider, within the bound.
No kernel may reach another device: no remote copies, remote signals or barrier semaphores. Data moves between devices by JAX's collectives and lax.ppermute only.
A program may use at most 128 MiB of HBM per device.

v0:
```python
import jax
import jax.numpy as jnp
from jax import lax
from jax.sharding import PartitionSpec as P

HEAD_DIM = 64
CHAIN_BLOCK = 4
CH = 16


EPSILON = 1e-05
MASKED = -1000000000.0


def layer_norm(values, scale_vec, shift_vec):
    row_mean = jnp.mean(values, axis=-1, keepdims=True)
    centred = values - row_mean
    row_var = jnp.mean(centred * centred, axis=-1, keepdims=True)
    return centred * lax.rsqrt(row_var + EPSILON) * scale_vec + shift_vec


def gelu_exact(values):
    return jax.nn.gelu(values, approximate=False)


def masked_scores(queries, key_vecs, visible):
    score_scale = queries.shape[-1] ** (-0.5)
    scores = (
        jnp.einsum("cqhd,ckhd->chqk", queries, key_vecs, preferred_element_type=jnp.float32)
        * score_scale
    )
    return (jnp.where(visible[:, None, None, :], scores, MASKED), score_scale)


def attend_block(block_in):
    queries, key_vecs, value_vecs, visible = block_in
    scores, score_scale = masked_scores(queries, key_vecs, visible)
    row_max = jnp.max(scores, axis=-1, keepdims=True)
    shifted = jnp.exp(scores - row_max)
    row_sum = jnp.sum(shifted, axis=-1, keepdims=True)
    weights = (shifted / row_sum).astype(jnp.bfloat16)
    context = jnp.einsum("chqk,ckhd->cqhd", weights, value_vecs, preferred_element_type=jnp.float32)
    return (context.astype(jnp.bfloat16), (row_max + jnp.log(row_sum))[..., 0])


def attend_back(block_in):
    queries, key_vecs, value_vecs, visible, log_total, grad_ctx = block_in
    scores, score_scale = masked_scores(queries, key_vecs, visible)
    attention = jnp.exp(scores - log_total[..., None])
    grad_value = jnp.einsum(
        "chqk,cqhd->ckhd",
        attention.astype(jnp.bfloat16),
        grad_ctx,
        preferred_element_type=jnp.float32,
    )
    grad_weights = jnp.einsum(
        "cqhd,ckhd->chqk", grad_ctx, value_vecs, preferred_element_type=jnp.float32
    )
    row_dot = jnp.sum(attention * grad_weights, axis=-1, keepdims=True)
    grad_scores = (attention * (grad_weights - row_dot)).astype(jnp.bfloat16)
    grad_query = (
        jnp.einsum("chqk,ckhd->cqhd", grad_scores, key_vecs, preferred_element_type=jnp.float32)
        * score_scale
    )
    grad_key = (
        jnp.einsum("chqk,cqhd->ckhd", grad_scores, queries, preferred_element_type=jnp.float32)
        * score_scale
    )
    return (
        grad_query.astype(jnp.bfloat16),
        grad_key.astype(jnp.bfloat16),
        grad_value.astype(jnp.bfloat16),
    )


def on_device(
    hidden_in,
    lengths,
    span_start,
    span_len,
    mask_embed,
    w_query,
    b_query,
    w_key,
    w_value,
    b_value,
    w_out,
    b_out,
    g_attn,
    s_attn,
    w_in,
    b_in,
    w_back,
    b_back,
    g_ffn,
    s_ffn,
    cotangent,
):
    group_size = lax.axis_size("tensor")
    tensor_rank = lax.axis_index("tensor")
    local_rows = hidden_in.shape[0]
    chain_count = lengths.shape[0]
    group_rows = local_rows * group_size
    seq_len = group_rows // chain_count
    width_mine = w_query.shape[1]
    local_heads = width_mine // HEAD_DIM
    position = jnp.arange(seq_len, dtype=jnp.int32)
    visible = position[None, :] < lengths[:, None]
    span_end = span_start + span_len
    in_span = (
        (position[None, :] >= span_start[:, None]) & (position[None, :] < span_end[:, None])
    ).reshape(group_rows)
    span_mine = lax.dynamic_slice_in_dim(in_span, tensor_rank * local_rows, local_rows)
    mixed_in = jnp.where(span_mine[:, None], mask_embed[None, :], hidden_in)
    inputs_full = lax.all_gather(mixed_in, "tensor", axis=0, tiled=True)
    proj_mats = jnp.concatenate((w_query, w_key, w_value), axis=1)
    projected = jnp.dot(inputs_full, proj_mats, preferred_element_type=jnp.float32)
    queries = (projected[:, :width_mine] + b_query.astype(jnp.float32)).astype(jnp.bfloat16)
    key_vecs = projected[:, width_mine : 2 * width_mine].astype(jnp.bfloat16)
    value_vecs = (projected[:, 2 * width_mine :] + b_value.astype(jnp.float32)).astype(jnp.bfloat16)
    block_chains = min(CHAIN_BLOCK, CH)
    block_count = chain_count // block_chains
    shape_five = (block_count, block_chains, seq_len, local_heads, HEAD_DIM)
    visible_blocks = visible.reshape(block_count, block_chains, seq_len)
    blocked = (
        queries.reshape(shape_five),
        key_vecs.reshape(shape_five),
        value_vecs.reshape(shape_five),
        visible_blocks,
    )
    context, log_total = lax.map(attend_block, blocked)
    context = context.reshape(group_rows, width_mine)
    attn_rows = lax.psum_scatter(
        jnp.dot(context, w_out, preferred_element_type=jnp.float32),
        "tensor",
        scatter_dimension=0,
        tiled=True,
    )
    first_sum = mixed_in.astype(jnp.float32) + attn_rows + b_out.astype(jnp.float32)
    normed, norm_pull_one = jax.vjp(
        layer_norm, first_sum, g_attn.astype(jnp.float32), s_attn.astype(jnp.float32)
    )
    normed_low = normed.astype(jnp.bfloat16)
    normed_full = lax.all_gather(normed_low, "tensor", axis=0, tiled=True)
    pre_act = jnp.dot(normed_full, w_in, preferred_element_type=jnp.float32) + b_in.astype(
        jnp.float32
    )
    activated, gelu_pull = jax.vjp(gelu_exact, pre_act)
    activated = activated.astype(jnp.bfloat16)
    ffn_rows = lax.psum_scatter(
        jnp.dot(activated, w_back, preferred_element_type=jnp.float32),
        "tensor",
        scatter_dimension=0,
        tiled=True,
    )
    second_sum = normed + ffn_rows + b_back.astype(jnp.float32)
    layer_out, norm_pull_two = jax.vjp(
        layer_norm, second_sum, g_ffn.astype(jnp.float32), s_ffn.astype(jnp.float32)
    )
    grad_second, grad_g_ffn, grad_s_ffn = norm_pull_two(cotangent.astype(jnp.float32))
    grad_b_back = jnp.sum(grad_second, axis=0)
    ffn_grad_full = lax.all_gather(grad_second.astype(jnp.bfloat16), "tensor", axis=0, tiled=True)
    grad_w_back = jnp.einsum(
        "tf,td->fd", activated, ffn_grad_full, preferred_element_type=jnp.float32
    )
    grad_act = jnp.einsum("td,fd->tf", ffn_grad_full, w_back, preferred_element_type=jnp.float32)
    grad_pre = gelu_pull(grad_act)[0].astype(jnp.bfloat16)
    grad_w_in = jnp.einsum("td,tf->df", normed_full, grad_pre, preferred_element_type=jnp.float32)
    grad_b_in = jnp.sum(grad_pre, axis=0, dtype=jnp.float32)
    grad_normed = (
        lax.psum_scatter(
            jnp.einsum("tf,df->td", grad_pre, w_in, preferred_element_type=jnp.float32).astype(
                jnp.bfloat16
            ),
            "tensor",
            scatter_dimension=0,
            tiled=True,
        ).astype(jnp.float32)
        + grad_second
    )
    grad_first, grad_g_attn, grad_s_attn = norm_pull_one(grad_normed)
    grad_b_out = jnp.sum(grad_first, axis=0)
    attn_grad_full = lax.all_gather(grad_first.astype(jnp.bfloat16), "tensor", axis=0, tiled=True)
    grad_w_out = jnp.einsum(
        "tc,td->cd", context, attn_grad_full, preferred_element_type=jnp.float32
    )
    grad_ctx = jnp.einsum(
        "td,cd->tc", attn_grad_full, w_out, preferred_element_type=jnp.float32
    ).astype(jnp.bfloat16)
    grad_query_blocks, grad_key_blocks, grad_value_blocks = lax.map(
        attend_back, blocked + (log_total, grad_ctx.reshape(shape_five))
    )
    grad_proj = jnp.concatenate(
        (
            grad_query_blocks.reshape(group_rows, width_mine),
            grad_key_blocks.reshape(group_rows, width_mine),
            grad_value_blocks.reshape(group_rows, width_mine),
        ),
        axis=1,
    )
    grad_proj_mats = jnp.einsum(
        "td,te->de", inputs_full, grad_proj, preferred_element_type=jnp.float32
    )
    proj_sums = jnp.sum(grad_proj, axis=0, dtype=jnp.float32)
    grad_w_query = grad_proj_mats[:, :width_mine]
    grad_w_key = grad_proj_mats[:, width_mine : 2 * width_mine]
    grad_w_value = grad_proj_mats[:, 2 * width_mine :]
    grad_b_query = proj_sums[:width_mine]
    grad_b_value = proj_sums[2 * width_mine :]
    grad_mixed = (
        lax.psum_scatter(
            jnp.einsum(
                "te,de->td", grad_proj, proj_mats, preferred_element_type=jnp.float32
            ).astype(jnp.bfloat16),
            "tensor",
            scatter_dimension=0,
            tiled=True,
        ).astype(jnp.float32)
        + grad_first
    )
    grad_input = jnp.where(span_mine[:, None], 0.0, grad_mixed).astype(jnp.bfloat16)
    grad_embed = jnp.sum(jnp.where(span_mine[:, None], grad_mixed, 0.0), axis=0)
    (
        grad_w_query,
        grad_b_query,
        grad_w_key,
        grad_w_value,
        grad_b_value,
        grad_w_out,
        grad_w_back,
        grad_w_in,
        grad_b_in,
    ) = lax.psum(
        (
            grad_w_query,
            grad_b_query,
            grad_w_key,
            grad_w_value,
            grad_b_value,
            grad_w_out,
            grad_w_back,
            grad_w_in,
            grad_b_in,
        ),
        "dp",
    )
    grad_embed, grad_b_out, grad_g_attn, grad_s_attn, grad_b_back, grad_g_ffn, grad_s_ffn = (
        lax.psum(
            (grad_embed, grad_b_out, grad_g_attn, grad_s_attn, grad_b_back, grad_g_ffn, grad_s_ffn),
            ("dp", "tensor"),
        )
    )
    return (
        layer_out.astype(jnp.bfloat16),
        grad_input,
        grad_embed,
        grad_w_query,
        grad_b_query,
        grad_w_key,
        grad_w_value,
        grad_b_value,
        grad_w_out,
        grad_b_out,
        grad_g_attn,
        grad_s_attn,
        grad_w_in,
        grad_b_in,
        grad_w_back,
        grad_b_back,
        grad_g_ffn,
        grad_s_ffn,
    )


def solution(mesh):
    placed = (
        P(("dp", "tensor"), None),
        P("dp"),
        P("dp"),
        P("dp"),
        P(),
        P(None, "tensor"),
        P("tensor"),
        P(None, "tensor"),
        P(None, "tensor"),
        P("tensor"),
        P("tensor", None),
        P(),
        P(),
        P(),
        P(None, "tensor"),
        P("tensor"),
        P("tensor", None),
        P(),
        P(),
        P(),
        P(("dp", "tensor"), None),
    )
    return jax.shard_map(
        on_device,
        mesh=mesh,
        in_specs=placed,
        out_specs=(
            P(("dp", "tensor"), None),
            P(("dp", "tensor"), None),
            P(),
            P(None, "tensor"),
            P("tensor"),
            P(None, "tensor"),
            P(None, "tensor"),
            P("tensor"),
            P("tensor", None),
            P(),
            P(),
            P(),
            P(None, "tensor"),
            P("tensor"),
            P("tensor", None),
            P(),
            P(),
            P(),
        ),
        check_vma=False,
    )
```

profile of v0, /device:TPU:0, one launch (start us, length us, event | category | flops | bytes accessed | tf_op | source)
XLA Modules:
  0.0 879.6 jit_solution(12868973838429662114)
XLA Ops:
  14.3 63.1 %all-gather.5.cloned.1.call-done = bf16[2048,768]{1,0:T(8,128)(2,1)} async-done(((bf16[512,768]{1,0:T(8,128)(2,1)}), bf16[2048,768]{1,0:T(8,128)(2,1)}) %all-gather.5.cloned.1.call-update) | async-done | bytes 3145744 | tf_op jit(solution)/shard_map/all_gather | solution.py:115
  77.4 3.9 fusion.62
  91.5 8.8 while.26
  103.1 4.9 fusion.63
  108.7 108.9 %reduce-scatter.5.cloned.1.call-done = f32[512,768]{1,0:T(8,128)} async-done(((f32[2048,768]{1,0:T(8,128)}), f32[512,768]{1,0:T(8,128)}) %reduce-scatter.5.cloned.1.call-update) | async-done | bytes 1572880 | tf_op jit(solution)/shard_map/reduce_scatter | solution.py:133
  223.1 62.9 %all-gather.7.cloned.1.call-done = bf16[2048,768]{1,0:T(8,128)(2,1)} async-done(((bf16[512,768]{1,0:T(8,128)(2,1)}), bf16[2048,768]{1,0:T(8,128)(2,1)}) %all-gather.7.cloned.1.call-update) | async-done | bytes 3145744 | tf_op jit(solution)/shard_map/all_gather | solution.py:144
  286.0 18.4 %multiply_convert_fusion.1 = (bf16[2048,768]{1,0:T(8,128)(2,1)S(1)}, f32[2048,768]{1,0:T(8,128)}, f32[2048,768]{1,0:T(8,128)}) fusion(f32[768]{0:T(1024)S(1)} %convert_element_type.124, bf16[2048,768]{1,0:T(8,128)(2,1)} %all-gather.7.cloned.1.call-done, bf16[768,768]{1,0:T(8,128)(2,1)S(1)} %copy-done), kind=kOutput, calls=%fused_computation.60 | convolution fusion | flops 2519728128 | bytes 20057088 | tf_op jit(solution)/shard_map/dot_general | solution.py:145
  306.2 4.5 fusion.64
  313.9 106.3 %reduce-scatter.7.cloned.1.call-done = f32[512,768]{1,0:T(8,128)} async-done(((f32[2048,768]{1,0:T(8,128)}), f32[512,768]{1,0:T(8,128)}) %reduce-scatter.7.cloned.1.call-update) | async-done | bytes 1572880 | tf_op jit(solution)/shard_map/reduce_scatter | solution.py:150
  427.8 64.0 %all-gather.9.cloned.1.call-done = bf16[2048,768]{1,0:T(8,128)(2,1)} async-done(((bf16[512,768]{1,0:T(8,128)(2,1)}), bf16[2048,768]{1,0:T(8,128)(2,1)}) %all-gather.9.cloned.1.call-update) | async-done | bytes 3145744 | tf_op jit(solution)/shard_map/all_gather | solution.py:162
  491.8 11.0 %convert_reduce_fusion = (f32[768]{0:T(1024)}, bf16[2048,768]{1,0:T(8,128)(2,1)S(1)}) fusion(f32[2048,768]{1,0:T(8,128)} %get-tuple-element.217, f32[2048,768]{1,0:T(8,128)} %get-tuple-element.235, f32[768]{0:T(1024)} %copy-done.36, bf16[2048,768]{1,0:T(8,128)(2,1)} %all-gather.9.cloned.1.call-done, bf16[768,768]{1,0:T(8,128)(2,1)} %param.41), kind=kOutput, calls=%fused_computation.58 | convolution fusion | flops 2442657024 | bytes 20060160 | tf_op jit(solution)/shard_map/td,fd->tf/dot_general | solution.py:166
  504.5 4.0 convolution_convert_fusion.2
  508.5 59.0 %reduce-scatter.9.cloned.1.call-done = bf16[512,768]{1,0:T(8,128)(2,1)} async-done(((bf16[2048,768]{1,0:T(8,128)(2,1)}), bf16[512,768]{1,0:T(8,128)(2,1)}) %reduce-scatter.9.cloned.1.call-update) | async-done | bytes 786448 | tf_op jit(solution)/shard_map/reduce_scatter | solution.py:171
  567.6 3.2 multiply_reduce_fusion.1
  574.8 63.4 %all-gather.11.cloned.1.call-done = bf16[2048,768]{1,0:T(8,128)(2,1)} async-done(((bf16[512,768]{1,0:T(8,128)(2,1)}), bf16[2048,768]{1,0:T(8,128)(2,1)}) %all-gather.11.cloned.1.call-update) | async-done | bytes 3145744 | tf_op jit(solution)/shard_map/all_gather | solution.py:183
  638.3 3.9 convolution_convert_fusion.4
  647.9 24.6 %while.27 = (s32[]{:T(128)}, bf16[4,4,128,3,64]{2,1,0,4,3:T(4,128)(2,1)}, bf16[4,4,128,3,64]{2,1,0,4,3:T(4,128)(2,1)}, bf16[4,4,128,3,64]{2,1,0,4,3:T(4,128)(2,1...) while((s32[]{:T(128)}, ...), condition=%wide.region_17.18_spmd, body=%wide.region_15.17_spmd.sunk | while | flops 128088576 | bytes 9472661 | solution.py:190
  678.3 6.0 convolution_convert_fusion.3
  684.7 7.1 fusion.66
  691.7 4.2 fusion.67
  703.5 14.4 %all-reduce.1 = (f32[192]{0:T(256)}, f32[192]{0:T(256)}, f32[768]{0:T(1024)}) all-reduce(f32[192]{0:T(256)S(1)} %get-tuple-element.234, f32[192]{0:T(256)S(1)} %get-tuple-element.233, f32[768]{0:T(1024)S(1)} %copy-done.35), channel_id=1, replica_groups=mesh['dp'=8,'tensor'=4] {'dp'}, use_global_device_ids=true, to_apply=%region_23.24 | all-reduce | flops 1152 | bytes 9216 | tf_op jit(solution)/shard_map/psum | solution.py:233
  717.9 25.5 %reduce-scatter.11.cloned.1.call-done = bf16[512,768]{1,0:T(8,128)(2,1)} async-done(((bf16[2048,768]{1,0:T(8,128)(2,1)}), bf16[512,768]{1,0:T(8,128)(2,1)}) %reduce-scatter.11.cloned.1.call-update) | async-done | bytes 786448 | tf_op jit(solution)/shard_map/reduce_scatter | solution.py:211
  745.9 41.7 %all-reduce = (f32[768]{0:T(1024)}, f32[768]{0:T(1024)}, f32[768]{0:T(1024)}, f32[768]{0:T(1024)}, f32[768]{0:T(1024)}, /*index=5*/f32[768]{0:T(1024)}, f32[768]{0:T(1024)}) all-reduce(f32[768]{0:T(1024)S(1)} %get-tuple-element.156, f32[768]{0:T(1024)S(1)} %get-tuple-element.155, ...), channel_id=1, replica_groups=mesh['dp'=8,'tensor'=4] {'dp','tensor'}, use_global_device_ids=true, to_apply=%region_20.21 | all-reduce | flops 5376 | bytes 43008 | tf_op jit(solution)/shard_map/psum | solution.py:248
  787.6 75.7 %all-reduce.5.cloned.1.call-done = (f32[768,192]{0,1:T(8,128)}, f32[768,192]{0,1:T(8,128)}, f32[768,192]{0,1:T(8,128)}, f32[192,768]{1,0:T(8,128)}, f32[768,768]{1,0:T(8,128)}, /*index=5*/f32[768,768]{1,0:T(8,128)}) async-done(((f32[768,192]{0,1:T(8,128)}, f32[768,192]{0,1:T(8,128)}, f32[768,192]{0,1:T(8,128)}, f32[192,768]{1,0:T(8,128)}, f32[768,768]{1,0:T(8,128)}, /*index=5*/f32[768,768]{1,0:T(8,128)}), ...) | async-done | bytes 7077904 | tf_op jit(solution)/shard_map/psum | solution.py:233
  (251 shorter events, 108.8 us)
Async XLA Ops:
  7.2 278.8 %copy-start = (bf16[768,768]{1,0:T(8,128)(2,1)S(1)}, bf16[768,768]{1,0:T(8,128)(2,1)}, u32[]{:S(2)}) copy-start(bf16[768,768]{1,0:T(8,128)(2,1)} %param.39) | copy-start | bytes 3538948
  7.2 70.2 %all-gather.5.cloned.1.call-start = ((), (), s32[]{:S(2)}) async-start(), calls=%async_computation.4 | async-start | bytes 3932160 | tf_op jit(solution)/shard_map/all_gather | solution.py:115
  11.1 206.5 %reduce-scatter.5.cloned.1.call-start = ((), (), s32[]{:S(2)}) async-start(), calls=%async_computation.5 | async-start | bytes 7864320 | tf_op jit(solution)/shard_map/reduce_scatter | solution.py:133
  14.2 63.2 %copy-start.22 = (bf16[768,576]{0,1:T(8,128)(2,1)}, bf16[768,576]{0,1:T(8,128)(2,1)S(1)}, u32[]{:S(2)}) copy-start(bf16[768,576]{0,1:T(8,128)(2,1)S(1)} %constant_dynamic-update-slice_fusion) | copy-start | bytes 2654212
  108.0 109.6 %copy-start.32 = (bf16[768]{0:T(1024)(128)(2,1)S(1)}, bf16[768]{0:T(1024)(128)(2,1)}, u32[]{:S(2)}) copy-start(bf16[768]{0:T(1024)(128)(2,1)} %param.29) | copy-start | bytes 4612
  108.0 178.0 %all-gather.7.cloned.1.call-start = ((), (), s32[]{:S(2)}) async-start(), calls=%async_computation.6 | async-start | bytes 3932160 | tf_op jit(solution)/shard_map/all_gather | solution.py:144
  108.7 113.1 %copy-start.24 = (f32[768]{0:T(1024)}, f32[768]{0:T(1024)S(1)}, u32[]{:S(2)}) copy-start(f32[768]{0:T(1024)S(1)} %convert_element_type.122) | copy-start | bytes 9220
  221.8 198.4 %reduce-scatter.7.cloned.1.call-start = ((), (), s32[]{:S(2)}) async-start(), calls=%async_computation.7 | async-start | bytes 7864320 | tf_op jit(solution)/shard_map/reduce_scatter | solution.py:150
  223.1 81.4 %copy-start.36 = (f32[768]{0:T(1024)}, f32[768]{0:T(1024)S(1)}, u32[]{:S(2)}) copy-start(f32[768]{0:T(1024)S(1)} %convert_element_type.124) | copy-start | bytes 9220
  286.0 20.2 %copy-start.44 = (bf16[768,768]{1,0:T(8,128)(2,1)S(1)}, bf16[768,768]{1,0:T(8,128)(2,1)}, u32[]{:S(2)}) copy-start(bf16[768,768]{1,0:T(8,128)(2,1)} %param.41) | copy-start | bytes 3538948
  310.6 181.2 %all-gather.9.cloned.1.call-start = ((), (), s32[]{:S(2)}) async-start(), calls=%async_computation.8 | async-start | bytes 3932160 | tf_op jit(solution)/shard_map/all_gather | solution.py:162
  427.6 139.9 %reduce-scatter.9.cloned.1.call-start = ((), (), s32[]{:S(2)}) async-start(), calls=%async_computation.9 | async-start | bytes 3932160 | tf_op jit(solution)/shard_map/reduce_scatter | solution.py:171
  508.5 129.8 %all-gather.11.cloned.1.call-start = ((), (), s32[]{:S(2)}) async-start(), calls=%async_computation.10 | async-start | bytes 3932160 | tf_op jit(solution)/shard_map/all_gather | solution.py:183
  572.4 65.9 %copy-start.19 = (bf16[192,768]{1,0:T(8,128)(2,1)S(1)}, bf16[192,768]{1,0:T(8,128)(2,1)}, u32[]{:S(2)}) copy-start(bf16[192,768]{1,0:T(8,128)(2,1)} %param.35) | copy-start | bytes 884740
  574.6 168.8 %reduce-scatter.11.cloned.1.call-start = ((), (), s32[]{:S(2)}) async-start(), calls=%async_computation.11 | async-start | bytes 3932160 | tf_op jit(solution)/shard_map/reduce_scatter | solution.py:211
  684.3 179.0 %all-reduce.5.cloned.1.call-start = ((), (), s32[]{:S(2)}) async-start(), calls=%async_computation.12 | async-start | bytes 14155776 | tf_op jit(solution)/shard_map/psum | solution.py:233
  684.6 7.1 copy-start.43
  701.2 42.2 %copy-start.6 = (f32[512,768]{1,0:T(8,128)S(1)}, f32[512,768]{1,0:T(8,128)}, u32[]{:S(2)}) copy-start(f32[512,768]{1,0:T(8,128)} %copy-done.5) | copy-start | bytes 4718596
  701.2 42.2 %copy-start.34 = (pred[512]{0:T(512)(128)(4,1)S(1)}, pred[512]{0:T(512)(128)(4,1)}, u32[]{:S(2)}) copy-start(pred[512]{0:T(512)(128)(4,1)} %copy-done.33) | copy-start | bytes 1540
  701.2 44.7 %copy-start.26 = (f32[768]{0:T(1024)S(1)}, f32[768]{0:T(1024)}, u32[]{:S(2)}) copy-start(f32[768]{0:T(1024)} %get-tuple-element.151) | copy-start | bytes 9220
  701.3 44.6 %copy-start.27 = (f32[768]{0:T(1024)S(1)}, f32[768]{0:T(1024)}, u32[]{:S(2)}) copy-start(f32[768]{0:T(1024)} %get-tuple-element.157) | copy-start | bytes 9220
  701.3 44.6 %copy-start.29 = (f32[768]{0:T(1024)S(1)}, f32[768]{0:T(1024)}, u32[]{:S(2)}) copy-start(f32[768]{0:T(1024)} %get-tuple-element.149) | copy-start | bytes 9220
  701.3 44.6 %copy-start.30 = (f32[768]{0:T(1024)S(1)}, f32[768]{0:T(1024)}, u32[]{:S(2)}) copy-start(f32[768]{0:T(1024)} %get-tuple-element.153) | copy-start | bytes 9220
  701.3 44.6 %copy-start.31 = (f32[768]{0:T(1024)S(1)}, f32[768]{0:T(1024)}, u32[]{:S(2)}) copy-start(f32[768]{0:T(1024)} %get-tuple-element.154) | copy-start | bytes 9220
  (33 other events, 108.2 us)
Sparse Core Ops, SparseCore 0:
  11.2 66.1 all-gather.4
  108.1 109.3 reduce-scatter.4
  221.9 64.0 all-gather.6
  310.8 109.3 reduce-scatter.6
  427.7 64.0 all-gather.8
  508.6 58.8 reduce-scatter.8
  574.7 63.5 all-gather.10
  684.5 58.8 reduce-scatter.10
  748.6 114.6 all-reduce.4
where the time goes:
time: 888 us; the launch traced here: 880 us
  waiting for transfers between devices  629 us (71%)
  matrix products  84.6 us (10%)
  local copies, waits for them, and re-layouts  60.6 us (7%)
  blocking collectives  56.1 us (6%)
  other arithmetic  33 us (4%)
  between operations  14.6 us (2%)
    reduce_scatter x1, waiting for transfers between devices, on_device(): lax.psum_scatter(jnp.dot(context, w_out, preferred_element_type=jnp.float...  109 us
    reduce_scatter x1, waiting for transfers between devices, on_device(): lax.psum_scatter(jnp.dot(activated, w_back, preferred_element_type=jnp.fl...  106 us
    psum x1, waiting for transfers between devices, on_device(): lax.psum((grad_w_query, grad_b_query, grad_w_key, grad_w_value, grad_b_va...  75.7 us
    all_gather x1, waiting for transfers between devices, on_device(): lax.all_gather(grad_second.astype(jnp.bfloat16), 'tensor', axis=0, tiled=...  64 us
    all_gather x1, waiting for transfers between devices, on_device(): lax.all_gather(grad_first.astype(jnp.bfloat16), 'tensor', axis=0, tiled=T...  63.4 us
    all_gather x1, waiting for transfers between devices, on_device(): inputs_full = lax.all_gather(mixed_in, 'tensor', axis=0, tiled=True)  63.1 us
    all_gather x1, waiting for transfers between devices, on_device(): normed_full = lax.all_gather(normed_low, 'tensor', axis=0, tiled=True)  62.9 us
    reduce_scatter x1, waiting for transfers between devices, on_device(): lax.psum_scatter(jnp.einsum('tf,df->td', grad_pre, w_in, preferred_elemen...  59 us
  transfers between devices with their start and end apart: 9, of which 9 were waited for; matrix products, arithmetic and copies ran while one was open for 3% of the time, Pallas kernels for 0%

commit v1 on v0

v1 whole, which is shorter than its diff:
```python
import functools

import jax
import jax.numpy as jnp
from jax import lax
from jax.experimental import pallas as pl
from jax.experimental.pallas import tpu as pltpu
from jax.sharding import PartitionSpec as P

HEAD_DIM = 64
EPSILON = 1e-05
MASKED = -1000000000.0
AXES = ("dp", "tensor")
BF = jnp.bfloat16
F32 = jnp.float32
MIB = 1024 * 1024
BIAS_ROWS = 16


class Moves:
    def __init__(self, dp_size, group):
        self.dp_size, self.group = dp_size, group

    def build(self, source):
        pairs = []
        for d in range(self.dp_size):
            for t in range(self.group):
                sd, st = source(d, t)
                pairs.append((sd * self.group + st, d * self.group + t))
        return lambda value: lax.ppermute(value, AXES, pairs)

    def core(self, value):
        return self.build(lambda d, t: (d ^ 1, t))(value)

    def near(self, value):
        return self.build(lambda d, t: (d ^ (4 if d & 1 else 2), t))(value)

    def far(self, value):
        return self.build(lambda d, t: (d ^ (2 if d & 1 else 4), t))(value)

    def fetch(self, value, turn):
        return self.build(lambda d, t: (d, (t + turn) % self.group))(value)

    def give(self, value, turn):
        return self.build(lambda d, t: (d, (t - turn) % self.group))(value)

    def flip(self, value, mask_dp, mask_t):
        return self.build(lambda d, t: (d ^ mask_dp, t ^ mask_t))(value)


def spread(moves, mine):
    rows = mine.shape[0]
    other = moves.core(mine)
    near = moves.near(jnp.concatenate((mine, other), axis=0))
    far = moves.far(near[:rows])
    near_other = moves.core(near)
    far_other = moves.core(far)
    return (mine, other, near, near_other, far, far_other)


def gather_places(core, chip):
    near, over = chip ^ (1 + core), chip ^ (2 - core)
    return (
        (0, 0, core, chip),
        (1, 0, 1 - core, chip),
        (2, 0, core, near),
        (2, 1, 1 - core, near),
        (3, 0, 1 - core, over),
        (3, 1, core, over),
        (4, 0, core, chip ^ 3),
        (5, 0, 1 - core, chip ^ 3),
    )


def low_sum(*values):
    total = values[0].astype(F32)
    for value in values[1:]:
        total = total + value.astype(F32)
    return total.astype(BF)


def reduce_plane(moves, core, kept, given, more=None):
    rows = kept.shape[0] // 4
    come = moves.core(given)
    total = low_sum(kept, come) if more is None else low_sum(kept, come, more)
    diagonal = moves.far(total[2 * rows : 3 * rows])
    slots = lax.broadcasted_iota(jnp.int32, (2, 1, 1), 0)
    added = jnp.where(slots == core, diagonal.astype(F32)[None], 0.0)
    pair = (total[: 2 * rows].reshape(2, rows, -1).astype(F32) + added).astype(BF)
    come = moves.near(pair.reshape(2 * rows, -1))
    over = moves.core(lax.dynamic_slice_in_dim(come, (1 - core) * rows, rows))
    return low_sum(total[3 * rows :], lax.dynamic_slice_in_dim(come, core * rows, rows), over)


def dot_nn(left, right):
    return jnp.dot(left, right, preferred_element_type=F32)


def dot_nt(left, right):
    return lax.dot_general(left, right, (((1,), (1,)), ((), ())), preferred_element_type=F32)


def dot_tn(left, right):
    return lax.dot_general(left, right, (((0,), (0,)), ((), ())), preferred_element_type=F32)


def row_sum(values):
    return jnp.sum(values, axis=0, keepdims=True)


def copy_in(core, chip, refs, rows, turns, out_ref, sems, place):
    started = []
    for turn in range(turns):
        mine = []
        for index, (array, half, part, where) in enumerate(gather_places(core, chip)):
            ref = refs[array]
            start = (half * turns + turn) * rows
            copy = pltpu.make_async_copy(
                ref.at[pl.ds(start, rows)],
                out_ref.at[pl.ds(pl.multiple_of(place(turn, part, where), rows), rows)],
                sems.at[turn * 8 + index],
            )
            copy.start()
            mine.append(copy)
        started.append(mine)
    return started


def attn_place(rows):
    return lambda turn, part, where: turn * 8 * rows + (2 * where + part) * rows


def ffn_place(rows):
    return lambda turn, part, where: ((turn * 2 + part) * 4 + where) * rows


def scatter_out(core, chip, source_ref, rows, turns, turn, kept_ref, given_ref, place):
    for ref, mine in ((kept_ref, core), (given_ref, 1 - core)):
        near = chip ^ (1 + mine)
        slots = ((0, near), (1, near), (mine, chip ^ 3), (mine, chip))
        for slot, (part, where) in enumerate(slots):
            start = pl.multiple_of(place(0, part, where), rows)
            ref[(slot * turns + turn) * rows : (slot * turns + turn + 1) * rows, :] = source_ref[
                pl.ds(start, rows), :
            ]


def attend(width, scal_ref, mixed, mat, bias, qkv_ref, soft_ref, ctx_ref, seq):
    chains = mixed.shape[0] // seq
    heads = width // HEAD_DIM
    projected = dot_nn(mixed, mat[:, : 3 * width])
    qkv_ref[:, :width] = (projected[:, :width] + bias[:, :width]).astype(BF)
    qkv_ref[:, width : 2 * width] = projected[:, width : 2 * width].astype(BF)
    qkv_ref[:, 2 * width :] = (projected[:, 2 * width :] + bias[:, width : 2 * width]).astype(BF)
    column = lax.broadcasted_iota(jnp.int32, (1, seq), 1)
    for chain in range(chains):
        seen = column < scal_ref[2 + chain]
        rows = slice(chain * seq, (chain + 1) * seq)
        for head in range(heads):
            cut = slice(head * HEAD_DIM, (head + 1) * HEAD_DIM)
            queries = qkv_ref[rows, cut]
            keys = qkv_ref[rows, width + cut.start : width + cut.stop]
            values = qkv_ref[rows, 2 * width + cut.start : 2 * width + cut.stop]
            scores = dot_nt(queries, keys) * (HEAD_DIM**-0.5)
            scores = jnp.where(seen, scores, MASKED)
            shifted = jnp.exp(scores - jnp.max(scores, axis=1, keepdims=True))
            weights = (shifted / jnp.sum(shifted, axis=1, keepdims=True)).astype(BF)
            soft_ref[chain * heads + head] = weights
            ctx_ref[rows, cut] = dot_nn(weights, values).astype(BF)
    return dot_nt(ctx_ref[...], mat[:, 3 * width :])


def norm_back(grad, hat, inv, gain):
    scaled = grad * gain
    mean_one = jnp.mean(scaled, axis=1, keepdims=True)
    mean_two = jnp.mean(scaled * hat, axis=1, keepdims=True)
    return inv * (scaled - mean_one - hat * mean_two)


def norm_parts(values):
    centred = values - jnp.mean(values, axis=1, keepdims=True)
    inv = lax.rsqrt(jnp.mean(centred * centred, axis=1, keepdims=True) + EPSILON)
    return centred * inv, inv


def in_span(scal_ref, chain, chains, seq):
    position = lax.broadcasted_iota(jnp.int32, (seq, 1), 0)
    start = scal_ref[2 + chains + chain]
    return (position >= start) & (position < start + scal_ref[2 + 2 * chains + chain])


def attn_own_kernel(width, seq, scal, hidden, embed, mat, bias, mixed, qkv, soft, ctx, part):
    chains = hidden.shape[0] // seq
    for chain in range(chains):
        rows = slice(chain * seq, (chain + 1) * seq)
        mixed[rows, :] = jnp.where(in_span(scal, chain, chains, seq), embed[...], hidden[rows, :])
    part[...] = attend(
        width, scal, mixed[...], mat[...], bias[1:2, :].astype(F32), qkv, soft, ctx, seq
    )


def attn_rest_kernel(
    width, seq, turns, part_rows, scal, mixed, part, b_out, gain, shift, *refs
):
    firsts, refs = refs[:turns], refs[turns:]
    pieces, refs = refs[:6], refs[6:]
    qkvs, refs = refs[:turns], refs[turns:]
    softs, refs = refs[:turns], refs[turns:]
    ctxs, refs = refs[:turns], refs[turns:]
    hat, inv, normed, bias_in, mats, sems = refs
    core, chip = scal[0], scal[1]
    copies = copy_in(core, chip, pieces, part_rows, turns, mats, sems, attn_place(part_rows))
    total = part[...] + mixed[...].astype(F32) + b_out[...].astype(F32)
    height = 8 * part_rows
    for turn in range(turns):
        for copy in copies[turn]:
            copy.wait()
        bias_in[turn * 8 : turn * 8 + 8, :] = jnp.broadcast_to(
            firsts[turn][part_rows : part_rows + 1, :].astype(F32), (8, bias_in.shape[1])
        )
        total = total + attend(
            width,
            scal,
            mixed[...],
            mats[turn * height : (turn + 1) * height, :],
            firsts[turn][part_rows + 1 : part_rows + 2, :].astype(F32),
            qkvs[turn],
            softs[turn],
            ctxs[turn],
            seq,
        )
    ahat, ainv = norm_parts(total)
    hat[...] = ahat
    inv[...] = jnp.broadcast_to(ainv, inv.shape)
    normed[...] = (ahat * gain[...].astype(F32) + shift[...].astype(F32)).astype(BF)


def gelu_both(pre):
    cdf = 0.5 * (1.0 + lax.erf(pre * (0.5**0.5)))
    pdf = jnp.exp(-0.5 * pre * pre) * (0.5 / 3.141592653589793) ** 0.5
    return pre * cdf, cdf + pre * pdf


def ffn_step(normed, mat_in, mat_back, bias, act, slope):
    pre = dot_nn(normed[...], mat_in) + bias
    value, rate = gelu_both(pre)
    act[...] = value.astype(BF)
    slope[...] = rate.astype(BF)
    return dot_nn(act[...], mat_back)


def ffn_own_kernel(normed, mat_in, mat_back, bias, act, slope, total):
    total[...] = ffn_step(
        normed, mat_in[...], mat_back[...], bias[0:1, :].astype(F32), act, slope
    )


def ffn_rest_kernel(turns, part_rows, bias_rows, last, scal, normed, part, bias_in, *refs):
    if last:
        (hat1, gain1, shift1, b_back, gain2, shift2, cot), refs = refs[:7], refs[7:]
    pieces, refs = refs[:6], refs[6:]
    acts, refs = refs[:turns], refs[turns:]
    slopes, refs = refs[:turns], refs[turns:]
    if last:
        layer_out, grad_second, grad_low, small, mats, sems = refs
    else:
        total, mats, sems = refs
    core, chip = scal[0], scal[1]
    copies = copy_in(core, chip, pieces, part_rows, turns, mats, sems, ffn_place(part_rows))
    height = 4 * part_rows
    value = part[...]
    for turn in range(turns):
        for copy in copies[turn]:
            copy.wait()
        base = turn * 2 * height
        value = value + ffn_step(
            normed,
            mats[base : base + height, :],
            mats[base + height : base + 2 * height, :],
            bias_in[bias_rows[turn] * 8 : bias_rows[turn] * 8 + 1, :],
            acts[turn],
            slopes[turn],
        )
    if not last:
        total[...] = value
        return
    first = hat1[...] * gain1[...].astype(F32) + shift1[...].astype(F32)
    hat, inv = norm_parts(first + value + b_back[...].astype(F32))
    gain = gain2[...].astype(F32)
    layer_out[...] = (hat * gain + shift2[...].astype(F32)).astype(BF)
    grad = cot[...].astype(F32)
    back = norm_back(grad, hat, inv, gain)
    grad_second[...] = back
    grad_low[...] = back.astype(BF)
    small[0:1, :] = row_sum(grad * hat)
    small[1:2, :] = row_sum(grad)
    small[2:3, :] = row_sum(back)
    small[3:, :] = jnp.zeros_like(small[3:, :])


def ffn_back_kernel(turns, own, part_rows, scal, grad_low, normed, part, *refs):
    acts, refs = refs[:turns], refs[turns:]
    slopes, refs = refs[:turns], refs[turns:]
    count = 2 if own else 6
    pieces, refs = refs[:count], refs[count:]
    kept, given, total, bias_grad, whole = refs[:5]
    core, chip = scal[0], scal[1]
    if not own:
        mats, sems = refs[5:]
        copies = copy_in(core, chip, pieces, part_rows, turns, mats, sems, ffn_place(part_rows))
    height = 4 * part_rows
    value = part[...]
    bias_grad[...] = jnp.zeros_like(bias_grad)
    for turn in range(turns):
        whole[height:, :] = dot_tn(acts[turn][...], grad_low[...]).astype(BF)
        if own:
            mat_in, mat_back = pieces[0][...], pieces[1][...]
        else:
            for copy in copies[turn]:
                copy.wait()
            base = turn * 2 * height
            mat_in = mats[base : base + height, :]
            mat_back = mats[base + height : base + 2 * height, :]
        grad_act = dot_nt(grad_low[...], mat_back)
        grad_pre = (grad_act * slopes[turn][...].astype(F32)).astype(BF)
        bias_grad[turn : turn + 1, :] = row_sum(grad_pre.astype(F32))
        whole[:height, :] = dot_tn(normed[...], grad_pre).astype(BF)
        value = value + dot_nt(grad_pre, mat_in)
        scatter_out(
            core, chip, whole, part_rows, turns, turn, kept, given, ffn_place(part_rows)
        )
    total[...] = value


def attend_back(width, seq, grad_low, mat, mixed, qkv, soft, ctx, grad_qkv, whole):
    chains = grad_low.shape[0] // seq
    heads = width // HEAD_DIM
    scale = HEAD_DIM**-0.5
    whole[:, 3 * width :] = dot_tn(grad_low, ctx[...]).astype(BF)
    grad_ctx = dot_nn(grad_low, mat[:, 3 * width :]).astype(BF)
    for chain in range(chains):
        rows = slice(chain * seq, (chain + 1) * seq)
        for head in range(heads):
            cut = slice(head * HEAD_DIM, (head + 1) * HEAD_DIM)
            key_cut = slice(width + cut.start, width + cut.stop)
            value_cut = slice(2 * width + cut.start, 2 * width + cut.stop)
            weights = soft[chain * heads + head]
            grad_out = grad_ctx[rows, cut]
            grad_weights = dot_nt(grad_out, qkv[rows, value_cut])
            wide = weights.astype(F32)
            row_dot = jnp.sum(wide * grad_weights, axis=1, keepdims=True)
            grad_scores = (wide * (grad_weights - row_dot)).astype(BF)
            grad_qkv[rows, cut] = (dot_nn(grad_scores, qkv[rows, key_cut]) * scale).astype(BF)
            grad_qkv[rows, key_cut] = (dot_tn(grad_scores, qkv[rows, cut]) * scale).astype(BF)
            grad_qkv[rows, value_cut] = dot_tn(weights, grad_out).astype(BF)
    whole[:, : 3 * width] = dot_tn(mixed, grad_qkv[...]).astype(BF)
    sums = row_sum(grad_qkv[...].astype(F32))
    return dot_nt(grad_qkv[...], mat[:, : 3 * width]), sums


def attn_back_kernel(width, seq, turns, first, part_rows, scal, mixed, part, *refs):
    if first:
        (hat, inv, gain), refs = refs[:3], refs[3:]
    else:
        (grad_low_in,), refs = refs[:1], refs[1:]
    qkvs, refs = refs[:turns], refs[turns:]
    softs, refs = refs[:turns], refs[turns:]
    ctxs, refs = refs[:turns], refs[turns:]
    count = 6 if first else 1
    pieces, refs = refs[:count], refs[count:]
    kept, given, total, bias_grad = refs[:4]
    refs = refs[4:]
    core, chip = scal[0], scal[1]
    if first:
        grad_low, small, grad_qkv, whole, mats, sems = refs
        copies = copy_in(core, chip, pieces, part_rows, turns, mats, sems, attn_place(part_rows))
        grad = part[...]
        value = norm_back(grad, hat[...], inv[:, :1], gain[...].astype(F32))
        grad_low[...] = value.astype(BF)
        small[0:1, :] = row_sum(grad * hat[...])
        small[1:2, :] = row_sum(grad)
        small[2:3, :] = row_sum(value)
        small[3:, :] = jnp.zeros_like(small[3:, :])
    else:
        grad_low = grad_low_in
        grad_qkv, whole = refs
        value = part[...]
    height = 8 * part_rows
    bias_grad[...] = jnp.zeros_like(bias_grad)
    for turn in range(turns):
        if first:
            for copy in copies[turn]:
                copy.wait()
            mat = mats[turn * height : (turn + 1) * height, :]
        else:
            mat = pieces[0][...]
        back, sums = attend_back(
            width,
            seq,
            grad_low[...],
            mat,
            mixed[...],
            qkvs[turn],
            softs[turn],
            ctxs[turn],
            grad_qkv,
            whole,
        )
        value = value + back
        bias_grad[turn : turn + 1, :width] = sums[:, :width]
        bias_grad[turn : turn + 1, width : 2 * width] = sums[:, 2 * width :]
        scatter_out(
            core, chip, whole, part_rows, turns, turn, kept, given, attn_place(part_rows)
        )
    if first:
        total[...] = value
        return
    chains = value.shape[0] // seq
    embed_sum = jnp.zeros((1, value.shape[1]), F32)
    for chain in range(chains):
        rows = slice(chain * seq, (chain + 1) * seq)
        span = in_span(scal, chain, chains, seq)
        total[rows, :] = jnp.where(span, 0.0, value[rows, :]).astype(BF)
        embed_sum = embed_sum + row_sum(jnp.where(span, value[rows, :], 0.0))
    bias_grad[turns : turns + 1, :] = embed_sum


def ffn_out_kernel(part_rows, scal, *refs):
    pieces, outs = refs[:6], refs[6:]
    for array, half, part, where in gather_places(scal[0], scal[1]):
        block = pieces[array][half * part_rows : (half + 1) * part_rows, :].astype(F32)
        start = pl.multiple_of(where * part_rows, part_rows)
        for index in range(2):
            @pl.when(part == index)
            def _():
                outs[index][pl.ds(start, part_rows), :] = block


def attn_out_kernel(width, part_rows, scal, *refs):
    pieces, outs, whole = refs[:6], refs[6:10], refs[10]
    for array, half, part, where in gather_places(scal[0], scal[1]):
        block = pieces[array][half * part_rows : (half + 1) * part_rows, :]
        start = pl.multiple_of((2 * where + part) * part_rows, part_rows)
        whole[pl.ds(start, part_rows), :] = block.astype(F32)
    for index in range(3):
        outs[index][...] = whole[:, index * width : (index + 1) * width]
    outs[3][...] = whole[:, 3 * width :].T


SMEM = pl.BlockSpec(memory_space=pltpu.SMEM)
VMEM = pl.BlockSpec(memory_space=pltpu.VMEM)
ANY = pl.BlockSpec(memory_space=pl.ANY)


def call(kernel, ins, outs, scratch=(), flops=0, vmem=40, name=None):
    arrays = [array for array, _ in ins]
    moved = sum(a.size * a.dtype.itemsize for a in arrays) + sum(
        o.size * o.dtype.itemsize for o in outs
    )
    return pl.pallas_call(
        kernel,
        in_specs=[spec for _, spec in ins],
        out_specs=[VMEM] * len(outs),
        out_shape=list(outs),
        scratch_shapes=list(scratch),
        compiler_params=pltpu.CompilerParams(vmem_limit_bytes=vmem * MIB),
        cost_estimate=pl.CostEstimate(flops=flops, bytes_accessed=moved, transcendentals=0),
        name=name,
    )(*arrays)


def shape(rows, columns, kind=F32):
    return jax.ShapeDtypeStruct((rows, columns), kind)


def on_device(
    hidden_in,
    lengths,
    span_start,
    span_len,
    mask_embed,
    w_query,
    b_query,
    w_key,
    w_value,
    b_value,
    w_out,
    b_out,
    g_attn,
    s_attn,
    w_in,
    b_in,
    w_back,
    b_back,
    g_ffn,
    s_ffn,
    cotangent,
):
    group = lax.axis_size("tensor")
    dp_size = lax.axis_size("dp")
    moves = Moves(dp_size, group)
    dp = lax.axis_index("dp")
    rank = lax.axis_index("tensor")
    core, chip = dp & 1, (dp >> 1) & 3
    rows, model = hidden_in.shape
    seq = rows * group // lengths.shape[0]
    chains = rows // seq
    width = w_query.shape[1]
    heads = width // HEAD_DIM
    hidden = w_in.shape[1]
    piece = model // 4
    half = piece // 2
    turns = tuple(range(1, group))
    n_turns = len(turns)

    def local(values):
        return lax.dynamic_slice_in_dim(values, rank * chains, chains)

    scal = jnp.concatenate(
        (
            jnp.stack((core, chip)).astype(jnp.int32),
            local(lengths),
            local(span_start),
            local(span_len),
        )
    )
    row = lambda values: values.reshape(1, -1)

    own_attn = jnp.concatenate((w_query, w_key, w_value, w_out.T), axis=1)
    bias_pack = jnp.concatenate(
        (
            row(b_in),
            jnp.concatenate((row(b_query), row(b_value), jnp.zeros((1, model - 2 * width), BF)), axis=1),
            jnp.zeros((BIAS_ROWS - 2, model), BF),
        ),
        axis=0,
    )
    attn_mine = jnp.concatenate(
        (lax.dynamic_slice_in_dim(own_attn, chip * piece + core * half, half), bias_pack), axis=0
    )
    attn_firsts = [moves.fetch(attn_mine, turn) for turn in turns]
    attn_parts = spread(moves, jnp.concatenate([first[:half] for first in attn_firsts], axis=0))

    ffn_mine = jnp.where(
        core == 0,
        lax.dynamic_slice_in_dim(w_in, chip * piece, piece),
        lax.dynamic_slice_in_dim(w_back, chip * piece, piece),
    )
    chunk_one, chunk_two = (1, 3), (2,)
    ffn_one = spread(
        moves, jnp.concatenate([moves.fetch(ffn_mine, turn) for turn in chunk_one], axis=0)
    )
    ffn_two = spread(
        moves, jnp.concatenate([moves.fetch(ffn_mine, turn) for turn in chunk_two], axis=0)
    )

    dma = lambda count: pltpu.SemaphoreType.DMA((8 * count,))
    soft_shape = jax.ShapeDtypeStruct((chains * heads, seq, seq), BF)
    turn_flops = 2 * rows * model * 4 * width
    mixed, qkv_own, soft_own, ctx_own, attn_part = call(
        functools.partial(attn_own_kernel, width, seq),
        [(scal, SMEM), (hidden_in, VMEM), (row(mask_embed), VMEM), (own_attn, VMEM), (bias_pack, VMEM)],
        [shape(rows, model, BF), shape(rows, 3 * width, BF), soft_shape, shape(rows, width, BF), shape(rows, model)],
        flops=turn_flops,
        name="attn_own",
    )
    rest = call(
        functools.partial(attn_rest_kernel, width, seq, n_turns, half),
        [(scal, SMEM), (mixed, VMEM), (attn_part, VMEM), (row(b_out), VMEM), (row(g_attn), VMEM), (row(s_attn), VMEM)]
        + [(first, VMEM) for first in attn_firsts]
        + [(part, ANY) for part in attn_parts],
        [shape(rows, 3 * width, BF)] * n_turns
        + [soft_shape] * n_turns
        + [shape(rows, width, BF)] * n_turns
        + [shape(rows, model), shape(rows, 128), shape(rows, model, BF), shape(8 * n_turns, model)],
        [pltpu.VMEM((n_turns * model, model), BF), dma(n_turns)],
        flops=n_turns * turn_flops,
        name="attn_rest",
    )
    qkvs, softs, ctxs = rest[:n_turns], rest[n_turns : 2 * n_turns], rest[2 * n_turns : 3 * n_turns]
    hat1, inv1, normed, bias_in = rest[3 * n_turns :]

    ffn_flops = 2 * rows * model * hidden * 2
    act_own, slope_own, ffn_part = call(
        ffn_own_kernel,
        [(normed, VMEM), (w_in, VMEM), (w_back, VMEM), (bias_pack, VMEM)],
        [shape(rows, hidden, BF), shape(rows, hidden, BF), shape(rows, model)],
        flops=ffn_flops,
        name="ffn_own",
    )
    act_one1, act_one3, slope_one1, slope_one3, ffn_part = call(
        functools.partial(ffn_rest_kernel, 2, piece, (0, 2), False),
        [(scal, SMEM), (normed, VMEM), (ffn_part, VMEM), (bias_in, VMEM)] + [(part, ANY) for part in ffn_one],
        [shape(rows, hidden, BF)] * 4 + [shape(rows, model)],
        [pltpu.VMEM((4 * model, model), BF), dma(2)],
        flops=2 * ffn_flops,
        name="ffn_one",
    )
    act_two, slope_two, layer_out, grad_second, grad_low, small_ffn = call(
        functools.partial(ffn_rest_kernel, 1, piece, (1,), True),
        [(scal, SMEM), (normed, VMEM), (ffn_part, VMEM), (bias_in, VMEM), (hat1, VMEM)]
        + [(row(v), VMEM) for v in (g_attn, s_attn, b_back, g_ffn, s_ffn)]
        + [(cotangent, VMEM)]
        + [(part, ANY) for part in ffn_two],
        [shape(rows, hidden, BF)] * 2
        + [shape(rows, model, BF), shape(rows, model), shape(rows, model, BF), shape(8, model)],
        [pltpu.VMEM((2 * model, model), BF), dma(1)],
        flops=ffn_flops,
        name="ffn_two",
    )

    def ffn_back(count, acts, slopes, weights, part, own, name):
        scratch = [pltpu.VMEM((2 * model, model), BF)]
        if not own:
            scratch += [pltpu.VMEM((2 * count * model, model), BF), dma(count)]
        return call(
            functools.partial(ffn_back_kernel, count, own, piece),
            [(scal, SMEM), (grad_low, VMEM), (normed, VMEM), (part, VMEM)]
            + [(v, VMEM) for v in acts]
            + [(v, VMEM) for v in slopes]
            + [(v, VMEM if own else ANY) for v in weights],
            [shape(4 * count * piece, model, BF)] * 2 + [shape(rows, model), shape(8, model)],
            scratch,
            flops=2 * count * ffn_flops,
            name=name,
        )

    kept_two, given_two, grad_part, bias_two = ffn_back(
        1, (act_two,), (slope_two,), ffn_two, grad_second, False, "ffn_back_two"
    )
    kept_one, given_one, grad_part, bias_one = ffn_back(
        2, (act_one1, act_one3), (slope_one1, slope_one3), ffn_one, grad_part, False, "ffn_back_one"
    )
    kept_own, given_own, grad_part, bias_own = ffn_back(
        1, (act_own,), (slope_own,), (w_in, w_back), grad_part, True, "ffn_back_own"
    )
    done_two = moves.give(reduce_plane(moves, core, kept_two, given_two), 2)
    sums_one = reduce_plane(moves, core, kept_one, given_one)
    done_one = [
        moves.give(sums_one[index * piece : (index + 1) * piece], turn)
        for index, turn in enumerate(chunk_one)
    ]
    done_own = reduce_plane(moves, core, kept_own, given_own)
    ffn_final = low_sum(done_own, done_two, *done_one)

    back = call(
        functools.partial(attn_back_kernel, width, seq, n_turns, True, half),
        [(scal, SMEM), (mixed, VMEM), (grad_part, VMEM), (hat1, VMEM), (inv1, VMEM), (row(g_attn), VMEM)]
        + [(v, VMEM) for v in (*qkvs, *softs, *ctxs)]
        + [(part, ANY) for part in attn_parts],
        [shape(4 * n_turns * half, model, BF)] * 2
        + [shape(rows, model), shape(8, model), shape(rows, model, BF), shape(8, model)],
        [
            pltpu.VMEM((rows, 3 * width), BF),
            pltpu.VMEM((model, model), BF),
            pltpu.VMEM((n_turns * model, model), BF),
            dma(n_turns),
        ],
        flops=2 * n_turns * turn_flops,
        name="attn_back_rest",
    )
    kept_rest, given_rest, grad_mixed, bias_rest, attn_low, small_attn = back
    kept_mine, given_mine, grad_input, bias_mine = call(
        functools.partial(attn_back_kernel, width, seq, 1, False, half),
        [(scal, SMEM), (mixed, VMEM), (grad_mixed, VMEM), (attn_low, VMEM), (qkv_own, VMEM), (soft_own, VMEM), (ctx_own, VMEM), (own_attn, VMEM)],
        [shape(4 * half, model, BF)] * 2 + [shape(rows, model, BF), shape(8, model)],
        [pltpu.VMEM((rows, 3 * width), BF), pltpu.VMEM((model, model), BF)],
        flops=2 * turn_flops,
        name="attn_back_own",
    )
    sums_rest = reduce_plane(moves, core, kept_rest, given_rest)
    done_rest = [
        moves.give(sums_rest[index * half : (index + 1) * half], turn)
        for index, turn in enumerate(turns)
    ]
    done_mine = reduce_plane(moves, core, kept_mine, given_mine)
    attn_final = low_sum(done_mine, *done_rest)

    by_turn_ffn = jnp.concatenate((bias_own[:1], bias_one[:1], bias_two[:1], bias_one[1:2]), axis=0)
    by_turn_attn = jnp.concatenate((bias_mine[:1], bias_rest[:n_turns]), axis=0)
    small = jnp.concatenate(
        (
            small_ffn[:3],
            small_attn[:3],
            bias_mine[1:2],
            jnp.zeros((1, model), F32),
            jnp.roll(by_turn_ffn, rank, axis=0),
            jnp.roll(by_turn_attn, rank, axis=0),
        ),
        axis=0,
    )
    step = 1
    while step < dp_size:
        small = small + moves.flip(small, step, 0)
        step *= 2
    step = 1
    while step < group:
        small = small + moves.flip(small, 0, step)
        step *= 2

    if dp_size > 8:
        groups = [list(range(i, dp_size, 8)) for i in range(8)]
        ffn_final, attn_final = (
            lax.psum(v.astype(F32), "dp", axis_index_groups=groups).astype(BF)
            for v in (ffn_final, attn_final)
        )
    grad_w_in, grad_w_back = call(
        functools.partial(ffn_out_kernel, piece),
        [(scal, SMEM)] + [(part, VMEM) for part in spread(moves, ffn_final)],
        [shape(model, hidden), shape(hidden, model)],
        name="ffn_out",
    )
    grad_w_query, grad_w_key, grad_w_value, grad_w_out = call(
        functools.partial(attn_out_kernel, width, half),
        [(scal, SMEM)] + [(part, VMEM) for part in spread(moves, attn_final)],
        [shape(model, width)] * 3 + [shape(width, model)],
        [pltpu.VMEM((model, model), F32)],
        name="attn_out",
    )
    my_in = lax.dynamic_index_in_dim(small, 8 + rank, keepdims=False)
    my_attn = lax.dynamic_index_in_dim(small, 8 + group + rank, keepdims=False)
    return (
        layer_out,
        grad_input,
        small[6],
        grad_w_query,
        my_attn[:width],
        grad_w_key,
        grad_w_value,
        my_attn[width : 2 * width],
        grad_w_out,
        small[5],
        small[3],
        small[4],
        grad_w_in,
        my_in,
        grad_w_back,
        small[2],
        small[0],
        small[1],
    )


def solution(mesh):
    rows = P(("dp", "tensor"), None)
    placed = (
        rows,
        P("dp"),
        P("dp"),
        P("dp"),
        P(),
        P(None, "tensor"),
        P("tensor"),
        P(None, "tensor"),
        P(None, "tensor"),
        P("tensor"),
        P("tensor", None),
        P(),
        P(),
        P(),
        P(None, "tensor"),
        P("tensor"),
        P("tensor", None),
        P(),
        P(),
        P(),
        rows,
    )
    return jax.shard_map(
        on_device,
        mesh=mesh,
        in_specs=placed,
        out_specs=(
            rows,
            rows,
            P(),
            P(None, "tensor"),
            P("tensor"),
            P(None, "tensor"),
            P(None, "tensor"),
            P("tensor"),
            P("tensor", None),
            P(),
            P(),
            P(),
            P(None, "tensor"),
            P("tensor"),
            P("tensor", None),
            P(),
            P(),
            P(),
        ),
        check_vma=False,
    )
```

time: 888 us -> 366 us (0.41)
  waiting for transfers between devices: 629 us -> 114 us
  Pallas kernels: 0 us -> 90.1 us
  matrix products: 84.6 us -> 0 us
  starting transfers between devices: 1.53 us -> 62.1 us
  blocking collectives: 56.1 us -> 0 us
  between operations: 14.6 us -> 2.2 us
    reduce_scatter x4 -> x0, waiting for transfers between devices: 300 us -> none  [the longest x1 109 us: on_device(): lax.psum_scatter(jnp.dot(context, w_out, preferred_element_type=jnp.float...]
    all_gather x4 -> x0, waiting for transfers between devices: 253 us -> none  [the longest x1 64 us: on_device(): lax.all_gather(grad_second.astype(jnp.bfloat16), 'tensor', axis=0, tiled=...]
    ppermute x0 -> x62, waiting for transfers between devices: none -> 114 us  [build(): return lambda value: lax.ppermute(value, AXES, pairs)]
    pallas_call x0 -> x12, Pallas kernels: none -> 90.1 us  [call(): pl.pallas_call(kernel, in_specs=[spec for _, spec in ins], out_specs=[VME...]
    dot_general x40 -> x0, matrix products: 84.6 us -> none  [the longest x1 18.4 us: on_device(): jnp.dot(normed_full, w_in, preferred_element_type=jnp.float32)]
    psum x1 -> x0, waiting for transfers between devices: 75.7 us -> none  [on_device(): lax.psum((grad_w_query, grad_b_query, grad_w_key, grad_w_value, grad_b_va...]
    ppermute x0 -> x62, starting transfers between devices: none -> 62.1 us  [build(): return lambda value: lax.ppermute(value, AXES, pairs)]
    psum x2 -> x0, blocking collectives: 56.1 us -> none  [the longest x1 41.7 us: on_device(): lax.psum((grad_embed, grad_b_out, grad_g_attn, grad_s_attn, grad_b_back,...]
  transfers between devices with their start and end apart: 9 -> 62, of which waited for: 9 -> 23; matrix products, arithmetic and copies ran while one was open for 3% -> 15% of each run, Pallas kernels for 0% -> 19%
where the time goes in v1:
time: 366 us; the launch traced here: 359 us
  waiting for transfers between devices  114 us (31%)
  Pallas kernels  90.1 us (25%)
  local copies, waits for them, and re-layouts  62.3 us (17%)
  starting transfers between devices  62.1 us (17%)
  other arithmetic  28.5 us (8%)
    ppermute x62, waiting for transfers between devices, build(): return lambda value: lax.ppermute(value, AXES, pairs)  114 us
    pallas_call x12, Pallas kernels, call(): pl.pallas_call(kernel, in_specs=[spec for _, spec in ins], out_specs=[VME...  90.1 us
    ppermute x62, starting transfers between devices, build(): return lambda value: lax.ppermute(value, AXES, pairs)  62.1 us
    unnamed x222, local copies, waits for them, and re-layouts  39.9 us
    convert_element_type x10, other arithmetic, low_sum(): return total.astype(BF)  15.7 us
  transfers between devices with their start and end apart: 62, of which 23 were waited for; matrix products, arithmetic and copies ran while one was open for 15% of the time, Pallas kernels for 19%

profile of v1, /device:TPU:0, one launch (start us, length us, event | category | flops | bytes accessed | tf_op | source)
XLA Modules:
  0.0 359.3 jit_solution(11341926169138764646)
XLA Ops:
  2.6 5.0 %collective-permute-start.8 = (bf16[192,768]{1,0:T(8,128)(2,1)}, bf16[192,768]{1,0:T(8,128)(2,1)S(1)}, u32[]{:S(2)}, u32[]{:S(2)}) collective-permute-start(bf16[192,768]{1,0:T(8,128)(2,1)} %dynamic-slice_select_fusion), channel_id=1, source_target_pairs={{1,0},{2,1},{3,2},{0,3},{5,4},{6,5},{7,6},{4,7},{9,8},{10,9},{11,1... | collective-permute-start | bytes 884744 | tf_op jit(solution)/shard_map/ppermute | solution.py:30
  9.9 5.5 %collective-permute-done.8 = bf16[192,768]{1,0:T(8,128)(2,1)S(1)} collective-permute-done((bf16[192,768]{1,0:T(8,128)(2,1)}, bf16[192,768]{1,0:T(8,128)(2,1)S(1)}, u32[]{:S(2)}, u32[]{:S(2)}) %collective-permute-start.8) | collective-permute-done | bytes 294944 | tf_op jit(solution)/shard_map/ppermute | solution.py:30
  15.4 5.9 %collective-permute-done.9 = bf16[192,768]{1,0:T(8,128)(2,1)S(1)} collective-permute-done((bf16[192,768]{1,0:T(8,128)(2,1)}, bf16[192,768]{1,0:T(8,128)(2,1)S(1)}, u32[]{:S(2)}, u32[]{:S(2)}) %collective-permute-start.9) | collective-permute-done | bytes 294944 | tf_op jit(solution)/shard_map/ppermute | solution.py:30
  25.7 5.0 %collective-permute-done.2.refs_2_ = bf16[112,768]{1,0:T(8,128)(2,1)S(1)} collective-permute-done((bf16[112,768]{1,0:T(8,128)(2,1)S(1)}, bf16[112,768]{1,0:T(8,128)(2,1)S(1)}, u32[]{:S(2)}, u32[]{:S(2)}) %collective-permute-start.2) | collective-permute-done | bytes 172064 | tf_op jit(solution)/shard_map/ppermute | solution.py:30
  30.8 6.9 %collective-permute-done.1.refs_1_ = bf16[112,768]{1,0:T(8,128)(2,1)S(1)} collective-permute-done((bf16[112,768]{1,0:T(8,128)(2,1)S(1)}, bf16[112,768]{1,0:T(8,128)(2,1)S(1)}, u32[]{:S(2)}, u32[]{:S(2)}) %collective-permute-start.1) | collective-permute-done | bytes 172064 | tf_op jit(solution)/shard_map/ppermute | solution.py:30
  44.1 13.4 %collective-permute-done.15.refs_7_.refs_2_ = bf16[192,768]{1,0:T(8,128)(2,1)S(1)} collective-permute-done((bf16[192,768]{1,0:T(8,128)(2,1)}, bf16[192,768]{1,0:T(8,128)(2,1)S(1)}, u32[]{:S(2)}, u32[]{:S(2)}) %collective-permute-start.15) | collective-permute-done | bytes 294944 | tf_op jit(solution)/shard_map/ppermute | solution.py:30
  62.4 4.3 %collective-permute-done.4.refs_5_.refs_14_ = bf16[576,768]{1,0:T(8,128)(2,1)} collective-permute-done((bf16[576,768]{1,0:T(8,128)(2,1)S(1)}, bf16[576,768]{1,0:T(8,128)(2,1)}, u32[]{:S(2)}, u32[]{:S(2)}) %collective-permute-start.4) | collective-permute-done | bytes 884768 | tf_op jit(solution)/shard_map/ppermute | solution.py:30
  69.4 9.9 %collective-permute-done.17.refs_9_.refs_4_ = bf16[384,768]{1,0:T(8,128)(2,1)S(1)} collective-permute-done((bf16[384,768]{1,0:T(8,128)(2,1)S(1)}, bf16[384,768]{1,0:T(8,128)(2,1)S(1)}, u32[]{:S(2)}, u32[]{:S(2)}) %collective-permute-start.17) | collective-permute-done | bytes 589856 | tf_op jit(solution)/shard_map/ppermute | solution.py:30
  92.2 5.1 %attn_own.1 = (bf16[512,768]{1,0:T(8,128)(2,1)S(1)}, bf16[512,576]{1,0:T(8,128)(2,1)S(1)}, bf16[12,128,128]{2,1,0:T(8,128)(2,1)S(1)}, bf16[512,192]{1,0:T(8,128)(2,1)S(1)}, f32[512,768]{1,0:T(8,128)S(1)}) custom-call(s32[14]{0:T(128)S(1)} %concatenate.51.scal, bf16[512,768]{1,0:T(8,128)(2,1)S(1)} %copy-done.49, bf16[1,768]{1,0:T(2,128)(2,1)S(1)} %copy-done.44, ...), custom_call_target="tpu_custom_call" | custom-call | flops 603979776 | bytes 5531192 | tf_op jit(solution)/shard_map/attn_own/pallas_call | solution.py:460
  104.1 17.3 %attn_rest.1 = (bf16[512,576]{1,0:T(8,128)(2,1)S(1)}, bf16[512,576]{1,0:T(8,128)(2,1)S(1)}, bf16[512,576]{1,0:T(8,128)(2,1)S(1)}, bf16[12,128,128]{2,1,0:T(8,128...) custom-call(s32[14]{0:T(128)S(1)} %concatenate.51.scal, ...), custom_call_target="tpu_custom_call" | custom-call | flops 1811939328 | bytes 12653112 | tf_op jit(solution)/shard_map/attn_rest/pallas_call | solution.py:460
  126.9 6.1 %ffn_one.1 = (bf16[512,768]{1,0:T(8,128)(2,1)S(1)}, bf16[512,768]{1,0:T(8,128)(2,1)S(1)}, bf16[512,768]{1,0:T(8,128)(2,1)S(1)}, bf16[512,768]{1,0:T(8,128)(2,1)S(1)}, f32[512,768]{1,0:T(8,128)S(1)}) custom-call(s32[14]{0:T(128)S(1)} %concatenate.51.scal, bf16[512,768]{1,0:T(8,128)(2,1)S(1)} %get-tuple-element.81.normed, ...), custom_call_target="tpu_custom_call" | custom-call | flops 2415919104 | bytes 11870264 | tf_op jit(solution)/shard_map/ffn_one/pallas_call | solution.py:460
  136.6 5.8 %ffn_two.1 = (bf16[512,768]{1,0:T(8,128)(2,1)S(1)}, bf16[512,768]{1,0:T(8,128)(2,1)S(1)}, bf16[512,768]{1,0:T(8,128)(2,1)}, f32[512,768]{1,0:T(8,128)S(1)}, bf16...) custom-call(s32[14]{0:T(128)S(1)} %concatenate.51.scal, bf16[512,768]{1,0:T(8,128)(2,1)S(1)} %get-tuple-element.81.normed, ...), custom_call_target="tpu_custom_call" | custom-call | flops 1207959552 | bytes 11902520 | tf_op jit(solution)/shard_map/ffn_two/pallas_call | solution.py:460
  142.5 4.7 %ffn_back_two.1 = (bf16[768,768]{1,0:T(8,128)(2,1)S(1)}, bf16[768,768]{1,0:T(8,128)(2,1)}, f32[512,768]{1,0:T(8,128)S(1)}, f32[8,768]{1,0:T(8,128)S(1)}) custom-call(s32[14]{0:T(128)S(1)} %concatenate.51.scal, bf16[512,768]{1,0:T(8,128)(2,1)S(1)} %get-tuple-element.87.grad_low, bf16[512,768]{1,0:T(8,128)(2,1)S(1)} %get-tuple-element.81.normed, ...), custom_call_target="tpu_custom_call" | custom-call | flops 2415919104 | bytes 11034680 | tf_op jit(solution)/shard_map/ffn_back_two/pallas_call | solution.py:460
  150.6 9.2 %ffn_back_one.1 = (bf16[1536,768]{1,0:T(8,128)(2,1)}, bf16[1536,768]{1,0:T(8,128)(2,1)}, f32[512,768]{1,0:T(8,128)S(1)}, f32[8,768]{1,0:T(8,128)S(1)}) custom-call(s32[14]{0:T(128)S(1)} %concatenate.51.scal, bf16[512,768]{1,0:T(8,128)(2,1)S(1)} %get-tuple-element.87.grad_low, bf16[512,768]{1,0:T(8,128)(2,1)S(1)} %get-tuple-element.81.normed, ...), custom_call_target="tpu_custom_call" | custom-call | flops 4831838208 | bytes 17326136 | tf_op jit(solution)/shard_map/ffn_back_one/pallas_call | solution.py:460
  161.2 4.0 %ffn_back_own.1 = (bf16[768,768]{1,0:T(8,128)(2,1)S(1)}, bf16[768,768]{1,0:T(8,128)(2,1)}, f32[512,768]{1,0:T(8,128)S(1)}, f32[8,768]{1,0:T(8,128)S(1)}) custom-call(s32[14]{0:T(128)S(1)} %concatenate.51.scal, bf16[512,768]{1,0:T(8,128)(2,1)S(1)} %get-tuple-element.87.grad_low, bf16[512,768]{1,0:T(8,128)(2,1)S(1)} %get-tuple-element.81.normed, ...), custom_call_target="tpu_custom_call" | custom-call | flops 2415919104 | bytes 11034680 | tf_op jit(solution)/shard_map/ffn_back_own/pallas_call | solution.py:460
  169.5 22.4 %attn_back_rest.1 = (bf16[1152,768]{1,0:T(8,128)(2,1)}, bf16[1152,768]{1,0:T(8,128)(2,1)}, f32[512,768]{1,0:T(8,128)S(1)}, f32[8,768]{1,0:T(8,128)S(1)}, bf16[51...) custom-call(s32[14]{0:T(128)S(1)} %concatenate.51.scal, bf16[512,768]{1,0:T(8,128)(2,1)S(1)} %get-tuple-element.79.mixed, ...), custom_call_target="tpu_custom_call" | custom-call | flops 3623878656 | bytes 17221176 | tf_op jit(solution)/shard_map/attn_back_rest/pallas_call | solution.py:460
  201.6 5.2 %collective-permute-done.52 = bf16[384,768]{1,0:T(8,128)(2,1)} collective-permute-done((bf16[384,768]{1,0:T(8,128)(2,1)}, bf16[384,768]{1,0:T(8,128)(2,1)}, u32[]{:S(2)}, u32[]{:S(2)}) %collective-permute-start.52) | collective-permute-done | bytes 589856 | tf_op jit(solution)/shard_map/ppermute | solution.py:30
  220.4 7.4 %attn_back_own.1 = (bf16[384,768]{1,0:T(8,128)(2,1)S(1)}, bf16[384,768]{1,0:T(8,128)(2,1)S(1)}, bf16[512,768]{1,0:T(8,128)(2,1)}, f32[8,768]{1,0:T(8,128)S(1)}) custom-call(s32[14]{0:T(128)S(1)} %concatenate.51.scal, bf16[512,768]{1,0:T(8,128)(2,1)S(1)} %get-tuple-element.79.mixed, f32[512,768]{1,0:T(8,128)S(1)} %get-tuple-element.110.part, ...), custom_call_target="tpu_custom_call" | custom-call | flops 1207959552 | bytes 7495736 | tf_op jit(solution)/shard_map/attn_back_own/pallas_call | solution.py:460
  236.0 16.3 %collective-permute-done.48 = bf16[384,768]{1,0:T(8,128)(2,1)S(1)} collective-permute-done((bf16[384,768]{1,0:T(8,128)(2,1)S(1)}, bf16[384,768]{1,0:T(8,128)(2,1)S(1)}, u32[]{:S(2)}, u32[]{:S(2)}) %collective-permute-start.48) | collective-permute-done | bytes 589856 | tf_op jit(solution)/shard_map/ppermute | solution.py:30
  266.8 5.4 %collective-permute-start.50 = (bf16[192,768]{1,0:T(8,128)(2,1)}, bf16[192,768]{1,0:T(8,128)(2,1)}, u32[]{:S(2)}, u32[]{:S(2)}) collective-permute-start(bf16[192,768]{1,0:T(8,128)(2,1)} %add_convert_fusion.8), channel_id=1, source_target_pairs={{2,0},{3,1},{0,2},{1,3},{6,4},{7,5},{4,6},{5,7},{10,8},{11,9},{8,1... | collective-permute-start | bytes 884744 | tf_op jit(solution)/shard_map/ppermute | solution.py:30
  281.5 11.6 %collective-permute-done.50 = bf16[192,768]{1,0:T(8,128)(2,1)} collective-permute-done((bf16[192,768]{1,0:T(8,128)(2,1)}, bf16[192,768]{1,0:T(8,128)(2,1)}, u32[]{:S(2)}, u32[]{:S(2)}) %collective-permute-start.50) | collective-permute-done | bytes 294944 | tf_op jit(solution)/shard_map/ppermute | solution.py:30
  298.2 5.1 %collective-permute-start.34 = (bf16[96,768]{1,0:T(8,128)(2,1)}, bf16[96,768]{1,0:T(8,128)(2,1)S(1)}, u32[]{:S(2)}, u32[]{:S(2)}) collective-permute-start(bf16[96,768]{1,0:T(8,128)(2,1)} %get-tuple-element.167), channel_id=1, source_target_pairs={{3,0},{0,1},{1,2},{2,3},{7,4},{4,5},{5,6},{6,7},{11,8},{8,9},{9,10... | collective-permute-start | bytes 442376 | tf_op jit(solution)/shard_map/ppermute | solution.py:30
  311.5 6.2 %collective-permute-done.35 = bf16[96,768]{1,0:T(8,128)(2,1)S(1)} collective-permute-done((bf16[96,768]{1,0:T(8,128)(2,1)S(1)}, bf16[96,768]{1,0:T(8,128)(2,1)S(1)}, u32[]{:S(2)}, u32[]{:S(2)}) %collective-permute-start.35) | collective-permute-done | bytes 147488 | tf_op jit(solution)/shard_map/ppermute | solution.py:30
  355.2 3.9 %ffn_out.1 = (f32[768,768]{1,0:T(8,128)}, f32[768,768]{1,0:T(8,128)}) custom-call(s32[14]{0:T(128)S(1)} %concatenate.51.scal, bf16[192,768]{1,0:T(8,128)(2,1)S(1)} %add_convert_fusion.7.refs_0_, bf16[192,768]{1,0:T(8,128)(2,1)S(1)} %collective-permute-done.57.refs_1_, bf16[384,768]{1,0:T(8,128)(2,1)S(1)} %collective-permute-done.58.refs_2_, ...), custom_call_target="tpu_custom_call" | custom-call | bytes 7077944 | tf_op jit(solution)/shard_map/ffn_out/pallas_call | solution.py:460
  (427 shorter events, 165.4 us)
Async XLA Ops:
  39.3 21.0 %collective-permute-start.11 = (bf16[768,768]{1,0:T(8,128)(2,1)S(1)}, bf16[768,768]{1,0:T(8,128)(2,1)}, u32[]{:S(2)}, u32[]{:S(2)}) collective-permute-start(bf16[768,768]{1,0:T(8,128)(2,1)S(1)} %pad_maximum_fusion.1), channel_id=1, source_target_pairs={{8,0},{9,1},{10,2},{11,3},{20,4},{21,5},{22,6},{23,7},{0,8},{1,9},... | collective-permute-start | bytes 3538952 | tf_op jit(solution)/shard_map/ppermute | solution.py:30
  43.5 23.3 %collective-permute-start.4 = (bf16[576,768]{1,0:T(8,128)(2,1)S(1)}, bf16[576,768]{1,0:T(8,128)(2,1)}, u32[]{:S(2)}, u32[]{:S(2)}) collective-permute-start(bf16[576,768]{1,0:T(8,128)(2,1)S(1)} %pad_maximum_fusion.2), channel_id=1, source_target_pairs={{8,0},{9,1},{10,2},{11,3},{20,4},{21,5},{22,6},{23,7},{0,8},{1,9},... | collective-permute-start | bytes 2654216 | tf_op jit(solution)/shard_map/ppermute | solution.py:30
  59.2 20.1 %collective-permute-start.17 = (bf16[384,768]{1,0:T(8,128)(2,1)S(1)}, bf16[384,768]{1,0:T(8,128)(2,1)S(1)}, u32[]{:S(2)}, u32[]{:S(2)}) collective-permute-start(bf16[384,768]{1,0:T(8,128)(2,1)S(1)} %pad_maximum_fusion.3), channel_id=1, source_target_pairs={{8,0},{9,1},{10,2},{11,3},{20,4},{21,5},{22,6},{23,7},{0,8},{1,9},... | collective-permute-start | bytes 1769480 | tf_op jit(solution)/shard_map/ppermute | solution.py:30
  61.4 20.9 %collective-permute-start.13 = (bf16[384,768]{1,0:T(8,128)(2,1)S(1)}, bf16[384,768]{1,0:T(8,128)(2,1)}, u32[]{:S(2)}, u32[]{:S(2)}) collective-permute-start(bf16[384,768]{1,0:T(8,128)(2,1)S(1)} %slice.196), channel_id=1, source_target_pairs={{16,0},{17,1},{18,2},{19,3},{12,4},{13,5},{14,6},{15,7},{24,8},{25... | collective-permute-start | bytes 1769480 | tf_op jit(solution)/shard_map/ppermute | solution.py:30
  62.4 64.4 %collective-permute-start.12 = (bf16[768,768]{1,0:T(8,128)(2,1)}, bf16[768,768]{1,0:T(8,128)(2,1)}, u32[]{:S(2)}, u32[]{:S(2)}) collective-permute-start(bf16[768,768]{1,0:T(8,128)(2,1)} %collective-permute-done.11.refs_2_.refs_6_), channel_id=1, source_target_pairs={{4,0},{5,1},{6,2},{7,3},{0,4},{1,5},{2,6},{3,7},{12,8},{13,9},{14,... | collective-permute-start | bytes 3538952 | tf_op jit(solution)/shard_map/ppermute | solution.py:30
  69.4 29.9 %collective-permute-start.5 = (bf16[576,768]{1,0:T(8,128)(2,1)}, bf16[576,768]{1,0:T(8,128)(2,1)}, u32[]{:S(2)}, u32[]{:S(2)}) collective-permute-start(bf16[576,768]{1,0:T(8,128)(2,1)} %collective-permute-done.4.refs_5_.refs_14_), channel_id=1, source_target_pairs={{4,0},{5,1},{6,2},{7,3},{0,4},{1,5},{2,6},{3,7},{12,8},{13,9},{14,... | collective-permute-start | bytes 2654216 | tf_op jit(solution)/shard_map/ppermute | solution.py:30
  82.4 44.4 %collective-permute-start.14 = (bf16[384,768]{1,0:T(8,128)(2,1)}, bf16[384,768]{1,0:T(8,128)(2,1)}, u32[]{:S(2)}, u32[]{:S(2)}) collective-permute-start(bf16[384,768]{1,0:T(8,128)(2,1)} %collective-permute-done.13.refs_4_.refs_8_), channel_id=1, source_target_pairs={{4,0},{5,1},{6,2},{7,3},{0,4},{1,5},{2,6},{3,7},{12,8},{13,9},{14,... | collective-permute-start | bytes 1769480 | tf_op jit(solution)/shard_map/ppermute | solution.py:30
  86.2 50.4 %collective-permute-start.18 = (bf16[384,768]{1,0:T(8,128)(2,1)S(1)}, bf16[384,768]{1,0:T(8,128)(2,1)}, u32[]{:S(2)}, u32[]{:S(2)}) collective-permute-start(bf16[384,768]{1,0:T(8,128)(2,1)S(1)} %collective-permute-done.17.refs_9_.refs_4_), channel_id=1, source_target_pairs={{4,0},{5,1},{6,2},{7,3},{0,4},{1,5},{2,6},{3,7},{12,8},{13,9},{14,... | collective-permute-start | bytes 1769480 | tf_op jit(solution)/shard_map/ppermute | solution.py:30
  98.8 37.8 %collective-permute-start.20 = (bf16[192,768]{1,0:T(8,128)(2,1)}, bf16[192,768]{1,0:T(8,128)(2,1)S(1)}, u32[]{:S(2)}, u32[]{:S(2)}) collective-permute-start(bf16[192,768]{1,0:T(8,128)(2,1)} %collective-permute-done.19.refs_11_.refs_6_), channel_id=1, source_target_pairs={{4,0},{5,1},{6,2},{7,3},{0,4},{1,5},{2,6},{3,7},{12,8},{13,9},{14,... | collective-permute-start | bytes 884744 | tf_op jit(solution)/shard_map/ppermute | solution.py:30
  159.8 32.6 %collective-permute-start.51 = (bf16[1536,768]{1,0:T(8,128)(2,1)}, bf16[1536,768]{1,0:T(8,128)(2,1)}, u32[]{:S(2)}, u32[]{:S(2)}) collective-permute-start(bf16[1536,768]{1,0:T(8,128)(2,1)} %get-tuple-element.136), channel_id=1, source_target_pairs={{4,0},{5,1},{6,2},{7,3},{0,4},{1,5},{2,6},{3,7},{12,8},{13,9},{14,... | collective-permute-start | bytes 7077896 | tf_op jit(solution)/shard_map/ppermute | solution.py:30
  167.5 30.7 %collective-permute-start.42 = (bf16[768,768]{1,0:T(8,128)(2,1)}, bf16[768,768]{1,0:T(8,128)(2,1)}, u32[]{:S(2)}, u32[]{:S(2)}) collective-permute-start(bf16[768,768]{1,0:T(8,128)(2,1)} %get-tuple-element.132), channel_id=1, source_target_pairs={{4,0},{5,1},{6,2},{7,3},{0,4},{1,5},{2,6},{3,7},{12,8},{13,9},{14,... | collective-permute-start | bytes 3538952 | tf_op jit(solution)/shard_map/ppermute | solution.py:30
  167.8 43.0 %collective-permute-start.46 = (bf16[768,768]{1,0:T(8,128)(2,1)}, bf16[768,768]{1,0:T(8,128)(2,1)}, u32[]{:S(2)}, u32[]{:S(2)}) collective-permute-start(bf16[768,768]{1,0:T(8,128)(2,1)} %get-tuple-element.134), channel_id=1, source_target_pairs={{4,0},{5,1},{6,2},{7,3},{0,4},{1,5},{2,6},{3,7},{12,8},{13,9},{14,... | collective-permute-start | bytes 3538952 | tf_op jit(solution)/shard_map/ppermute | solution.py:30
  191.9 41.3 %collective-permute-start.30 = (bf16[1152,768]{1,0:T(8,128)(2,1)}, bf16[1152,768]{1,0:T(8,128)(2,1)}, u32[]{:S(2)}, u32[]{:S(2)}) collective-permute-start(bf16[1152,768]{1,0:T(8,128)(2,1)} %get-tuple-element.126), channel_id=1, source_target_pairs={{4,0},{5,1},{6,2},{7,3},{0,4},{1,5},{2,6},{3,7},{12,8},{13,9},{14,... | collective-permute-start | bytes 5308424 | tf_op jit(solution)/shard_map/ppermute | solution.py:30
  201.1 26.8 %collective-permute-start.43 = (bf16[192,768]{1,0:T(8,128)(2,1)}, bf16[192,768]{1,0:T(8,128)(2,1)}, u32[]{:S(2)}, u32[]{:S(2)}) collective-permute-start(bf16[192,768]{1,0:T(8,128)(2,1)} %slice.214), channel_id=1, source_target_pairs={{16,0},{17,1},{18,2},{19,3},{12,4},{13,5},{14,6},{15,7},{24,8},{25... | collective-permute-start | bytes 884744 | tf_op jit(solution)/shard_map/ppermute | solution.py:30
  209.3 43.8 %collective-permute-start.53 = (bf16[768,768]{1,0:T(8,128)(2,1)}, bf16[768,768]{1,0:T(8,128)(2,1)}, u32[]{:S(2)}, u32[]{:S(2)}) collective-permute-start(bf16[768,768]{1,0:T(8,128)(2,1)} %fusion.1), channel_id=1, source_target_pairs={{8,0},{9,1},{10,2},{11,3},{20,4},{21,5},{22,6},{23,7},{0,8},{1,9},... | collective-permute-start | bytes 3538952 | tf_op jit(solution)/shard_map/ppermute | solution.py:30
  227.8 27.7 %collective-permute-start.26 = (bf16[384,768]{1,0:T(8,128)(2,1)S(1)}, bf16[384,768]{1,0:T(8,128)(2,1)S(1)}, u32[]{:S(2)}, u32[]{:S(2)}) collective-permute-start(bf16[384,768]{1,0:T(8,128)(2,1)S(1)} %get-tuple-element.124), channel_id=1, source_target_pairs={{4,0},{5,1},{6,2},{7,3},{0,4},{1,5},{2,6},{3,7},{12,8},{13,9},{14,... | collective-permute-start | bytes 1769480 | tf_op jit(solution)/shard_map/ppermute | solution.py:30
  231.2 32.0 %collective-permute-start.44 = (bf16[384,768]{1,0:T(8,128)(2,1)}, bf16[384,768]{1,0:T(8,128)(2,1)}, u32[]{:S(2)}, u32[]{:S(2)}) collective-permute-start(bf16[384,768]{1,0:T(8,128)(2,1)} %get-tuple-element.176), channel_id=1, source_target_pairs={{8,0},{9,1},{10,2},{11,3},{20,4},{21,5},{22,6},{23,7},{0,8},{1,9},... | collective-permute-start | bytes 1769480 | tf_op jit(solution)/shard_map/ppermute | solution.py:30
  231.3 21.0 %collective-permute-start.48 = (bf16[384,768]{1,0:T(8,128)(2,1)S(1)}, bf16[384,768]{1,0:T(8,128)(2,1)S(1)}, u32[]{:S(2)}, u32[]{:S(2)}) collective-permute-start(bf16[384,768]{1,0:T(8,128)(2,1)S(1)} %get-tuple-element.177), channel_id=1, source_target_pairs={{8,0},{9,1},{10,2},{11,3},{20,4},{21,5},{22,6},{23,7},{0,8},{1,9},... | collective-permute-start | bytes 1769480 | tf_op jit(solution)/shard_map/ppermute | solution.py:30
  236.0 20.7 %collective-permute-start.31 = (bf16[288,768]{1,0:T(8,128)(2,1)}, bf16[288,768]{1,0:T(8,128)(2,1)}, u32[]{:S(2)}, u32[]{:S(2)}) collective-permute-start(bf16[288,768]{1,0:T(8,128)(2,1)} %slice.204), channel_id=1, source_target_pairs={{16,0},{17,1},{18,2},{19,3},{12,4},{13,5},{14,6},{15,7},{24,8},{25... | collective-permute-start | bytes 1327112 | tf_op jit(solution)/shard_map/ppermute | solution.py:30
  266.8 26.2 %collective-permute-start.50 = (bf16[192,768]{1,0:T(8,128)(2,1)}, bf16[192,768]{1,0:T(8,128)(2,1)}, u32[]{:S(2)}, u32[]{:S(2)}) collective-permute-start(bf16[192,768]{1,0:T(8,128)(2,1)} %add_convert_fusion.8), channel_id=1, source_target_pairs={{2,0},{3,1},{0,2},{1,3},{6,4},{7,5},{4,6},{5,7},{10,8},{11,9},{8,1... | collective-permute-start | bytes 884744 | tf_op jit(solution)/shard_map/ppermute | solution.py:30
  274.7 18.4 %collective-permute-start.55 = (bf16[192,768]{1,0:T(8,128)(2,1)}, bf16[192,768]{1,0:T(8,128)(2,1)}, u32[]{:S(2)}, u32[]{:S(2)}) collective-permute-start(bf16[192,768]{1,0:T(8,128)(2,1)} %get-tuple-element.165), channel_id=1, source_target_pairs={{3,0},{0,1},{1,2},{2,3},{7,4},{4,5},{5,6},{6,7},{11,8},{8,9},{9,10... | collective-permute-start | bytes 884744 | tf_op jit(solution)/shard_map/ppermute | solution.py:30
  275.7 19.0 %collective-permute-start.56 = (bf16[192,768]{1,0:T(8,128)(2,1)}, bf16[192,768]{1,0:T(8,128)(2,1)}, u32[]{:S(2)}, u32[]{:S(2)}) collective-permute-start(bf16[192,768]{1,0:T(8,128)(2,1)} %get-tuple-element.166), channel_id=1, source_target_pairs={{1,0},{2,1},{3,2},{0,3},{5,4},{6,5},{7,6},{4,7},{9,8},{10,9},{11,1... | collective-permute-start | bytes 884744 | tf_op jit(solution)/shard_map/ppermute | solution.py:30
  281.0 28.2 %collective-permute-start.29 = (bf16[96,768]{1,0:T(8,128)(2,1)}, bf16[96,768]{1,0:T(8,128)(2,1)}, u32[]{:S(2)}, u32[]{:S(2)}) collective-permute-start(bf16[96,768]{1,0:T(8,128)(2,1)} %constant_dynamic-slice_fusion.5), channel_id=1, source_target_pairs={{4,0},{5,1},{6,2},{7,3},{0,4},{1,5},{2,6},{3,7},{12,8},{13,9},{14,... | collective-permute-start | bytes 442376 | tf_op jit(solution)/shard_map/ppermute | solution.py:30
  324.8 30.4 %collective-permute-start.59 = (bf16[384,768]{1,0:T(8,128)(2,1)S(1)}, bf16[384,768]{1,0:T(8,128)(2,1)}, u32[]{:S(2)}, u32[]{:S(2)}) collective-permute-start(bf16[384,768]{1,0:T(8,128)(2,1)S(1)} %collective-permute-done.58.refs_2_), channel_id=1, source_target_pairs={{4,0},{5,1},{6,2},{7,3},{0,4},{1,5},{2,6},{3,7},{12,8},{13,9},{14,... | collective-permute-start | bytes 1769480 | tf_op jit(solution)/shard_map/ppermute | solution.py:30
  (145 other events, 1306.4 us)

commit v2 on v0

v2 whole, which is shorter than its diff:
```python
import functools

import jax
import jax.numpy as jnp
from jax import lax
from jax.experimental import pallas as pl
from jax.experimental.pallas import tpu as pltpu
from jax.sharding import PartitionSpec as P

HEAD_DIM = 64
EPSILON = 1e-05
MASKED = -1000000000.0
AXES = ("dp", "tensor")
BF = jnp.bfloat16
F32 = jnp.float32
MIB = 1024 * 1024
BIAS_ROWS = 16


class Moves:
    def __init__(self, dp_size, group):
        self.dp_size, self.group = dp_size, group

    def build(self, value, source):
        pairs = []
        for d in range(self.dp_size):
            for t in range(self.group):
                sd, st = source(d, t)
                pairs.append((sd * self.group + st, d * self.group + t))
        return lax.ppermute(value, AXES, pairs)

    def core(self, value):
        return self.build(value, lambda d, t: (d ^ 1, t))

    def near(self, value):
        return self.build(value, lambda d, t: (d ^ (4 if d & 1 else 2), t))

    def far(self, value):
        return self.build(value, lambda d, t: (d ^ (2 if d & 1 else 4), t))

    def fetch(self, value, turn):
        return self.build(value, lambda d, t: (d, (t + turn) % self.group))

    def give(self, value, turn):
        return self.build(value, lambda d, t: (d, (t - turn) % self.group))

    def flip(self, value, mask_dp, mask_t):
        return self.build(value, lambda d, t: (d ^ mask_dp, t ^ mask_t))


def after(value, *first):
    return lax.optimization_barrier((value, *first))[0]


def over_rest(values, dp_size):
    groups = [list(range(i, dp_size, 8)) for i in range(8)]
    return lax.psum(values.astype(F32), "dp", axis_index_groups=groups).astype(BF)


def sync(*values):
    return lax.optimization_barrier(values)


def gather_places(core, chip):
    near, over = chip ^ (1 + core), chip ^ (2 - core)
    own = ((core, chip), (core, near), (core, over), (core, chip ^ 3))
    return own + ((1 - core, chip), (1 - core, over), (1 - core, near), (1 - core, chip ^ 3))


class Block:
    def __init__(self, array, row=0, rows=None):
        self.array, self.row = array, row
        self.rows = array.shape[0] - row if rows is None else rows

    def at(self, row, rows):
        return Block(self.array, self.row + row, rows)


class Refs:
    def __init__(self):
        self.arrays = []

    def add(self, block):
        for index, array in enumerate(self.arrays):
            if array is block.array:
                return index, block.row
        self.arrays.append(block.array)
        return len(self.arrays) - 1, block.row


def dot_nn(left, right):
    return jnp.dot(left, right, preferred_element_type=F32)


def dot_nt(left, right):
    return lax.dot_general(left, right, (((1,), (1,)), ((), ())), preferred_element_type=F32)


def dot_tn(left, right):
    return lax.dot_general(left, right, (((0,), (0,)), ((), ())), preferred_element_type=F32)


def row_sum(values):
    return jnp.sum(values, axis=0, keepdims=True)


def where_am_i():
    dp = lax.axis_index("dp")
    return dp & 1, (dp >> 1) & 3


def copy_in(refs, layout, rows, out_ref, sems, place):
    started = []
    for index, ((part, where), (array, row)) in enumerate(zip(gather_places(*where_am_i()), layout)):
        start = pl.multiple_of(place(part, where), rows)
        copy = pltpu.make_async_copy(
            refs[array].at[pl.ds(row, rows)], out_ref.at[pl.ds(start, rows)], sems.at[index]
        )
        copy.start()
        started.append(copy)
    return started


def attn_place(rows):
    return lambda part, where: (2 * where + part) * rows


def ffn_place(rows):
    return lambda part, where: (part * 4 + where) * rows


def scatter_out(source_ref, rows, kept_ref, given_ref, base, place):
    core, chip = where_am_i()
    for ref, mine, first in ((kept_ref, core, 0), (given_ref, 1 - core, base)):
        for slot, where in enumerate((chip ^ (1 + mine), chip ^ (2 - mine), chip ^ 3, chip)):
            start = pl.multiple_of(place(mine, where), rows)
            begin = first + slot * rows
            ref[begin : begin + rows, :] = source_ref[pl.ds(start, rows), :]


def block_of(values, chain, head, seq):
    return values[head * HEAD_DIM : (head + 1) * HEAD_DIM, chain * seq : (chain + 1) * seq]


def attend(width, seq, lengths, mixed, mats, bias, qkv, soft, ctx):
    chains = mixed.shape[0] // seq
    heads = width // HEAD_DIM
    base = lax.axis_index("tensor") * chains
    column = jnp.broadcast_to(bias, (8, bias.shape[1])).T[:, :1]
    scale = HEAD_DIM**-0.5
    parts = []
    for index in range(3):
        cut = slice(index * width, (index + 1) * width)
        values = dot_nt(mats[index], mixed)
        if index != 1:
            values = values + column[cut]
        parts.append(values.astype(BF))
    scaled = (parts[0].astype(F32) * scale).astype(BF)
    for index, values in enumerate((scaled, parts[1], parts[2])):
        qkv[index * width : (index + 1) * width, :] = values
    position = lax.broadcasted_iota(jnp.int32, (seq, 1), 0)
    blocks = [(chain, head) for chain in range(chains) for head in range(heads)]
    scores = [
        jnp.where(
            position < lengths[base + chain],
            dot_tn(block_of(parts[1], chain, head, seq), block_of(scaled, chain, head, seq)),
            MASKED,
        )
        for chain, head in blocks
    ]
    shifted = [jnp.exp(value - jnp.max(value, axis=0, keepdims=True)) for value in scores]
    weights = [(value * (1.0 / row_sum(value))).astype(BF) for value in shifted]
    for index, (chain, head) in enumerate(blocks):
        soft[index] = weights[index]
        ctx[head * HEAD_DIM : (head + 1) * HEAD_DIM, chain * seq : (chain + 1) * seq] = dot_nn(
            block_of(parts[2], chain, head, seq), weights[index]
        ).astype(BF)
    return dot_tn(ctx[...], mats[3])


def norm_back(grad, hat, inv, gain):
    scaled = grad * gain
    mean_one = jnp.mean(scaled, axis=1, keepdims=True)
    mean_two = jnp.mean(scaled * hat, axis=1, keepdims=True)
    return inv * (scaled - mean_one - hat * mean_two)


def norm_parts(values):
    centred = values - jnp.mean(values, axis=1, keepdims=True)
    inv = lax.rsqrt(jnp.mean(centred * centred, axis=1, keepdims=True) + EPSILON)
    return centred * inv, inv


def in_span(starts, counts, chain, chains, seq):
    index = lax.axis_index("tensor") * chains + chain
    position = lax.broadcasted_iota(jnp.int32, (seq, 1), 0)
    return (position >= starts[index]) & (position < starts[index] + counts[index])


EMBED, B_OUT, G_ATTN, S_ATTN, B_BACK, G_FFN, S_FFN = range(7)


def prep_kernel(half, piece, bias, wq, wk, wv, wo, w_in, w_back, attn_mine, ffn_mine, sems):
    core, chip = where_am_i()
    copies = [pltpu.make_async_copy(bias, attn_mine.at[pl.ds(half, BIAS_ROWS)], sems.at[0])]
    copies[0].start()
    for index, ref in enumerate((wq, wk, wv, wo)):
        start = pl.multiple_of(core * half, half)
        copy = pltpu.make_async_copy(
            ref.at[pl.ds(start, half)], attn_mine.at[pl.ds(0, half)], sems.at[1]
        )
        pl.when(chip == index)(copy.start)
    copies.append(copy)
    for index, ref in enumerate((w_in, w_back)):
        start = pl.multiple_of(chip * piece, piece)
        copy = pltpu.make_async_copy(ref.at[pl.ds(start, piece)], ffn_mine, sems.at[2])
        pl.when(core == index)(copy.start)
    copies.append(copy)
    for copy in copies:
        copy.wait()


def attn_own_kernel(
    width, seq, lengths, starts, counts, hidden, vecs, bias, wq, wk, wv, wo, mixed, qkv, soft, ctx, part
):
    chains = hidden.shape[0] // seq
    for chain in range(chains):
        rows = slice(chain * seq, (chain + 1) * seq)
        span = in_span(starts, counts, chain, chains, seq)
        mixed[rows, :] = jnp.where(span, vecs[EMBED : EMBED + 1, :], hidden[rows, :].astype(F32)).astype(BF)
    mats = (wq[...], wk[...], wv[...], wo[...])
    part[...] = attend(
        width, seq, lengths, mixed[...], mats, bias[1:2, :].astype(F32), qkv, soft, ctx
    )


def attn_mats(mats, width):
    return [mats[i * width : (i + 1) * width, :] for i in range(4)]


def attn_turn_kernel(
    width, seq, layout, last, part_rows, count, lengths, mixed, part, vecs, first, *refs
):
    pieces, refs = refs[:count], refs[count:]
    qkv, soft, ctx, bias_in, mats = refs[:5]
    sems = refs[-1]
    copies = copy_in(pieces, layout, part_rows, mats, sems, attn_place(part_rows))
    bias_in[...] = jnp.broadcast_to(first[part_rows : part_rows + 1, :].astype(F32), bias_in.shape)
    for copy in copies:
        copy.wait()
    bias = first[part_rows + 1 : part_rows + 2, :].astype(F32)
    total = part[...] + attend(
        width, seq, lengths, mixed[...], attn_mats(mats, width), bias, qkv, soft, ctx
    )
    if not last:
        refs[5][...] = total
        return
    hat, inv, normed = refs[5:8]
    ahat, ainv = norm_parts(total + mixed[...].astype(F32) + vecs[B_OUT : B_OUT + 1, :])
    hat[...] = ahat
    inv[...] = jnp.broadcast_to(ainv, inv.shape)
    normed[...] = (ahat * vecs[G_ATTN : G_ATTN + 1, :] + vecs[S_ATTN : S_ATTN + 1, :]).astype(BF)


def gelu_both(pre):
    cdf = 0.5 * (1.0 + lax.erf(pre * (0.5**0.5)))
    pdf = jnp.exp(-0.5 * pre * pre) * (0.5 / 3.141592653589793) ** 0.5
    return pre * cdf, cdf + pre * pdf


def ffn_step(normed, mat_in, mat_back, bias, act, slope):
    pre = dot_nn(normed[...], mat_in) + bias
    value, rate = gelu_both(pre)
    act[...] = value.astype(BF)
    slope[...] = rate.astype(BF)
    return dot_nn(act[...], mat_back)


def ffn_own_kernel(normed, mat_in, mat_back, bias, act, slope, total):
    total[...] = ffn_step(
        normed, mat_in[...], mat_back[...], bias[0:1, :].astype(F32), act, slope
    )


def ffn_rest_kernel(part_rows, layout, last, count, normed, part, bias_in, *refs):
    if last:
        (hat1, vecs, cot), refs = refs[:3], refs[3:]
    pieces, refs = refs[:count], refs[count:]
    act, slope, mats = refs[:3]
    sems = refs[-1]
    copies = copy_in(pieces, layout, part_rows, mats, sems, ffn_place(part_rows))
    height = 4 * part_rows
    for copy in copies:
        copy.wait()
    value = part[...] + ffn_step(
        normed, mats[:height, :], mats[height:, :], bias_in[0:1, :], act, slope
    )
    if not last:
        refs[3][...] = value
        return
    layer_out, grad_second, grad_low, small = refs[3:7]
    first = hat1[...] * vecs[G_ATTN : G_ATTN + 1, :] + vecs[S_ATTN : S_ATTN + 1, :]
    hat, inv = norm_parts(first + value + vecs[B_BACK : B_BACK + 1, :])
    gain = vecs[G_FFN : G_FFN + 1, :]
    layer_out[...] = (hat * gain + vecs[S_FFN : S_FFN + 1, :]).astype(BF)
    grad = cot[...].astype(F32)
    back = norm_back(grad, hat, inv, gain)
    grad_second[...] = back
    grad_low[...] = back.astype(BF)
    small[0:1, :] = row_sum(grad * hat)
    small[1:2, :] = row_sum(grad)
    small[2:3, :] = row_sum(back)
    small[3:, :] = jnp.zeros_like(small[3:, :])


def ffn_back_kernel(counts, part_rows, grad_low, normed, part, *refs):
    turns = []
    for count in counts:
        act, slope, *mats = refs[: 2 + count]
        refs = refs[2 + count :]
        turns.append((act, slope, mats))
    kepts, refs = refs[: len(turns)], refs[len(turns) :]
    given, total, bias_grad, whole = refs
    height = 4 * part_rows
    value = part[...]
    bias_grad[...] = jnp.zeros_like(bias_grad)
    for index, (act, slope, mats) in enumerate(turns):
        if len(mats) == 2:
            mat_in, mat_back = mats[0][...], mats[1][...]
        else:
            mat_in, mat_back = mats[0][:height, :], mats[0][height:, :]
        whole[height:, :] = dot_tn(act[...], grad_low[...]).astype(BF)
        grad_act = dot_nt(grad_low[...], mat_back)
        grad_pre = (grad_act * slope[...].astype(F32)).astype(BF)
        bias_grad[index : index + 1, :] = row_sum(grad_pre.astype(F32))
        whole[:height, :] = dot_tn(normed[...], grad_pre).astype(BF)
        value = value + dot_nt(grad_pre, mat_in)
        base = index * 4 * part_rows
        scatter_out(whole, part_rows, kepts[index], given, base, ffn_place(part_rows))
    total[...] = value


def attend_back(width, seq, grad_low, mats, mixed, qkv, soft, ctx, grad_qkv, whole):
    chains = grad_low.shape[0] // seq
    heads = width // HEAD_DIM
    scale = HEAD_DIM**-0.5
    whole[3 * width :, :] = dot_nn(ctx[...], grad_low).astype(BF)
    grad_ctx = dot_nt(mats[3], grad_low).astype(BF)
    queries, keys, values = (qkv[i * width : (i + 1) * width, :] for i in range(3))
    blocks = [(chain, head) for chain in range(chains) for head in range(heads)]
    grad_weights = [
        dot_tn(block_of(values, chain, head, seq), block_of(grad_ctx, chain, head, seq))
        for chain, head in blocks
    ]
    grad_scores = []
    for index, value in enumerate(grad_weights):
        wide = soft[index].astype(F32)
        product = wide * value
        grad_scores.append((product - wide * row_sum(product)).astype(BF))
    for index, (chain, head) in enumerate(blocks):
        columns = slice(chain * seq, (chain + 1) * seq)
        for slot, value in enumerate(
            (
                dot_nn(block_of(keys, chain, head, seq), grad_scores[index]) * scale,
                dot_nt(block_of(queries, chain, head, seq), grad_scores[index]),
                dot_nt(block_of(grad_ctx, chain, head, seq), soft[index]),
            )
        ):
            start = slot * width + head * HEAD_DIM
            grad_qkv[start : start + HEAD_DIM, columns] = value.astype(BF)
    whole[: 3 * width, :] = dot_nn(grad_qkv[...], mixed).astype(BF)
    ones = jnp.ones((8, grad_low.shape[0]), BF)
    back = dot_tn(grad_qkv[:width, :], mats[0])
    back = back + dot_tn(grad_qkv[width : 2 * width, :], mats[1])
    back = back + dot_tn(grad_qkv[2 * width :, :], mats[2])
    return back, dot_nt(ones, grad_qkv[...])


def attn_back_kernel(width, seq, own, first, part_rows, counts, mixed, part, *refs):
    if first:
        (hat, inv, vecs), refs = refs[:3], refs[3:]
    else:
        (grad_low,), refs = refs[:1], refs[1:]
    if own:
        (starts, counts_ref), refs = refs[:2], refs[2:]
    turns = []
    for count in counts:
        qkv, soft, ctx, *mats = refs[: 3 + count]
        refs = refs[3 + count :]
        turns.append((qkv, soft, ctx, mats))
    kepts, refs = refs[: len(turns)], refs[len(turns) :]
    given, total, bias_grad = refs[:3]
    refs = refs[3:]
    if first:
        (grad_low, small), refs = refs[:2], refs[2:]
    grad_qkv, whole = refs
    if first:
        grad = part[...]
        value = norm_back(grad, hat[...], inv[:, :1], vecs[G_ATTN : G_ATTN + 1, :])
        grad_low[...] = value.astype(BF)
        small[0:1, :] = row_sum(grad * hat[...])
        small[1:2, :] = row_sum(grad)
        small[2:3, :] = row_sum(value)
        small[3:, :] = jnp.zeros_like(small[3:, :])
    else:
        value = part[...]
    bias_grad[...] = jnp.zeros_like(bias_grad)
    for index, (qkv, soft, ctx, refs_in) in enumerate(turns):
        mats = [ref[...] for ref in refs_in] if len(refs_in) == 4 else attn_mats(refs_in[0], width)
        back, sums = attend_back(
            width, seq, grad_low[...], mats, mixed[...], qkv, soft, ctx, grad_qkv, whole
        )
        value = value + back
        bias_grad[index : index + 1, :width] = sums[0:1, :width]
        bias_grad[index : index + 1, width : 2 * width] = sums[0:1, 2 * width :]
        base = index * 4 * part_rows
        scatter_out(whole, part_rows, kepts[index], given, base, attn_place(part_rows))
    if not own:
        total[...] = value
        return
    chains = value.shape[0] // seq
    embed_sum = jnp.zeros((1, value.shape[1]), F32)
    for chain in range(chains):
        rows = slice(chain * seq, (chain + 1) * seq)
        span = in_span(starts, counts_ref, chain, chains, seq)
        total[rows, :] = jnp.where(span, 0.0, value[rows, :]).astype(BF)
        embed_sum = embed_sum + row_sum(jnp.where(span, value[rows, :], 0.0))
    bias_grad[1:2, :] = embed_sum


def mix_kernel(count, plan, *refs):
    for out, blocks in zip(refs[count:], plan):
        start = 0
        for rows, sources in blocks:
            array, row = sources[0]
            value = refs[array][row : row + rows, :]
            if len(sources) > 1:
                value = value.astype(F32)
                for array, row in sources[1:]:
                    value = value + refs[array][row : row + rows, :].astype(F32)
                value = value.astype(BF)
            out[start : start + rows, :] = value
            start += rows


def ffn_out_kernel(part_rows, layout, count, *refs):
    outs = refs[count:]
    for (array, row), (part, where) in zip(layout, gather_places(*where_am_i())):
        start = pl.multiple_of(where * part_rows, part_rows)
        for index in range(2):

            @pl.when(part == index)
            def _():
                block = refs[array][row : row + part_rows, :]
                outs[index][pl.ds(start, part_rows), :] = block.astype(F32)


def attn_out_kernel(part_rows, layout, count, *refs):
    outs = refs[count:]
    for (array, row), (part, where) in zip(layout, gather_places(*where_am_i())):
        start = pl.multiple_of(part * part_rows, part_rows)
        for index in range(4):

            @pl.when(where == index)
            def _():
                block = refs[array][row : row + part_rows, :]
                outs[index][pl.ds(start, part_rows), :] = block.astype(F32)


def small_kernel(group, rows_of, small_ffn, small_attn, *refs):
    out = refs[-1]
    rank = lax.axis_index("tensor")
    out[...] = jnp.zeros_like(out)
    out[0:3, :] = small_ffn[0:3, :]
    out[3:6, :] = small_attn[0:3, :]
    for index, (array, source) in enumerate(rows_of[:-1]):
        row = 8 + index // group * group + lax.rem(index % group + rank, group)
        out[pl.ds(row, 1), :] = refs[array][source : source + 1, :]
    array, source = rows_of[-1]
    out[6:7, :] = refs[array][source : source + 1, :]


SMEM = pl.BlockSpec(memory_space=pltpu.SMEM)
VMEM = pl.BlockSpec(memory_space=pltpu.VMEM)
ANY = pl.BlockSpec(memory_space=pl.ANY)


def call(kernel, ins, outs, scratch=(), flops=0, vmem=16, name=None):
    arrays = [array for array, _ in ins]
    moved = sum(a.size * a.dtype.itemsize for a in arrays) + sum(
        o.size * o.dtype.itemsize for o in outs
    )
    return pl.pallas_call(
        kernel,
        in_specs=[spec for _, spec in ins],
        out_specs=[VMEM] * len(outs),
        out_shape=list(outs),
        scratch_shapes=list(scratch),
        compiler_params=pltpu.CompilerParams(vmem_limit_bytes=vmem * MIB),
        cost_estimate=pl.CostEstimate(flops=flops // 100, bytes_accessed=moved // 100, transcendentals=0),
        name=name,
    )(*arrays)


def shape(rows, columns, kind=F32):
    return jax.ShapeDtypeStruct((rows, columns), kind)


def mix(*outs, name=None):
    refs, plan, shapes = Refs(), [], []
    for blocks in outs:
        mine = []
        for block in blocks:
            sources = block if isinstance(block, list) else [block]
            mine.append((sources[0].rows, tuple(refs.add(source) for source in sources)))
        plan.append(tuple(mine))
        first = blocks[0][0] if isinstance(blocks[0], list) else blocks[0]
        shapes.append(shape(sum(rows for rows, _ in mine), first.array.shape[1], BF))
    return call(
        functools.partial(mix_kernel, len(refs.arrays), tuple(plan)),
        [(array, VMEM) for array in refs.arrays],
        shapes,
        vmem=4,
        name=name,
    )


def on_device(
    hidden_in,
    lengths,
    span_start,
    span_len,
    mask_embed,
    w_query,
    b_query,
    w_key,
    w_value,
    b_value,
    w_out,
    b_out,
    g_attn,
    s_attn,
    w_in,
    b_in,
    w_back,
    b_back,
    g_ffn,
    s_ffn,
    cotangent,
):
    group = lax.axis_size("tensor")
    dp_size = lax.axis_size("dp")
    moves = Moves(dp_size, group)
    rank = lax.axis_index("tensor")
    rows, model = hidden_in.shape
    seq = rows * group // lengths.shape[0]
    chains = rows // seq
    width = w_query.shape[1]
    heads = width // HEAD_DIM
    hidden = w_in.shape[1]
    piece = model // 4
    half = piece // 2
    turns = (1, 3, 2)
    count = len(turns)

    vecs = jnp.stack(
        (mask_embed, b_out, g_attn, s_attn, b_back, g_ffn, s_ffn, jnp.zeros_like(b_out))
    ).astype(F32)
    none = jnp.zeros((width,), BF)
    bias_pack = jnp.pad(
        jnp.stack((b_in, jnp.concatenate((b_query, none, b_value, none)))),
        ((0, BIAS_ROWS - 2), (0, 0)),
    )
    own_mats = (w_query.T, w_key.T, w_value.T, w_out)
    dma = lambda n: pltpu.SemaphoreType.DMA((8 * n,))

    attn_mine, ffn_mine = call(
        functools.partial(prep_kernel, half, piece),
        [(v, ANY) for v in (bias_pack, *own_mats, w_in, w_back)],
        [shape(half + BIAS_ROWS, model, BF), shape(piece, model, BF)],
        [pltpu.SemaphoreType.DMA((3,))],
        vmem=60,
        name="prep",
    )
    first1, first3 = (moves.fetch(attn_mine, turn) for turn in turns[:2])

    soft_shape = jax.ShapeDtypeStruct((chains * heads, seq, seq), BF)
    turn_flops = 2 * rows * model * 4 * width
    mixed, qkv_own, soft_own, ctx_own, attn_part = call(
        functools.partial(attn_own_kernel, width, seq),
        [(v, SMEM) for v in (lengths, span_start, span_len)]
        + [(v, VMEM) for v in (hidden_in, vecs, bias_pack, *own_mats)],
        [
            shape(rows, model, BF),
            shape(3 * width, rows, BF),
            soft_shape,
            shape(width, rows, BF),
            shape(rows, model),
        ],
        flops=turn_flops,
        name="attn_own",
    )
    first1, first3, mixed, attn_mine, ffn_mine = sync(first1, first3, mixed, attn_mine, ffn_mine)
    first2 = moves.fetch(attn_mine, 2)
    (mine13,) = mix([Block(first1, 0, half), Block(first3, 0, half)], name="mix_1")
    near13, over13 = moves.near(mine13), moves.far(mine13)

    first2, near13, over13, ffn_mine = sync(first2, near13, over13, ffn_mine)
    ffn1 = moves.fetch(ffn_mine, 1)
    mine2, far = mix([Block(first2, 0, half)], [Block(near13), Block(first2, 0, half)], name="mix_2")
    near2, far13_2 = moves.near(mine2), moves.far(far)

    ffn1, near2, far13_2, ffn_mine = sync(ffn1, near2, far13_2, ffn_mine)
    ffn3 = moves.fetch(ffn_mine, 3)
    own13 = (Block(mine13), Block(near13), Block(over13), Block(far13_2, 0, 2 * half))
    far, other13 = mix([Block(near2), Block(ffn1)], own13, name="mix_3")
    near_f1, far2_f1, other13 = moves.near(ffn1), moves.far(far), moves.core(other13)

    ffn3, near_f1, far2_f1, other13, ffn_mine = sync(ffn3, near_f1, far2_f1, other13, ffn_mine)
    ffn2 = moves.fetch(ffn_mine, 2)
    own2 = (Block(mine2), Block(near2), Block(far13_2, 2 * half, half), Block(far2_f1, 0, half))
    far, other2 = mix([Block(near_f1), Block(ffn3)], own2, name="mix_4")
    near_f3, far_f1_f3, other2 = moves.near(ffn3), moves.far(far), moves.core(other2)

    def parts(own, other, turn=0, rows=None):
        rows = own[0].rows if rows is None else rows
        blocks = [block.at(turn * rows, rows) for block in own]
        count_turns = own[0].rows // rows
        return blocks + [Block(other, (i * count_turns + turn) * rows, rows) for i in range(4)]

    qkvs, softs, ctxs, bias_ins, attn_wholes = [], [], [], [], []
    for index, first in enumerate((first1, first3, first2)):
        last = index == count - 1
        if last:
            ffn2, near_f3, far_f1_f3, other2, attn_part = sync(ffn2, near_f3, far_f1_f3, other2, attn_part)
            own_f1 = (Block(ffn1), Block(near_f1), Block(far2_f1, half, piece), Block(far_f1_f3, 0, piece))
            far, other_f1 = mix([Block(near_f3), Block(ffn2)], own_f1, name="mix_5")
            near_f2, far_f3_f2, other_f1 = moves.near(ffn2), moves.far(far), moves.core(other_f1)
        blocks = parts(own2, other2) if last else parts(own13, other13, index, half)
        refs = Refs()
        layout = tuple(refs.add(block) for block in blocks)
        outs = [shape(3 * width, rows, BF), soft_shape, shape(width, rows, BF), shape(8, model)]
        outs += [shape(model, model, BF), shape(rows, model)]
        if last:
            outs += [shape(rows, 128), shape(rows, model, BF)]
        qkv, soft, ctx, bias_in, whole, *others = call(
            functools.partial(attn_turn_kernel, width, seq, layout, last, half, len(refs.arrays)),
            [(lengths, SMEM), (mixed, VMEM), (attn_part, VMEM), (vecs, VMEM), (first, VMEM)]
            + [(array, ANY) for array in refs.arrays],
            outs,
            [dma(1)],
            flops=turn_flops,
            name=f"attn_{turns[index]}",
        )
        for values, value in zip((qkvs, softs, ctxs, bias_ins, attn_wholes), (qkv, soft, ctx, bias_in, whole)):
            values.append(value)
        attn_part = others[0]
    hat1, inv1, normed = others

    ffn_flops = 2 * rows * model * hidden * 2
    act_own, slope_own, ffn_part = call(
        ffn_own_kernel,
        [(normed, VMEM), (w_in, VMEM), (w_back, VMEM), (bias_pack, VMEM)],
        [shape(rows, hidden, BF), shape(rows, hidden, BF), shape(rows, model)],
        flops=ffn_flops,
        name="ffn_own",
    )
    near_f2, far_f3_f2, other_f1, ffn_part = sync(near_f2, far_f3_f2, other_f1, ffn_part)
    own_f3 = (Block(ffn3), Block(near_f3), Block(far_f1_f3, piece, piece), Block(far_f3_f2, 0, piece))
    (other_f3,) = mix(own_f3, name="mix_6")
    far_f2, other_f3 = moves.far(near_f2), moves.core(other_f3)
    acts, slopes, ffn_wholes = [], [], []
    for index in range(count):
        last = index == count - 1
        if index == 0:
            blocks = parts(own_f1, other_f1)
        elif index == 1:
            far_f2, other_f3, ffn_part = sync(far_f2, other_f3, ffn_part)
            own_f2 = (Block(ffn2), Block(near_f2), Block(far_f3_f2, piece, piece), Block(far_f2))
            (other_f2,) = mix(own_f2, name="mix_7")
            other_f2 = moves.core(other_f2)
            blocks = parts(own_f3, other_f3)
        else:
            blocks = parts(own_f2, other_f2)
        refs = Refs()
        layout = tuple(refs.add(block) for block in blocks)
        ins = [(normed, VMEM), (ffn_part, VMEM), (bias_ins[index], VMEM)]
        outs = [shape(rows, hidden, BF)] * 2 + [shape(2 * model, model, BF)]
        if last:
            ins += [(hat1, VMEM), (vecs, VMEM), (cotangent, VMEM)]
            outs += [shape(rows, model, BF), shape(rows, model), shape(rows, model, BF), shape(8, model)]
        else:
            outs += [shape(rows, model)]
        act, slope, whole, *others = call(
            functools.partial(ffn_rest_kernel, piece, layout, last, len(refs.arrays)),
            ins + [(array, ANY) for array in refs.arrays],
            outs,
            [dma(1)],
            flops=ffn_flops,
            name=f"ffn_{turns[index]}",
        )
        for values, value in zip((acts, slopes, ffn_wholes), (act, slope, whole)):
            values.append(value)
        if last:
            layer_out, grad_second, grad_low, small_ffn = others
        else:
            (ffn_part,) = others

    def ffn_back(part, *turns_in, name):
        kinds = tuple(len(turn) - 2 for turn in turns_in)
        *kepts, given, part, bias = call(
            functools.partial(ffn_back_kernel, kinds, piece),
            [(v, VMEM) for v in (grad_low, normed, part)] + [(v, VMEM) for turn in turns_in for v in turn],
            [shape(4 * piece, model, BF)] * len(kinds)
            + [shape(4 * len(kinds) * piece, model, BF), shape(rows, model), shape(8, model)],
            [pltpu.VMEM((2 * model, model), BF)],
            flops=2 * len(kinds) * ffn_flops,
            name=name,
        )
        return kepts, given, part, bias

    def attn_back(part, grad_low, *turns_in, own=False, name):
        first = grad_low is None
        kinds = tuple(len(turn) - 3 for turn in turns_in)
        ins = [(mixed, VMEM), (part, VMEM)]
        ins += [(v, VMEM) for v in (hat1, inv1, vecs)] if first else [(grad_low, VMEM)]
        if own:
            ins += [(span_start, SMEM), (span_len, SMEM)]
        ins += [(v, VMEM) for turn in turns_in for v in turn]
        outs = [shape(4 * half, model, BF)] * len(kinds)
        outs += [shape(4 * len(kinds) * half, model, BF)]
        outs += [shape(rows, model, BF if own else F32), shape(8, model)]
        if first:
            outs += [shape(rows, model, BF), shape(8, model)]
        return call(
            functools.partial(attn_back_kernel, width, seq, own, first, half, kinds),
            ins,
            outs,
            [pltpu.VMEM((3 * width, rows), BF), pltpu.VMEM((model, model), BF)],
            flops=2 * len(kinds) * turn_flops,
            name=name,
        )

    def ffn_turn(index):
        return (acts[index], slopes[index], ffn_wholes[index])

    def attn_turn(index):
        return (qkvs[index], softs[index], ctxs[index], attn_wholes[index])

    class Slots:
        def __init__(self, kept, come, row=0, more=()):
            self.rows = kept.shape[0] // 4
            self.pieces = [(kept, 0), (come, row), *more]

        def slot(self, index):
            start = index * self.rows
            return [Block(array, row + start, self.rows) for array, row in self.pieces]

    (kept1,), given1, part, bias1 = ffn_back(grad_second, ffn_turn(0), name="ffn_back_1")
    come1 = moves.core(given1)
    (kept3,), given3, part, bias3 = ffn_back(part, ffn_turn(1), name="ffn_back_3")
    come1, kept3, given3, part = sync(come1, kept3, given3, part)

    cut_rows = (2 * piece, 2 * piece)
    early = mix(
        *([[Block(kept1, i * 2 * piece, n), Block(come1, i * 2 * piece, n)]] for i, n in enumerate(cut_rows)),
        name="mix_8",
    )
    part, given3, *early = sync(part, given3, *early)
    early[0] = moves.give(early[0], 1)
    come3 = moves.core(given3)
    (kept2, kept0), given20, part, bias20 = ffn_back(
        part, ffn_turn(2), (act_own, slope_own, w_in, w_back), name="ffn_back_20"
    )
    come3, given20, part, *early = sync(come3, given20, part, *early)

    f3 = Slots(kept3, come3)
    (far,) = mix([f3.slot(2), f3.slot(1)], name="mix_9")
    far, given20, part = sync(far, given20, part)
    far_f3 = moves.far(far)
    come20 = moves.core(given20)
    a_kept2, a_given2, part, a_bias2, attn_low, small_attn = attn_back(
        part, None, attn_turn(2), name="attn_back_2"
    )
    far_f3, come20, a_given2, part, *early = sync(far_f3, come20, a_given2, part, *early)

    f2 = Slots(kept2, come20)
    near, far = mix(
        [[*f3.slot(0), Block(far_f3, 0, piece)]],
        [f2.slot(2), f2.slot(1)],
        name="mix_10",
    )
    near, far, early[1], part, a_given2 = sync(near, far, early[1], part, a_given2)
    early[1] = moves.give(early[1], 1)
    near_f3, far_f2, a_come2 = moves.near(near), moves.far(far), moves.core(a_given2)
    a_kept1, a_kept3, a_given13, part, a_bias13 = attn_back(
        part, attn_low, attn_turn(0), attn_turn(1), name="attn_back_13"
    )
    near_f3, far_f2, a_come2, a_given13, part, *early = sync(
        near_f3, far_f2, a_come2, a_given13, part, *early
    )

    class Early:
        def slot(self, index):
            return Block(early[index // 2], index % 2 * piece, piece)

    f0 = Slots(kept0, come20, 4 * piece)
    a2 = Slots(a_kept2, a_come2)
    f0_slot = lambda index: f0.slot(index) + [Early().slot(index)]
    done3, near, far = mix(
        [[*f3.slot(3), Block(near_f3), Block(far_f3, piece, piece)]],
        [[*f2.slot(0), Block(far_f2, 0, piece)]],
        [f0_slot(2), a2.slot(2), f0_slot(1), a2.slot(1)],
        name="mix_11",
    )
    done3, near, far, part, a_given13 = sync(done3, near, far, part, a_given13)
    done3 = moves.give(done3, 3)
    near_f2, far_f0_a2, a_come13 = moves.near(near), moves.far(far), moves.core(a_given13)
    a_kept0, a_given0, grad_input, a_bias0 = attn_back(
        part, attn_low, (qkv_own, soft_own, ctx_own, *own_mats), own=True, name="attn_back_0"
    )
    near_f2, far_f0_a2, a_come13, done3, a_given0, grad_input, a_bias0 = sync(
        near_f2, far_f0_a2, a_come13, done3, a_given0, grad_input, a_bias0
    )

    wide = piece + half
    a1, a3 = Slots(a_kept1, a_come13), Slots(a_kept3, a_come13, 4 * half)
    done2, near, far = mix(
        [[*f2.slot(3), Block(near_f2), Block(far_f2, piece, piece)]],
        [[*f0_slot(0), Block(far_f0_a2, 0, piece)], [*a2.slot(0), Block(far_f0_a2, piece, half)]],
        [a1.slot(2), a3.slot(2), a1.slot(1), a3.slot(1)],
        name="mix_12",
    )
    biases = (bias20, bias1, bias3, a_bias0, a_bias13, a_bias2)
    rows_of = ((0, 1), (1, 0), (0, 0), (2, 0), (3, 0), (4, 0), (5, 0), (4, 1), (3, 1))
    (small,) = call(
        functools.partial(small_kernel, group, rows_of),
        [(v, VMEM) for v in (small_ffn, small_attn, *biases)],
        [shape(8 + 2 * group, model)],
        vmem=4,
        name="small",
    )
    flips = [(1 << bit, 0) for bit in range(dp_size.bit_length() - 1)]
    flips += [(0, 1 << bit) for bit in range(group.bit_length() - 1)]

    def small_step(value):
        return value + moves.flip(value, *flips.pop(0))

    done2, near, far, a_given0 = sync(done2, near, far, a_given0)
    done2 = moves.give(done2, 2)
    near_f0_a2, far_a13, a_come0 = moves.near(near), moves.far(far), moves.core(a_given0)
    small = small_step(small)
    near_f0_a2, far_a13, a_come0, done2, small = sync(near_f0_a2, far_a13, a_come0, done2, small)

    a0 = Slots(a_kept0, a_come0)
    over0 = Block(far_f0_a2, wide, piece)
    ffn_final, a_done2, near, far = mix(
        [[*f0_slot(3), Block(near_f0_a2, 0, piece), over0, Block(done3), Block(done2)]],
        [[*a2.slot(3), Block(near_f0_a2, piece, half), Block(far_f0_a2, wide + piece, half)]],
        [[*a1.slot(0), Block(far_a13, 0, half)], [*a3.slot(0), Block(far_a13, half, half)]],
        [a0.slot(2), a0.slot(1)],
        name="mix_13",
    )
    if dp_size > 8:
        ffn_final = over_rest(ffn_final, dp_size)
    near, far = mix([Block(near), Block(ffn_final)], [Block(far), Block(ffn_final)], name="mix_14")
    a_done2, near, far = sync(a_done2, near, far)
    a_done2 = moves.give(a_done2, 2)
    near_a13_f, far_a0_f = moves.near(near), moves.far(far)
    small = small_step(small)
    near_a13_f, far_a0_f, a_done2, small = sync(near_a13_f, far_a0_f, a_done2, small)

    a_done1, a_done3, near, far = mix(
        [[*a1.slot(3), Block(near_a13_f, 0, half), Block(far_a13, 2 * half, half)]],
        [[*a3.slot(3), Block(near_a13_f, half, half), Block(far_a13, 3 * half, half)]],
        [[*a0.slot(0), Block(far_a0_f, 0, half)]],
        [Block(near_a13_f, 2 * half, piece)],
        name="mix_15",
    )
    a_done1, a_done3, near, far = sync(a_done1, a_done3, near, far)
    a_done1, a_done3 = moves.give(a_done1, 1), moves.give(a_done3, 3)
    near_a0, ffn_corner = moves.near(near), moves.far(far)
    small = small_step(small)
    a_done1, a_done3, near_a0, ffn_corner, small = sync(a_done1, a_done3, near_a0, ffn_corner, small)

    own_ffn = (
        Block(ffn_final),
        Block(near_a13_f, 2 * half, piece),
        Block(far_a0_f, 2 * half, piece),
        Block(ffn_corner),
    )
    attn_final, other_ffn = mix(
        [[*a0.slot(3), Block(near_a0), Block(far_a0_f, half, half), *map(Block, (a_done1, a_done2, a_done3))]],
        own_ffn,
        name="mix_16",
    )
    if dp_size > 8:
        attn_final = over_rest(attn_final, dp_size)
    attn_final, other_ffn = sync(attn_final, other_ffn)
    attn_near, attn_over, other_ffn = moves.near(attn_final), moves.far(attn_final), moves.core(other_ffn)
    small = small_step(small)
    attn_near, attn_over, other_ffn, small = sync(attn_near, attn_over, other_ffn, small)

    attn_corner = moves.far(attn_near)
    while flips:
        small = small_step(small)

    def out(kernel, rows_in, own, other, outs, name):
        refs = Refs()
        layout = tuple(refs.add(block) for block in parts(own, other))
        return call(
            functools.partial(kernel, rows_in, layout, len(refs.arrays)),
            [(array, VMEM) for array in refs.arrays],
            outs,
            name=name,
        )

    outs = [shape(model, hidden), shape(hidden, model)]
    grad_w_in, grad_w_back = out(ffn_out_kernel, piece, own_ffn, other_ffn, outs, "ffn_out")
    attn_corner, grad_w_in, grad_w_back, small = sync(attn_corner, grad_w_in, grad_w_back, small)
    own_attn = tuple(map(Block, (attn_final, attn_near, attn_over, attn_corner)))
    (other_attn,) = mix(own_attn, name="mix_17")
    other_attn = moves.core(other_attn)
    attn_grads = out(attn_out_kernel, half, own_attn, other_attn, [shape(width, model)] * 4, "attn_out")
    grad_w_query, grad_w_key, grad_w_value = (v.T for v in attn_grads[:3])
    my_in = lax.dynamic_index_in_dim(small, 8 + rank, keepdims=False)
    my_attn = lax.dynamic_index_in_dim(small, 8 + group + rank, keepdims=False)
    return (
        layer_out,
        grad_input,
        small[6],
        grad_w_query,
        my_attn[:width],
        grad_w_key,
        grad_w_value,
        my_attn[width : 2 * width],
        attn_grads[3],
        small[5],
        small[3],
        small[4],
        grad_w_in,
        my_in,
        grad_w_back,
        small[2],
        small[0],
        small[1],
    )


def solution(mesh):
    rows = P(("dp", "tensor"), None)
    placed = (
        rows,
        P("dp"),
        P("dp"),
        P("dp"),
        P(),
        P(None, "tensor"),
        P("tensor"),
        P(None, "tensor"),
        P(None, "tensor"),
        P("tensor"),
        P("tensor", None),
        P(),
        P(),
        P(),
        P(None, "tensor"),
        P("tensor"),
        P("tensor", None),
        P(),
        P(),
        P(),
        rows,
    )
    return jax.shard_map(
        on_device,
        mesh=mesh,
        in_specs=placed,
        out_specs=(
            rows,
            rows,
            P(),
            P(None, "tensor"),
            P("tensor"),
            P(None, "tensor"),
            P(None, "tensor"),
            P("tensor"),
            P("tensor", None),
            P(),
            P(),
            P(),
            P(None, "tensor"),
            P("tensor"),
            P("tensor", None),
            P(),
            P(),
            P(),
        ),
        check_vma=False,
    )
```

time: 888 us -> 232 us (0.26)
  waiting for transfers between devices: 629 us -> 118 us
  matrix products: 84.6 us -> 0 us
  Pallas kernels: 0 us -> 61.5 us
  local copies, waits for them, and re-layouts: 60.6 us -> 2.21 us
  blocking collectives: 56.1 us -> 0 us
  starting transfers between devices: 1.53 us -> 44.9 us
  other arithmetic: 33 us -> 1.42 us
  between operations: 14.6 us -> 1.58 us
    reduce_scatter x4 -> x0, waiting for transfers between devices: 300 us -> none  [the longest x1 109 us: on_device(): lax.psum_scatter(jnp.dot(context, w_out, preferred_element_type=jnp.float...]
    all_gather x4 -> x0, waiting for transfers between devices: 253 us -> none  [the longest x1 64 us: on_device(): lax.all_gather(grad_second.astype(jnp.bfloat16), 'tensor', axis=0, tiled=...]
    ppermute x0 -> x56, waiting for transfers between devices: none -> 118 us  [build(): return lax.ppermute(value, AXES, pairs)]
    dot_general x40 -> x0, matrix products: 84.6 us -> none  [the longest x1 18.4 us: on_device(): jnp.dot(normed_full, w_in, preferred_element_type=jnp.float32)]
    psum x1 -> x0, waiting for transfers between devices: 75.7 us -> none  [on_device(): lax.psum((grad_w_query, grad_b_query, grad_w_key, grad_w_value, grad_b_va...]
    pallas_call x0 -> x35, Pallas kernels: none -> 61.5 us  [call(): pl.pallas_call(kernel, in_specs=[spec for _, spec in ins], out_specs=[VME...]
    psum x2 -> x0, blocking collectives: 56.1 us -> none  [the longest x1 41.7 us: on_device(): lax.psum((grad_embed, grad_b_out, grad_g_attn, grad_s_attn, grad_b_back,...]
    ppermute x0 -> x56, starting transfers between devices: none -> 44.9 us  [build(): return lax.ppermute(value, AXES, pairs)]
  transfers between devices with their start and end apart: 9 -> 56, of which waited for: 9 -> 27; matrix products, arithmetic and copies ran while one was open for 3% -> 1% of each run, Pallas kernels for 0% -> 20%
where the time goes in v2:
time: 232 us; the launch traced here: 229 us
  waiting for transfers between devices  118 us (51%)
  Pallas kernels  61.5 us (27%)
  starting transfers between devices  44.9 us (19%)
    ppermute x56, waiting for transfers between devices, build(): return lax.ppermute(value, AXES, pairs)  118 us
    pallas_call x35, Pallas kernels, call(): pl.pallas_call(kernel, in_specs=[spec for _, spec in ins], out_specs=[VME...  61.5 us
    ppermute x56, starting transfers between devices, build(): return lax.ppermute(value, AXES, pairs)  44.9 us
  transfers between devices with their start and end apart: 56, of which 27 were waited for; matrix products, arithmetic and copies ran while one was open for 1% of the time, Pallas kernels for 20%

profile of v2, /device:TPU:0, one launch (start us, length us, event | category | flops | bytes accessed | tf_op | source)
XLA Modules:
  0.0 229.5 jit_solution(17434951056843338174)
XLA Ops:
  4.9 5.1 %collective-permute-start = (bf16[112,768]{1,0:T(8,128)(2,1)}, bf16[112,768]{1,0:T(8,128)(2,1)S(1)}, u32[]{:S(2)}, u32[]{:S(2)}) collective-permute-start(bf16[112,768]{1,0:T(8,128)(2,1)} %get-tuple-element.236), channel_id=1, source_target_pairs={{1,0},{2,1},{3,2},{0,3},{5,4},{6,5},{7,6},{4,7},{9,8},{10,9},{11,1... | collective-permute-start | bytes 516104 | tf_op jit(solution)/shard_map/ppermute | solution.py:30
  15.1 3.3 %collective-permute-done.1.refs_1_.first = bf16[112,768]{1,0:T(8,128)(2,1)S(1)} collective-permute-done((bf16[112,768]{1,0:T(8,128)(2,1)}, bf16[112,768]{1,0:T(8,128)(2,1)S(1)}, u32[]{:S(2)}, u32[]{:S(2)}) %collective-permute-start.1) | collective-permute-done | bytes 172064 | tf_op jit(solution)/shard_map/ppermute | solution.py:30
  22.2 8.8 %collective-permute-done.2.refs_0_.first = bf16[112,768]{1,0:T(8,128)(2,1)S(1)} collective-permute-done((bf16[112,768]{1,0:T(8,128)(2,1)S(1)}, bf16[112,768]{1,0:T(8,128)(2,1)S(1)}, u32[]{:S(2)}, u32[]{:S(2)}) %collective-permute-start.2) | collective-permute-done | bytes 172064 | tf_op jit(solution)/shard_map/ppermute | solution.py:30
  33.3 5.9 %collective-permute-done.6.refs_0_.refs_3_.refs_1_ = bf16[96,768]{1,0:T(8,128)(2,1)S(1)} collective-permute-done((bf16[96,768]{1,0:T(8,128)(2,1)S(1)}, bf16[96,768]{1,0:T(8,128)(2,1)S(1)}, u32[]{:S(2)}, u32[]{:S(2)}) %collective-permute-start.6) | collective-permute-done | bytes 147488 | tf_op jit(solution)/shard_map/ppermute | solution.py:30
  42.6 10.1 %collective-permute-done.8.refs_1_.refs_0_ = bf16[192,768]{1,0:T(8,128)(2,1)S(1)} collective-permute-done((bf16[192,768]{1,0:T(8,128)(2,1)S(1)}, bf16[192,768]{1,0:T(8,128)(2,1)S(1)}, u32[]{:S(2)}, u32[]{:S(2)}) %collective-permute-start.8) | collective-permute-done | bytes 294944 | tf_op jit(solution)/shard_map/ppermute | solution.py:30
  54.7 3.9 %attn_1.1 = (bf16[576,512]{1,0:T(8,128)(2,1)S(1)}, bf16[12,128,128]{2,1,0:T(8,128)(2,1)S(1)}, bf16[192,512]{1,0:T(8,128)(2,1)S(1)}, f32[8,768]{1,0:T(8,128)S(1)}...) custom-call(s32[16]{0:T(128)S(1)} %copy-done.9, bf16[512,768]{1,0:T(8,128)(2,1)S(1)} %get-tuple-element.235.mixed, ...), custom_call_target="tpu_custom_call" | custom-call | flops 6039797 | bytes 90194 | tf_op jit(solution)/shard_map/attn_1/pallas_call | solution.py:493
  58.6 3.9 %attn_3.1 = (bf16[576,512]{1,0:T(8,128)(2,1)S(1)}, bf16[12,128,128]{2,1,0:T(8,128)(2,1)S(1)}, bf16[192,512]{1,0:T(8,128)(2,1)S(1)}, f32[8,768]{1,0:T(8,128)S(1)}...) custom-call(s32[16]{0:T(128)S(1)} %copy-done.9, bf16[512,768]{1,0:T(8,128)(2,1)S(1)} %get-tuple-element.235.mixed, ...), custom_call_target="tpu_custom_call" | custom-call | flops 6039797 | bytes 90194 | tf_op jit(solution)/shard_map/attn_3/pallas_call | solution.py:493
  62.6 6.2 %collective-permute-done.12.refs_1_.refs_0_.refs_3_ = bf16[192,768]{1,0:T(8,128)(2,1)S(1)} collective-permute-done((bf16[192,768]{1,0:T(8,128)(2,1)S(1)}, bf16[192,768]{1,0:T(8,128)(2,1)S(1)}, u32[]{:S(2)}, u32[]{:S(2)}) %collective-permute-start.12) | collective-permute-done | bytes 294944 | tf_op jit(solution)/shard_map/ppermute | solution.py:30
  71.9 4.4 %attn_2.1 = (bf16[576,512]{1,0:T(8,128)(2,1)S(1)}, bf16[12,128,128]{2,1,0:T(8,128)(2,1)S(1)}, bf16[192,512]{1,0:T(8,128)(2,1)S(1)}, f32[8,768]{1,0:T(8,128)S(1)}...) custom-call(s32[16]{0:T(128)S(1)} %copy-done.9, ...), custom_call_target="tpu_custom_call" | custom-call | flops 6039797 | bytes 93307 | tf_op jit(solution)/shard_map/attn_2/pallas_call | solution.py:493
  85.7 3.3 %collective-permute-done.19.refs_3_.refs_6_ = bf16[192,768]{1,0:T(8,128)(2,1)S(1)} collective-permute-done((bf16[192,768]{1,0:T(8,128)(2,1)S(1)}, bf16[192,768]{1,0:T(8,128)(2,1)S(1)}, u32[]{:S(2)}, u32[]{:S(2)}) %collective-permute-start.19) | collective-permute-done | bytes 294944 | tf_op jit(solution)/shard_map/ppermute | solution.py:30
  92.0 4.7 %ffn_2.1 = (bf16[512,768]{1,0:T(8,128)(2,1)S(1)}, bf16[512,768]{1,0:T(8,128)(2,1)S(1)}, bf16[1536,768]{1,0:T(8,128)(2,1)S(1)}, bf16[512,768]{1,0:T(8,128)(2,1)},...) custom-call(bf16[512,768]{1,0:T(8,128)(2,1)S(1)} %get-tuple-element.264.normed, ...), custom_call_target="tpu_custom_call" | custom-call | flops 12079595 | bytes 145244 | tf_op jit(solution)/shard_map/ffn_2/pallas_call | solution.py:493
  104.0 5.7 %ffn_back_20.1 = (bf16[768,768]{1,0:T(8,128)(2,1)S(1)}, bf16[768,768]{1,0:T(8,128)(2,1)S(1)}, bf16[1536,768]{1,0:T(8,128)(2,1)S(1)}, f32[512,768]{1,0:T(8,128)S(1)}, f32[8,768]{1,0:T(8,128)S(1)}) custom-call(bf16[512,768]{1,0:T(8,128)(2,1)S(1)} %get-tuple-element.285.grad_low, bf16[512,768]{1,0:T(8,128)(2,1)S(1)} %get-tuple-element.264.normed, ...), custom_call_target="tpu_custom_call" | custom-call | flops 48318384 | bytes 173260 | tf_op jit(solution)/shard_map/ffn_back_20/pallas_call | solution.py:493
  109.7 11.6 %collective-permute-done.24.refs_11_.refs_5_ = bf16[384,768]{1,0:T(8,128)(2,1)S(1)} collective-permute-done((bf16[384,768]{1,0:T(8,128)(2,1)S(1)}, bf16[384,768]{1,0:T(8,128)(2,1)S(1)}, u32[]{:S(2)}, u32[]{:S(2)}) %collective-permute-start.24) | collective-permute-done | bytes 589856 | tf_op jit(solution)/shard_map/ppermute | solution.py:30
  122.5 3.8 %attn_back_2.1 = (bf16[384,768]{1,0:T(8,128)(2,1)S(1)}, bf16[384,768]{1,0:T(8,128)(2,1)S(1)}, f32[512,768]{1,0:T(8,128)S(1)}, f32[8,768]{1,0:T(8,128)S(1)}, bf16...) custom-call(bf16[512,768]{1,0:T(8,128)(2,1)S(1)} %get-tuple-element.235.mixed, f32[512,768]{1,0:T(8,128)S(1)} %get-tuple-element.321.part, ...), custom_call_target="tpu_custom_call" | custom-call | flops 12079595 | bytes 101662 | tf_op jit(solution)/shard_map/attn_back_2/pallas_call | solution.py:493
  126.3 5.2 %collective-permute-done.25.refs_2_.refs_3_ = bf16[384,768]{1,0:T(8,128)(2,1)S(1)} collective-permute-done((bf16[384,768]{1,0:T(8,128)(2,1)S(1)}, bf16[384,768]{1,0:T(8,128)(2,1)S(1)}, u32[]{:S(2)}, u32[]{:S(2)}) %collective-permute-start.25) | collective-permute-done | bytes 589856 | tf_op jit(solution)/shard_map/ppermute | solution.py:30
  134.4 5.9 %attn_back_13.1 = (bf16[384,768]{1,0:T(8,128)(2,1)S(1)}, bf16[384,768]{1,0:T(8,128)(2,1)S(1)}, bf16[768,768]{1,0:T(8,128)(2,1)S(1)}, f32[512,768]{1,0:T(8,128)S(1)}, f32[8,768]{1,0:T(8,128)S(1)}) custom-call(bf16[512,768]{1,0:T(8,128)(2,1)S(1)} %get-tuple-element.235.mixed, f32[512,768]{1,0:T(8,128)S(1)} %get-tuple-element.342.part, ...), custom_call_target="tpu_custom_call" | custom-call | flops 24159192 | bytes 118210 | tf_op jit(solution)/shard_map/attn_back_13/pallas_call | solution.py:493
  144.8 5.5 %collective-permute-done.30.refs_8_.refs_2_ = bf16[384,768]{1,0:T(8,128)(2,1)S(1)} collective-permute-done((bf16[384,768]{1,0:T(8,128)(2,1)S(1)}, bf16[384,768]{1,0:T(8,128)(2,1)S(1)}, u32[]{:S(2)}, u32[]{:S(2)}) %collective-permute-start.30) | collective-permute-done | bytes 589856 | tf_op jit(solution)/shard_map/ppermute | solution.py:30
  153.4 4.3 %attn_back_0.1 = (bf16[384,768]{1,0:T(8,128)(2,1)S(1)}, bf16[384,768]{1,0:T(8,128)(2,1)S(1)}, bf16[512,768]{1,0:T(8,128)(2,1)}, f32[8,768]{1,0:T(8,128)S(1)}) custom-call(bf16[512,768]{1,0:T(8,128)(2,1)S(1)} %get-tuple-element.235.mixed, f32[512,768]{1,0:T(8,128)S(1)} %get-tuple-element.372.part, bf16[512,768]{1,0:T(8,128)(2,1)S(1)} %get-tuple-element.343.refs_0_, ...), custom_call_target="tpu_custom_call" | custom-call | flops 12079595 | bytes 74958 | tf_op jit(solution)/shard_map/attn_back_0/pallas_call | solution.py:493
  157.6 4.5 %collective-permute-done.31.refs_2_ = bf16[192,768]{1,0:T(8,128)(2,1)S(1)} collective-permute-done((bf16[192,768]{1,0:T(8,128)(2,1)S(1)}, bf16[192,768]{1,0:T(8,128)(2,1)S(1)}, u32[]{:S(2)}, u32[]{:S(2)}) %collective-permute-start.31) | collective-permute-done | bytes 294944 | tf_op jit(solution)/shard_map/ppermute | solution.py:30
  162.1 5.1 %collective-permute-done.32.refs_6_.refs_4_ = bf16[576,768]{1,0:T(8,128)(2,1)S(1)} collective-permute-done((bf16[576,768]{1,0:T(8,128)(2,1)S(1)}, bf16[576,768]{1,0:T(8,128)(2,1)S(1)}, u32[]{:S(2)}, u32[]{:S(2)}) %collective-permute-start.32) | collective-permute-done | bytes 884768 | tf_op jit(solution)/shard_map/ppermute | solution.py:30
  171.4 12.6 %collective-permute-done.38.refs_6_ = bf16[192,768]{1,0:T(8,128)(2,1)S(1)} collective-permute-done((bf16[192,768]{1,0:T(8,128)(2,1)S(1)}, bf16[192,768]{1,0:T(8,128)(2,1)S(1)}, u32[]{:S(2)}, u32[]{:S(2)}) %collective-permute-start.38) | collective-permute-done | bytes 294944 | tf_op jit(solution)/shard_map/ppermute | solution.py:30
  187.9 14.0 %collective-permute-done.43 = f32[16,768]{1,0:T(8,128)S(1)} collective-permute-done((f32[16,768]{1,0:T(8,128)S(1)}, f32[16,768]{1,0:T(8,128)S(1)}, u32[]{:S(2)}, u32[]{:S(2)}) %collective-permute-start.43) | collective-permute-done | bytes 49184 | tf_op jit(solution)/shard_map/ppermute | solution.py:30
  203.1 3.8 %collective-permute-start.45 = (bf16[96,768]{1,0:T(8,128)(2,1)S(1)}, bf16[96,768]{1,0:T(8,128)(2,1)S(1)}, u32[]{:S(2)}, u32[]{:S(2)}) collective-permute-start(bf16[96,768]{1,0:T(8,128)(2,1)S(1)} %get-tuple-element.420), channel_id=1, source_target_pairs={{1,0},{2,1},{3,2},{0,3},{5,4},{6,5},{7,6},{4,7},{9,8},{10,9},{11,1... | collective-permute-start | bytes 442376 | tf_op jit(solution)/shard_map/ppermute | solution.py:30
  214.8 4.1 %collective-permute-done.52 = f32[16,768]{1,0:T(8,128)S(1)} collective-permute-done((f32[16,768]{1,0:T(8,128)S(1)}, f32[16,768]{1,0:T(8,128)S(1)}, u32[]{:S(2)}, u32[]{:S(2)}) %collective-permute-start.52) | collective-permute-done | bytes 49184 | tf_op jit(solution)/shard_map/ppermute | solution.py:30
  (187 shorter events, 82.3 us)
Async XLA Ops:
  18.4 12.6 %collective-permute-start.3 = (bf16[192,768]{1,0:T(8,128)(2,1)S(1)}, bf16[192,768]{1,0:T(8,128)(2,1)S(1)}, u32[]{:S(2)}, u32[]{:S(2)}) collective-permute-start(bf16[192,768]{1,0:T(8,128)(2,1)S(1)} %mix_1.1.refs_2_.refs_0_), channel_id=1, source_target_pairs={{8,0},{9,1},{10,2},{11,3},{20,4},{21,5},{22,6},{23,7},{0,8},{1,9},... | collective-permute-start | bytes 884744 | tf_op jit(solution)/shard_map/ppermute | solution.py:30
  40.3 12.4 %collective-permute-start.11 = (bf16[768,768]{1,0:T(8,128)(2,1)S(1)}, bf16[768,768]{1,0:T(8,128)(2,1)S(1)}, u32[]{:S(2)}, u32[]{:S(2)}) collective-permute-start(bf16[768,768]{1,0:T(8,128)(2,1)S(1)} %get-tuple-element.251), channel_id=1, source_target_pairs={{4,0},{5,1},{6,2},{7,3},{0,4},{1,5},{2,6},{3,7},{12,8},{13,9},{14,... | collective-permute-start | bytes 3538952 | tf_op jit(solution)/shard_map/ppermute | solution.py:30
  40.3 12.3 %collective-permute-start.10 = (bf16[288,768]{1,0:T(8,128)(2,1)S(1)}, bf16[288,768]{1,0:T(8,128)(2,1)S(1)}, u32[]{:S(2)}, u32[]{:S(2)}) collective-permute-start(bf16[288,768]{1,0:T(8,128)(2,1)S(1)} %get-tuple-element.250), channel_id=1, source_target_pairs={{16,0},{17,1},{18,2},{19,3},{12,4},{13,5},{14,6},{15,7},{24,8},{25... | collective-permute-start | bytes 1327112 | tf_op jit(solution)/shard_map/ppermute | solution.py:30
  52.7 16.0 %collective-permute-start.14 = (bf16[384,768]{1,0:T(8,128)(2,1)S(1)}, bf16[384,768]{1,0:T(8,128)(2,1)S(1)}, u32[]{:S(2)}, u32[]{:S(2)}) collective-permute-start(bf16[384,768]{1,0:T(8,128)(2,1)S(1)} %get-tuple-element.256), channel_id=1, source_target_pairs={{16,0},{17,1},{18,2},{19,3},{12,4},{13,5},{14,6},{15,7},{24,8},{25... | collective-permute-start | bytes 1769480 | tf_op jit(solution)/shard_map/ppermute | solution.py:30
  53.5 15.2 %collective-permute-start.15 = (bf16[384,768]{1,0:T(8,128)(2,1)S(1)}, bf16[384,768]{1,0:T(8,128)(2,1)S(1)}, u32[]{:S(2)}, u32[]{:S(2)}) collective-permute-start(bf16[384,768]{1,0:T(8,128)(2,1)S(1)} %get-tuple-element.257), channel_id=1, source_target_pairs={{4,0},{5,1},{6,2},{7,3},{0,4},{1,5},{2,6},{3,7},{12,8},{13,9},{14,... | collective-permute-start | bytes 1769480 | tf_op jit(solution)/shard_map/ppermute | solution.py:30
  53.5 15.2 %collective-permute-start.12 = (bf16[192,768]{1,0:T(8,128)(2,1)S(1)}, bf16[192,768]{1,0:T(8,128)(2,1)S(1)}, u32[]{:S(2)}, u32[]{:S(2)}) collective-permute-start(bf16[192,768]{1,0:T(8,128)(2,1)S(1)} %copy-done.19), channel_id=1, source_target_pairs={{2,0},{3,1},{0,2},{1,3},{6,4},{7,5},{4,6},{5,7},{10,8},{11,9},{8,1... | collective-permute-start | bytes 884744 | tf_op jit(solution)/shard_map/ppermute | solution.py:30
  53.5 15.2 %collective-permute-start.13 = (bf16[192,768]{1,0:T(8,128)(2,1)S(1)}, bf16[192,768]{1,0:T(8,128)(2,1)S(1)}, u32[]{:S(2)}, u32[]{:S(2)}) collective-permute-start(bf16[192,768]{1,0:T(8,128)(2,1)S(1)} %collective-permute-done.8.refs_1_.refs_0_), channel_id=1, source_target_pairs={{8,0},{9,1},{10,2},{11,3},{20,4},{21,5},{22,6},{23,7},{0,8},{1,9},... | collective-permute-start | bytes 884744 | tf_op jit(solution)/shard_map/ppermute | solution.py:30
  68.9 13.2 %collective-permute-start.18 = (bf16[768,768]{1,0:T(8,128)(2,1)S(1)}, bf16[768,768]{1,0:T(8,128)(2,1)S(1)}, u32[]{:S(2)}, u32[]{:S(2)}) collective-permute-start(bf16[768,768]{1,0:T(8,128)(2,1)S(1)} %get-tuple-element.269), channel_id=1, source_target_pairs={{4,0},{5,1},{6,2},{7,3},{0,4},{1,5},{2,6},{3,7},{12,8},{13,9},{14,... | collective-permute-start | bytes 3538952 | tf_op jit(solution)/shard_map/ppermute | solution.py:30
  69.0 13.1 %collective-permute-start.17 = (bf16[384,768]{1,0:T(8,128)(2,1)S(1)}, bf16[384,768]{1,0:T(8,128)(2,1)S(1)}, u32[]{:S(2)}, u32[]{:S(2)}) collective-permute-start(bf16[384,768]{1,0:T(8,128)(2,1)S(1)} %get-tuple-element.268), channel_id=1, source_target_pairs={{16,0},{17,1},{18,2},{19,3},{12,4},{13,5},{14,6},{15,7},{24,8},{25... | collective-permute-start | bytes 1769480 | tf_op jit(solution)/shard_map/ppermute | solution.py:30
  103.3 18.0 %collective-permute-start.23 = (bf16[768,768]{1,0:T(8,128)(2,1)S(1)}, bf16[768,768]{1,0:T(8,128)(2,1)S(1)}, u32[]{:S(2)}, u32[]{:S(2)}) collective-permute-start(bf16[768,768]{1,0:T(8,128)(2,1)S(1)} %get-tuple-element.305), channel_id=1, source_target_pairs={{4,0},{5,1},{6,2},{7,3},{0,4},{1,5},{2,6},{3,7},{12,8},{13,9},{14,... | collective-permute-start | bytes 3538952 | tf_op jit(solution)/shard_map/ppermute | solution.py:30
  103.6 17.7 %collective-permute-start.24 = (bf16[384,768]{1,0:T(8,128)(2,1)S(1)}, bf16[384,768]{1,0:T(8,128)(2,1)S(1)}, u32[]{:S(2)}, u32[]{:S(2)}) collective-permute-start(bf16[384,768]{1,0:T(8,128)(2,1)S(1)} %get-tuple-element.314), channel_id=1, source_target_pairs={{3,0},{0,1},{1,2},{2,3},{7,4},{4,5},{5,6},{6,7},{11,8},{8,9},{9,10... | collective-permute-start | bytes 1769480 | tf_op jit(solution)/shard_map/ppermute | solution.py:30
  131.7 13.1 %collective-permute-start.28 = (bf16[384,768]{1,0:T(8,128)(2,1)S(1)}, bf16[384,768]{1,0:T(8,128)(2,1)S(1)}, u32[]{:S(2)}, u32[]{:S(2)}) collective-permute-start(bf16[384,768]{1,0:T(8,128)(2,1)S(1)} %get-tuple-element.340), channel_id=1, source_target_pairs={{16,0},{17,1},{18,2},{19,3},{12,4},{13,5},{14,6},{15,7},{24,8},{25... | collective-permute-start | bytes 1769480 | tf_op jit(solution)/shard_map/ppermute | solution.py:30
  132.7 12.2 %collective-permute-start.29 = (bf16[384,768]{1,0:T(8,128)(2,1)S(1)}, bf16[384,768]{1,0:T(8,128)(2,1)S(1)}, u32[]{:S(2)}, u32[]{:S(2)}) collective-permute-start(bf16[384,768]{1,0:T(8,128)(2,1)S(1)} %get-tuple-element.341), channel_id=1, source_target_pairs={{4,0},{5,1},{6,2},{7,3},{0,4},{1,5},{2,6},{3,7},{12,8},{13,9},{14,... | collective-permute-start | bytes 1769480 | tf_op jit(solution)/shard_map/ppermute | solution.py:30
  132.7 17.7 %collective-permute-start.30 = (bf16[384,768]{1,0:T(8,128)(2,1)S(1)}, bf16[384,768]{1,0:T(8,128)(2,1)S(1)}, u32[]{:S(2)}, u32[]{:S(2)}) collective-permute-start(bf16[384,768]{1,0:T(8,128)(2,1)S(1)} %get-tuple-element.355), channel_id=1, source_target_pairs={{3,0},{0,1},{1,2},{2,3},{7,4},{4,5},{5,6},{6,7},{11,8},{8,9},{9,10... | collective-permute-start | bytes 1769480 | tf_op jit(solution)/shard_map/ppermute | solution.py:30
  150.9 16.4 %collective-permute-start.33 = (bf16[768,768]{1,0:T(8,128)(2,1)S(1)}, bf16[768,768]{1,0:T(8,128)(2,1)S(1)}, u32[]{:S(2)}, u32[]{:S(2)}) collective-permute-start(bf16[768,768]{1,0:T(8,128)(2,1)S(1)} %get-tuple-element.370), channel_id=1, source_target_pairs={{4,0},{5,1},{6,2},{7,3},{0,4},{1,5},{2,6},{3,7},{12,8},{13,9},{14,... | collective-permute-start | bytes 3538952 | tf_op jit(solution)/shard_map/ppermute | solution.py:30
  151.0 16.3 %collective-permute-start.32 = (bf16[576,768]{1,0:T(8,128)(2,1)S(1)}, bf16[576,768]{1,0:T(8,128)(2,1)S(1)}, u32[]{:S(2)}, u32[]{:S(2)}) collective-permute-start(bf16[576,768]{1,0:T(8,128)(2,1)S(1)} %get-tuple-element.369), channel_id=1, source_target_pairs={{16,0},{17,1},{18,2},{19,3},{12,4},{13,5},{14,6},{15,7},{24,8},{25... | collective-permute-start | bytes 2654216 | tf_op jit(solution)/shard_map/ppermute | solution.py:30
  167.7 16.4 %collective-permute-start.36 = (bf16[384,768]{1,0:T(8,128)(2,1)S(1)}, bf16[384,768]{1,0:T(8,128)(2,1)S(1)}, u32[]{:S(2)}, u32[]{:S(2)}) collective-permute-start(bf16[384,768]{1,0:T(8,128)(2,1)S(1)} %get-tuple-element.391), channel_id=1, source_target_pairs={{16,0},{17,1},{18,2},{19,3},{12,4},{13,5},{14,6},{15,7},{24,8},{25... | collective-permute-start | bytes 1769480 | tf_op jit(solution)/shard_map/ppermute | solution.py:30
  168.9 15.2 %collective-permute-start.37 = (bf16[384,768]{1,0:T(8,128)(2,1)S(1)}, bf16[384,768]{1,0:T(8,128)(2,1)S(1)}, u32[]{:S(2)}, u32[]{:S(2)}) collective-permute-start(bf16[384,768]{1,0:T(8,128)(2,1)S(1)} %get-tuple-element.392), channel_id=1, source_target_pairs={{4,0},{5,1},{6,2},{7,3},{0,4},{1,5},{2,6},{3,7},{12,8},{13,9},{14,... | collective-permute-start | bytes 1769480 | tf_op jit(solution)/shard_map/ppermute | solution.py:30
  168.9 15.2 %collective-permute-start.35 = (bf16[288,768]{1,0:T(8,128)(2,1)S(1)}, bf16[288,768]{1,0:T(8,128)(2,1)S(1)}, u32[]{:S(2)}, u32[]{:S(2)}) collective-permute-start(bf16[288,768]{1,0:T(8,128)(2,1)S(1)} %get-tuple-element.390), channel_id=1, source_target_pairs={{8,0},{9,1},{10,2},{11,3},{20,4},{21,5},{22,6},{23,7},{0,8},{1,9},... | collective-permute-start | bytes 1327112 | tf_op jit(solution)/shard_map/ppermute | solution.py:30
  170.1 14.0 %collective-permute-start.38 = (bf16[192,768]{1,0:T(8,128)(2,1)S(1)}, bf16[192,768]{1,0:T(8,128)(2,1)S(1)}, u32[]{:S(2)}, u32[]{:S(2)}) collective-permute-start(bf16[192,768]{1,0:T(8,128)(2,1)S(1)} %get-tuple-element.393), channel_id=1, source_target_pairs={{2,0},{3,1},{0,2},{1,3},{6,4},{7,5},{4,6},{5,7},{10,8},{11,9},{8,1... | collective-permute-start | bytes 884744 | tf_op jit(solution)/shard_map/ppermute | solution.py:30
  184.7 17.3 %collective-permute-start.40 = (bf16[384,768]{1,0:T(8,128)(2,1)S(1)}, bf16[384,768]{1,0:T(8,128)(2,1)S(1)}, u32[]{:S(2)}, u32[]{:S(2)}) collective-permute-start(bf16[384,768]{1,0:T(8,128)(2,1)S(1)} %get-tuple-element.413), channel_id=1, source_target_pairs={{8,0},{9,1},{10,2},{11,3},{20,4},{21,5},{22,6},{23,7},{0,8},{1,9},... | collective-permute-start | bytes 1769480 | tf_op jit(solution)/shard_map/ppermute | solution.py:30
  186.0 16.0 %collective-permute-start.41 = (bf16[384,768]{1,0:T(8,128)(2,1)S(1)}, bf16[384,768]{1,0:T(8,128)(2,1)S(1)}, u32[]{:S(2)}, u32[]{:S(2)}) collective-permute-start(bf16[384,768]{1,0:T(8,128)(2,1)S(1)} %get-tuple-element.414), channel_id=1, source_target_pairs={{16,0},{17,1},{18,2},{19,3},{12,4},{13,5},{14,6},{15,7},{24,8},{25... | collective-permute-start | bytes 1769480 | tf_op jit(solution)/shard_map/ppermute | solution.py:30
  187.1 14.9 %collective-permute-start.42 = (bf16[96,768]{1,0:T(8,128)(2,1)S(1)}, bf16[96,768]{1,0:T(8,128)(2,1)S(1)}, u32[]{:S(2)}, u32[]{:S(2)}) collective-permute-start(bf16[96,768]{1,0:T(8,128)(2,1)S(1)} %get-tuple-element.415), channel_id=1, source_target_pairs={{2,0},{3,1},{0,2},{1,3},{6,4},{7,5},{4,6},{5,7},{10,8},{11,9},{8,1... | collective-permute-start | bytes 442376 | tf_op jit(solution)/shard_map/ppermute | solution.py:30
  187.1 14.9 %collective-permute-start.43 = (f32[16,768]{1,0:T(8,128)S(1)}, f32[16,768]{1,0:T(8,128)S(1)}, u32[]{:S(2)}, u32[]{:S(2)}) collective-permute-start(f32[16,768]{1,0:T(8,128)S(1)} %add.28), channel_id=1, source_target_pairs={{8,0},{9,1},{10,2},{11,3},{12,4},{13,5},{14,6},{15,7},{0,8},{1,9},... | collective-permute-start | bytes 147464 | tf_op jit(solution)/shard_map/ppermute | solution.py:30
  (53 other events, 407.4 us)

commit v3 on v2

--- a/solution.py
+++ b/solution.py
@@ -40,6 +40,12 @@
 
     def fetch(self, value, turn):
         return self.build(value, lambda d, t: (d, (t + turn) % self.group))
+
+    def pass_on(self, value):
+        return self.build(value, lambda d, t: (d, (t + (-1 if d & 1 else 1)) % self.group))
+
+    def hand_on(self, value):
+        return self.build(value, lambda d, t: (d, (t + (1 if d & 1 else -1)) % self.group))
 
     def give(self, value, turn):
         return self.build(value, lambda d, t: (d, (t - turn) % self.group))
@@ -200,24 +206,49 @@
 EMBED, B_OUT, G_ATTN, S_ATTN, B_BACK, G_FFN, S_FFN = range(7)
 
 
-def prep_kernel(half, piece, bias, wq, wk, wv, wo, w_in, w_back, attn_mine, ffn_mine, sems):
+def prep_kernel(
+    width, half, piece, b_in, b_query, b_value, *refs
+):
+    vectors, refs = refs[:7], refs[7:]
+    wq, wk, wv, wo, w_in, w_back, attn_mine, ffn_mine, bias, vecs, rows, sems = refs
     core, chip = where_am_i()
-    copies = [pltpu.make_async_copy(bias, attn_mine.at[pl.ds(half, BIAS_ROWS)], sems.at[0])]
-    copies[0].start()
+    copies = []
     for index, ref in enumerate((wq, wk, wv, wo)):
         start = pl.multiple_of(core * half, half)
         copy = pltpu.make_async_copy(
-            ref.at[pl.ds(start, half)], attn_mine.at[pl.ds(0, half)], sems.at[1]
+            ref.at[pl.ds(start, half)], attn_mine.at[pl.ds(0, half)], sems.at[0]
         )
         pl.when(chip == index)(copy.start)
     copies.append(copy)
     for index, ref in enumerate((w_in, w_back)):
         start = pl.multiple_of(chip * piece, piece)
-        copy = pltpu.make_async_copy(ref.at[pl.ds(start, piece)], ffn_mine, sems.at[2])
+        copy = pltpu.make_async_copy(ref.at[pl.ds(start, piece)], ffn_mine, sems.at[1])
         pl.when(core == index)(copy.start)
     copies.append(copy)
+    as_row = lambda ref: ref[...].astype(F32).reshape(1, -1)
+    rows[...] = jnp.zeros_like(rows)
+    rows[0:1, :] = as_row(b_in)
+    rows[1:2, :width] = as_row(b_query)
+    rows[1:2, 2 * width : 3 * width] = as_row(b_value)
+    bias[...] = rows[...].astype(BF)
+    for index, ref in enumerate(vectors):
+        vecs[index : index + 1, :] = as_row(ref)
+    vecs[7:8, :] = rows[2:3, :]
     for copy in copies:
         copy.wait()
+    attn_mine[half : half + BIAS_ROWS, :] = rows[...].astype(BF)
+
+
+def pick_kernel(own, other, out):
+    core, _ = where_am_i()
+
+    @pl.when(core == 0)
+    def _():
+        out[...] = own[...]
+
+    @pl.when(core == 1)
+    def _():
+        out[...] = other[...]
 
 
 def attn_own_kernel(
@@ -428,6 +459,19 @@
     bias_grad[1:2, :] = embed_sum
 
 
+def split_kernel(value, at_zero, at_one):
+    core, _ = where_am_i()
+    for index, out in enumerate((at_zero, at_one)):
+
+        @pl.when(core == index)
+        def _():
+            out[...] = value[...]
+
+        @pl.when(core != index)
+        def _():
+            out[...] = jnp.zeros_like(out)
+
+
 def mix_kernel(count, plan, *refs):
     for out, blocks in zip(refs[count:], plan):
         start = 0
@@ -506,7 +550,27 @@
     return jax.ShapeDtypeStruct((rows, columns), kind)
 
 
-def mix(*outs, name=None):
+def pick(own, other):
+    return call(
+        pick_kernel,
+        [(own, VMEM), (other, VMEM)],
+        [shape(*own.shape, own.dtype)],
+        vmem=4,
+        name="pick",
+    )[0]
+
+
+def split(value):
+    return call(
+        split_kernel,
+        [(value, VMEM)],
+        [shape(*value.shape, value.dtype)] * 2,
+        vmem=4,
+        name="split",
+    )
+
+
+def mix(*outs, first=(), name=None):
     refs, plan, shapes = Refs(), [], []
     for blocks in outs:
         mine = []
@@ -514,8 +578,10 @@
             sources = block if isinstance(block, list) else [block]
             mine.append((sources[0].rows, tuple(refs.add(source) for source in sources)))
         plan.append(tuple(mine))
-        first = blocks[0][0] if isinstance(blocks[0], list) else blocks[0]
-        shapes.append(shape(sum(rows for rows, _ in mine), first.array.shape[1], BF))
+        top = blocks[0][0] if isinstance(blocks[0], list) else blocks[0]
+        shapes.append(shape(sum(rows for rows, _ in mine), top.array.shape[1], BF))
+    if first:
+        refs.arrays[0] = after(refs.arrays[0], *first)
     return call(
         functools.partial(mix_kernel, len(refs.arrays), tuple(plan)),
         [(array, VMEM) for array in refs.arrays],
@@ -563,22 +629,21 @@
     turns = (1, 3, 2)
     count = len(turns)
 
-    vecs = jnp.stack(
-        (mask_embed, b_out, g_attn, s_attn, b_back, g_ffn, s_ffn, jnp.zeros_like(b_out))
-    ).astype(F32)
-    none = jnp.zeros((width,), BF)
-    bias_pack = jnp.pad(
-        jnp.stack((b_in, jnp.concatenate((b_query, none, b_value, none)))),
-        ((0, BIAS_ROWS - 2), (0, 0)),
-    )
     own_mats = (w_query.T, w_key.T, w_value.T, w_out)
     dma = lambda n: pltpu.SemaphoreType.DMA((8 * n,))
 
-    attn_mine, ffn_mine = call(
-        functools.partial(prep_kernel, half, piece),
-        [(v, ANY) for v in (bias_pack, *own_mats, w_in, w_back)],
-        [shape(half + BIAS_ROWS, model, BF), shape(piece, model, BF)],
-        [pltpu.SemaphoreType.DMA((3,))],
+    attn_mine, ffn_mine, bias_pack, vecs = call(
+        functools.partial(prep_kernel, width, half, piece),
+        [(v, VMEM) for v in (b_in, b_query, b_value)]
+        + [(v, VMEM) for v in (mask_embed, b_out, g_attn, s_attn, b_back, g_ffn, s_ffn)]
+        + [(v, ANY) for v in (*own_mats, w_in, w_back)],
+        [
+            shape(half + BIAS_ROWS, model, BF),
+            shape(piece, model, BF),
+            shape(BIAS_ROWS, model, BF),
+            shape(8, model),
+        ],
+        [pltpu.VMEM((BIAS_ROWS, model), F32), pltpu.SemaphoreType.DMA((2,))],
         vmem=60,
         name="prep",
     )
@@ -601,7 +666,7 @@
         name="attn_own",
     )
     first1, first3, mixed, attn_mine, ffn_mine = sync(first1, first3, mixed, attn_mine, ffn_mine)
-    first2 = moves.fetch(attn_mine, 2)
+    first2 = moves.pass_on(pick(first1, first3))
     (mine13,) = mix([Block(first1, 0, half), Block(first3, 0, half)], name="mix_1")
     near13, over13 = moves.near(mine13), moves.far(mine13)
 
@@ -617,7 +682,7 @@
     near_f1, far2_f1, other13 = moves.near(ffn1), moves.far(far), moves.core(other13)
 
     ffn3, near_f1, far2_f1, other13, ffn_mine = sync(ffn3, near_f1, far2_f1, other13, ffn_mine)
-    ffn2 = moves.fetch(ffn_mine, 2)
+    ffn2 = moves.pass_on(pick(ffn1, ffn3))
     own2 = (Block(mine2), Block(near2), Block(far13_2, 2 * half, half), Block(far2_f1, 0, half))
     far, other2 = mix([Block(near_f1), Block(ffn3)], own2, name="mix_4")
     near_f3, far_f1_f3, other2 = moves.near(ffn3), moves.far(far), moves.core(other2)
@@ -756,83 +821,71 @@
             start = index * self.rows
             return [Block(array, row + start, self.rows) for array, row in self.pieces]
 
-    (kept1,), given1, part, bias1 = ffn_back(grad_second, ffn_turn(0), name="ffn_back_1")
-    come1 = moves.core(given1)
-    (kept3,), given3, part, bias3 = ffn_back(part, ffn_turn(1), name="ffn_back_3")
-    come1, kept3, given3, part = sync(come1, kept3, given3, part)
-
-    cut_rows = (2 * piece, 2 * piece)
-    early = mix(
-        *([[Block(kept1, i * 2 * piece, n), Block(come1, i * 2 * piece, n)]] for i, n in enumerate(cut_rows)),
-        name="mix_8",
-    )
-    part, given3, *early = sync(part, given3, *early)
-    early[0] = moves.give(early[0], 1)
-    come3 = moves.core(given3)
-    (kept2, kept0), given20, part, bias20 = ffn_back(
-        part, ffn_turn(2), (act_own, slope_own, w_in, w_back), name="ffn_back_20"
-    )
-    come3, given20, part, *early = sync(come3, given20, part, *early)
-
-    f3 = Slots(kept3, come3)
-    (far,) = mix([f3.slot(2), f3.slot(1)], name="mix_9")
-    far, given20, part = sync(far, given20, part)
-    far_f3 = moves.far(far)
-    come20 = moves.core(given20)
-    a_kept2, a_given2, part, a_bias2, attn_low, small_attn = attn_back(
-        part, None, attn_turn(2), name="attn_back_2"
-    )
-    far_f3, come20, a_given2, part, *early = sync(far_f3, come20, a_given2, part, *early)
-
-    f2 = Slots(kept2, come20)
-    near, far = mix(
-        [[*f3.slot(0), Block(far_f3, 0, piece)]],
-        [f2.slot(2), f2.slot(1)],
+        def passed(self, index, *arrived):
+            return [self.slot(index) + [Block(array, row, self.rows) for array, row in arrived]]
+
+    (kept2,), given2, part, bias2 = ffn_back(grad_second, ffn_turn(2), name="ffn_back_2")
+    come2 = moves.core(given2)
+    (kept1,), given1, part, bias1 = ffn_back(part, ffn_turn(0), name="ffn_back_1")
+    come2, given1, part = sync(come2, given1, part)
+
+    f2 = Slots(kept2, come2)
+    (far,) = mix([f2.slot(2), f2.slot(1)], name="mix_8")
+    far, part, given1 = sync(far, part, given1)
+    far_f2, come1 = moves.far(far), moves.core(given1)
+    (kept3, kept0), given30, part, bias30 = ffn_back(
+        part, ffn_turn(1), (act_own, slope_own, w_in, w_back), name="ffn_back_30"
+    )
+    far_f2, come1, given30, part = sync(far_f2, come1, given30, part)
+
+    f1 = Slots(kept1, come1)
+    near, far = mix(f2.passed(0, (far_f2, 0)), [f1.slot(2), f1.slot(1)], name="mix_9")
+    near, far, given30, part = sync(near, far, given30, part)
+    near_f2, far_f1, come30 = moves.near(near), moves.far(far), moves.core(given30)
+    a_kept2, a_kept3, a_given23, part, a_bias23, attn_low, small_attn = attn_back(
+        part, None, attn_turn(2), attn_turn(1), name="attn_back_23"
+    )
+    near_f2, far_f1, come30, a_given23, part = sync(near_f2, far_f1, come30, a_given23, part)
+
+    f3, f0 = Slots(kept3, come30), Slots(kept0, come30, 4 * piece)
+    done2, near, far = mix(
+        f2.passed(3, (near_f2, 0), (far_f2, piece)),
+        f1.passed(0, (far_f1, 0)),
+        [f3.slot(2), f3.slot(1)],
         name="mix_10",
     )
-    near, far, early[1], part, a_given2 = sync(near, far, early[1], part, a_given2)
-    early[1] = moves.give(early[1], 1)
-    near_f3, far_f2, a_come2 = moves.near(near), moves.far(far), moves.core(a_given2)
-    a_kept1, a_kept3, a_given13, part, a_bias13 = attn_back(
-        part, attn_low, attn_turn(0), attn_turn(1), name="attn_back_13"
-    )
-    near_f3, far_f2, a_come2, a_given13, part, *early = sync(
-        near_f3, far_f2, a_come2, a_given13, part, *early
-    )
-
-    class Early:
-        def slot(self, index):
-            return Block(early[index // 2], index % 2 * piece, piece)
-
-    f0 = Slots(kept0, come20, 4 * piece)
-    a2 = Slots(a_kept2, a_come2)
-    f0_slot = lambda index: f0.slot(index) + [Early().slot(index)]
-    done3, near, far = mix(
-        [[*f3.slot(3), Block(near_f3), Block(far_f3, piece, piece)]],
-        [[*f2.slot(0), Block(far_f2, 0, piece)]],
-        [f0_slot(2), a2.slot(2), f0_slot(1), a2.slot(1)],
+    done2, near, far, a_given23, part = sync(done2, near, far, a_given23, part)
+    done2, near_f1, far_f3 = moves.hand_on(done2), moves.near(near), moves.far(far)
+    a_come23 = moves.core(a_given23)
+    a_kept1, a_given1, part, a_bias1 = attn_back(part, attn_low, attn_turn(0), name="attn_back_1")
+    near_f1, far_f3, a_come23, done2, a_given1, part = sync(near_f1, far_f3, a_come23, done2, a_given1, part)
+
+    for_one, for_three = split(done2)
+    a2, a3 = Slots(a_kept2, a_come23), Slots(a_kept3, a_come23, 4 * half)
+    done1, near, far = mix(
+        f1.passed(3, (near_f1, 0), (far_f1, piece), (for_one, 0)),
+        f3.passed(0, (far_f3, 0)),
+        [a2.slot(2), a3.slot(2), a2.slot(1), a3.slot(1)],
         name="mix_11",
     )
-    done3, near, far, part, a_given13 = sync(done3, near, far, part, a_given13)
-    done3 = moves.give(done3, 3)
-    near_f2, far_f0_a2, a_come13 = moves.near(near), moves.far(far), moves.core(a_given13)
+    done1, near, far, a_given1, part = sync(done1, near, far, a_given1, part)
+    done1, near_f3, far_a23 = moves.give(done1, 1), moves.near(near), moves.far(far)
+    a_come1 = moves.core(a_given1)
     a_kept0, a_given0, grad_input, a_bias0 = attn_back(
         part, attn_low, (qkv_own, soft_own, ctx_own, *own_mats), own=True, name="attn_back_0"
     )
-    near_f2, far_f0_a2, a_come13, done3, a_given0, grad_input, a_bias0 = sync(
-        near_f2, far_f0_a2, a_come13, done3, a_given0, grad_input, a_bias0
-    )
-
-    wide = piece + half
-    a1, a3 = Slots(a_kept1, a_come13), Slots(a_kept3, a_come13, 4 * half)
-    done2, near, far = mix(
-        [[*f2.slot(3), Block(near_f2), Block(far_f2, piece, piece)]],
-        [[*f0_slot(0), Block(far_f0_a2, 0, piece)], [*a2.slot(0), Block(far_f0_a2, piece, half)]],
-        [a1.slot(2), a3.slot(2), a1.slot(1), a3.slot(1)],
+    near_f3, far_a23, a_come1, done1, a_given0, grad_input, a_bias0 = sync(
+        near_f3, far_a23, a_come1, done1, a_given0, grad_input, a_bias0
+    )
+
+    done3, near, far = mix(
+        f3.passed(3, (near_f3, 0), (far_f3, piece), (for_three, 0)),
+        a2.passed(0, (far_a23, 0)) + a3.passed(0, (far_a23, half)),
+        [f0.slot(2), f0.slot(1)],
         name="mix_12",
     )
-    biases = (bias20, bias1, bias3, a_bias0, a_bias13, a_bias2)
-    rows_of = ((0, 1), (1, 0), (0, 0), (2, 0), (3, 0), (4, 0), (5, 0), (4, 1), (3, 1))
+    biases = (bias30, bias1, bias2, a_bias0, a_bias1, a_bias23)
+    rows_of = ((0, 1), (1, 0), (2, 0), (0, 0), (3, 0), (4, 0), (5, 0), (5, 1), (3, 1))
     (small,) = call(
         functools.partial(small_kernel, group, rows_of),
         [(v, VMEM) for v in (small_ffn, small_attn, *biases)],
@@ -846,64 +899,61 @@
     def small_step(value):
         return value + moves.flip(value, *flips.pop(0))
 
-    done2, near, far, a_given0 = sync(done2, near, far, a_given0)
-    done2 = moves.give(done2, 2)
-    near_f0_a2, far_a13, a_come0 = moves.near(near), moves.far(far), moves.core(a_given0)
+    done3, near, far, a_given0, small = sync(done3, near, far, a_given0, small)
+    done3, near_a23, far_f0 = moves.give(done3, 3), moves.near(near), moves.far(far)
+    a_come0 = moves.core(a_given0)
     small = small_step(small)
-    near_f0_a2, far_a13, a_come0, done2, small = sync(near_f0_a2, far_a13, a_come0, done2, small)
-
-    a0 = Slots(a_kept0, a_come0)
-    over0 = Block(far_f0_a2, wide, piece)
-    ffn_final, a_done2, near, far = mix(
-        [[*f0_slot(3), Block(near_f0_a2, 0, piece), over0, Block(done3), Block(done2)]],
-        [[*a2.slot(3), Block(near_f0_a2, piece, half), Block(far_f0_a2, wide + piece, half)]],
-        [[*a1.slot(0), Block(far_a13, 0, half)], [*a3.slot(0), Block(far_a13, half, half)]],
-        [a0.slot(2), a0.slot(1)],
+    done3, near_a23, far_f0, a_come0, small = sync(done3, near_a23, far_f0, a_come0, small)
+
+    a1, a0 = Slots(a_kept1, a_come1), Slots(a_kept0, a_come0)
+    a_done2, near, far = mix(
+        a2.passed(3, (near_a23, 0), (far_a23, 2 * half)),
+        f0.passed(0, (far_f0, 0)),
+        [a1.slot(2), a0.slot(2), a1.slot(1), a0.slot(1)],
         name="mix_13",
     )
+    a_done2, near, far, small = sync(a_done2, near, far, small)
+    a_done2, near_f0, far_a10 = moves.hand_on(a_done2), moves.near(near), moves.far(far)
+    small = small_step(small)
+    a_done2, near_f0, far_a10, small = sync(a_done2, near_f0, far_a10, small)
+
+    a_for_one, a_for_three = split(a_done2)
+    arrived = ((near_f0, 0), (far_f0, piece), (done1, 0), (done3, 0))
+    (ffn_final,) = mix(f0.passed(3, *arrived), name="mix_14")
     if dp_size > 8:
         ffn_final = over_rest(ffn_final, dp_size)
-    near, far = mix([Block(near), Block(ffn_final)], [Block(far), Block(ffn_final)], name="mix_14")
-    a_done2, near, far = sync(a_done2, near, far)
-    a_done2 = moves.give(a_done2, 2)
-    near_a13_f, far_a0_f = moves.near(near), moves.far(far)
+    a_done3, near = mix(
+        a3.passed(3, (near_a23, half), (far_a23, 3 * half), (a_for_three, 0)),
+        a1.passed(0, (far_a10, 0)) + a0.passed(0, (far_a10, half)) + [Block(ffn_final)],
+        name="mix_15",
+    )
+    ffn_final, near, a_done3, small = sync(ffn_final, near, a_done3, small)
+    near_a10_f, ffn_over, a_done3 = moves.near(near), moves.far(ffn_final), moves.give(a_done3, 3)
     small = small_step(small)
-    near_a13_f, far_a0_f, a_done2, small = sync(near_a13_f, far_a0_f, a_done2, small)
-
-    a_done1, a_done3, near, far = mix(
-        [[*a1.slot(3), Block(near_a13_f, 0, half), Block(far_a13, 2 * half, half)]],
-        [[*a3.slot(3), Block(near_a13_f, half, half), Block(far_a13, 3 * half, half)]],
-        [[*a0.slot(0), Block(far_a0_f, 0, half)]],
-        [Block(near_a13_f, 2 * half, piece)],
-        name="mix_15",
-    )
-    a_done1, a_done3, near, far = sync(a_done1, a_done3, near, far)
-    a_done1, a_done3 = moves.give(a_done1, 1), moves.give(a_done3, 3)
-    near_a0, ffn_corner = moves.near(near), moves.far(far)
+    near_a10_f, ffn_over, a_done3, small = sync(near_a10_f, ffn_over, a_done3, small)
+
+    a_done1, far = mix(
+        a1.passed(3, (near_a10_f, 0), (far_a10, 2 * half), (a_for_one, 0)),
+        [Block(near_a10_f, 2 * half, piece)],
+        name="mix_16",
+    )
+    a_done1, far, small = sync(a_done1, far, small)
+    ffn_corner, a_done1 = moves.far(far), moves.give(a_done1, 1)
     small = small_step(small)
-    a_done1, a_done3, near_a0, ffn_corner, small = sync(a_done1, a_done3, near_a0, ffn_corner, small)
-
-    own_ffn = (
-        Block(ffn_final),
-        Block(near_a13_f, 2 * half, piece),
-        Block(far_a0_f, 2 * half, piece),
-        Block(ffn_corner),
-    )
-    attn_final, other_ffn = mix(
-        [[*a0.slot(3), Block(near_a0), Block(far_a0_f, half, half), *map(Block, (a_done1, a_done2, a_done3))]],
-        own_ffn,
-        name="mix_16",
-    )
+    ffn_corner, a_done1, small = sync(ffn_corner, a_done1, small)
+
+    own_ffn = (Block(ffn_final), Block(near_a10_f, 2 * half, piece), Block(ffn_over), Block(ffn_corner))
+    arrived = ((near_a10_f, half), (far_a10, 3 * half), (a_done1, 0), (a_done3, 0))
+    attn_final, other_ffn = mix(a0.passed(3, *arrived), own_ffn, name="mix_18")
     if dp_size > 8:
         attn_final = over_rest(attn_final, dp_size)
-    attn_final, other_ffn = sync(attn_final, other_ffn)
+    attn_final, other_ffn, small = sync(attn_final, other_ffn, small)
     attn_near, attn_over, other_ffn = moves.near(attn_final), moves.far(attn_final), moves.core(other_ffn)
-    small = small_step(small)
-    attn_near, attn_over, other_ffn, small = sync(attn_near, attn_over, other_ffn, small)
-
-    attn_corner = moves.far(attn_near)
     while flips:
         small = small_step(small)
+    attn_near, attn_over, other_ffn, small = sync(attn_near, attn_over, other_ffn, small)
+
+    attn_corner = moves.far(attn_near)
 
     def out(kernel, rows_in, own, other, outs, name):
         refs = Refs()

time: 232 us -> 215 us (0.927)
  waiting for transfers between devices: 118 us -> 93.1 us
  starting transfers between devices: 44.9 us -> 51.4 us
    ppermute x56 -> x58, waiting for transfers between devices: 118 us -> 93.1 us  [build(): return lax.ppermute(value, AXES, pairs)]
    ppermute x56 -> x58, starting transfers between devices: 44.9 us -> 51.4 us  [build(): return lax.ppermute(value, AXES, pairs)]
    pallas_call x35 -> x40, Pallas kernels: 61.5 us -> 62.8 us  [call(): pl.pallas_call(kernel, in_specs=[spec for _, spec in ins], out_specs=[VME...]
  transfers between devices with their start and end apart: 56 -> 58, of which waited for: 27 -> 32; matrix products, arithmetic and copies ran while one was open for 1% -> 1% of each run, Pallas kernels for 20% -> 22%
where the time goes in v3:
time: 215 us; the launch traced here: 212 us
  waiting for transfers between devices  93.1 us (43%)
  Pallas kernels  62.8 us (29%)
  starting transfers between devices  51.4 us (24%)
  local copies, waits for them, and re-layouts  2.85 us (1%)
    ppermute x58, waiting for transfers between devices, build(): return lax.ppermute(value, AXES, pairs)  93.1 us
    pallas_call x40, Pallas kernels, call(): pl.pallas_call(kernel, in_specs=[spec for _, spec in ins], out_specs=[VME...  62.8 us
    ppermute x58, starting transfers between devices, build(): return lax.ppermute(value, AXES, pairs)  51.4 us
  transfers between devices with their start and end apart: 58, of which 32 were waited for; matrix products, arithmetic and copies ran while one was open for 1% of the time, Pallas kernels for 22%

profile of v3, /device:TPU:0, one launch (start us, length us, event | category | flops | bytes accessed | tf_op | source)
XLA Modules:
  0.0 211.6 jit_solution(5764419054349976651)
XLA Ops:
  3.5 5.1 %collective-permute-start = (bf16[112,768]{1,0:T(8,128)(2,1)}, bf16[112,768]{1,0:T(8,128)(2,1)S(1)}, u32[]{:S(2)}, u32[]{:S(2)}) collective-permute-start(bf16[112,768]{1,0:T(8,128)(2,1)} %get-tuple-element.244), channel_id=1, source_target_pairs={{1,0},{2,1},{3,2},{0,3},{5,4},{6,5},{7,6},{4,7},{9,8},{10,9},{11,1... | collective-permute-start | bytes 516104 | tf_op jit(solution)/shard_map/ppermute | solution.py:30
  13.7 3.3 %collective-permute-done.1.other.refs_1_.first = bf16[112,768]{1,0:T(8,128)(2,1)S(1)} collective-permute-done((bf16[112,768]{1,0:T(8,128)(2,1)}, bf16[112,768]{1,0:T(8,128)(2,1)S(1)}, u32[]{:S(2)}, u32[]{:S(2)}) %collective-permute-start.1) | collective-permute-done | bytes 172064 | tf_op jit(solution)/shard_map/ppermute | solution.py:30
  21.9 5.0 %collective-permute-done.2.refs_0_.first = bf16[112,768]{1,0:T(8,128)(2,1)S(1)} collective-permute-done((bf16[112,768]{1,0:T(8,128)(2,1)S(1)}, bf16[112,768]{1,0:T(8,128)(2,1)S(1)}, u32[]{:S(2)}, u32[]{:S(2)}) %collective-permute-start.2) | collective-permute-done | bytes 172064 | tf_op jit(solution)/shard_map/ppermute | solution.py:30
  30.3 4.9 %collective-permute-done.6.refs_0_.refs_3_.refs_1_ = bf16[96,768]{1,0:T(8,128)(2,1)S(1)} collective-permute-done((bf16[96,768]{1,0:T(8,128)(2,1)S(1)}, bf16[96,768]{1,0:T(8,128)(2,1)S(1)}, u32[]{:S(2)}, u32[]{:S(2)}) %collective-permute-start.6) | collective-permute-done | bytes 147488 | tf_op jit(solution)/shard_map/ppermute | solution.py:30
  39.4 8.7 %collective-permute-done.8.other.refs_1_.refs_0_ = bf16[192,768]{1,0:T(8,128)(2,1)S(1)} collective-permute-done((bf16[192,768]{1,0:T(8,128)(2,1)S(1)}, bf16[192,768]{1,0:T(8,128)(2,1)S(1)}, u32[]{:S(2)}, u32[]{:S(2)}) %collective-permute-start.8) | collective-permute-done | bytes 294944 | tf_op jit(solution)/shard_map/ppermute | solution.py:30
  52.5 3.9 %attn_1.1 = (bf16[576,512]{1,0:T(8,128)(2,1)S(1)}, bf16[12,128,128]{2,1,0:T(8,128)(2,1)S(1)}, bf16[192,512]{1,0:T(8,128)(2,1)S(1)}, f32[8,768]{1,0:T(8,128)S(1)}...) custom-call(s32[16]{0:T(128)S(1)} %copy-done.12, bf16[512,768]{1,0:T(8,128)(2,1)S(1)} %get-tuple-element.249.mixed, ...), custom_call_target="tpu_custom_call" | custom-call | flops 6039797 | bytes 90194 | tf_op jit(solution)/shard_map/attn_1/pallas_call | solution.py:537
  56.4 4.0 %attn_3.1 = (bf16[576,512]{1,0:T(8,128)(2,1)S(1)}, bf16[12,128,128]{2,1,0:T(8,128)(2,1)S(1)}, bf16[192,512]{1,0:T(8,128)(2,1)S(1)}, f32[8,768]{1,0:T(8,128)S(1)}...) custom-call(s32[16]{0:T(128)S(1)} %copy-done.12, bf16[512,768]{1,0:T(8,128)(2,1)S(1)} %get-tuple-element.249.mixed, ...), custom_call_target="tpu_custom_call" | custom-call | flops 6039797 | bytes 90194 | tf_op jit(solution)/shard_map/attn_3/pallas_call | solution.py:537
  63.3 4.4 %attn_2.1 = (bf16[576,512]{1,0:T(8,128)(2,1)S(1)}, bf16[12,128,128]{2,1,0:T(8,128)(2,1)S(1)}, bf16[192,512]{1,0:T(8,128)(2,1)S(1)}, f32[8,768]{1,0:T(8,128)S(1)}...) custom-call(s32[16]{0:T(128)S(1)} %copy-done.12, ...), custom_call_target="tpu_custom_call" | custom-call | flops 6039797 | bytes 93307 | tf_op jit(solution)/shard_map/attn_2/pallas_call | solution.py:537
  77.9 3.8 %collective-permute-done.19.refs_3_.refs_6_ = bf16[192,768]{1,0:T(8,128)(2,1)S(1)} collective-permute-done((bf16[192,768]{1,0:T(8,128)(2,1)S(1)}, bf16[192,768]{1,0:T(8,128)(2,1)S(1)}, u32[]{:S(2)}, u32[]{:S(2)}) %collective-permute-start.19) | collective-permute-done | bytes 294944 | tf_op jit(solution)/shard_map/ppermute | solution.py:30
  84.6 4.6 %ffn_2.1 = (bf16[512,768]{1,0:T(8,128)(2,1)S(1)}, bf16[512,768]{1,0:T(8,128)(2,1)S(1)}, bf16[1536,768]{1,0:T(8,128)(2,1)S(1)}, bf16[512,768]{1,0:T(8,128)(2,1)},...) custom-call(bf16[512,768]{1,0:T(8,128)(2,1)S(1)} %get-tuple-element.276.normed, ...), custom_call_target="tpu_custom_call" | custom-call | flops 12079595 | bytes 145244 | tf_op jit(solution)/shard_map/ffn_2/pallas_call | solution.py:537
  89.3 3.0 %ffn_back_2.1 = (bf16[768,768]{1,0:T(8,128)(2,1)S(1)}, bf16[768,768]{1,0:T(8,128)(2,1)S(1)}, f32[512,768]{1,0:T(8,128)S(1)}, f32[8,768]{1,0:T(8,128)S(1)}) custom-call(bf16[512,768]{1,0:T(8,128)(2,1)S(1)} %get-tuple-element.297.grad_low, bf16[512,768]{1,0:T(8,128)(2,1)S(1)} %get-tuple-element.276.normed, f32[512,768]{1,0:T(8,128)S(1)} %get-tuple-element.298.part, ...), custom_call_target="tpu_custom_call" | custom-call | flops 24159192 | bytes 110346 | tf_op jit(solution)/shard_map/ffn_back_2/pallas_call | solution.py:537
  92.6 3.0 %ffn_back_1.1 = (bf16[768,768]{1,0:T(8,128)(2,1)S(1)}, bf16[768,768]{1,0:T(8,128)(2,1)S(1)}, f32[512,768]{1,0:T(8,128)S(1)}, f32[8,768]{1,0:T(8,128)S(1)}) custom-call(bf16[512,768]{1,0:T(8,128)(2,1)S(1)} %get-tuple-element.297.grad_low, bf16[512,768]{1,0:T(8,128)(2,1)S(1)} %get-tuple-element.276.normed, f32[512,768]{1,0:T(8,128)S(1)} %get-tuple-element.302.part, ...), custom_call_target="tpu_custom_call" | custom-call | flops 24159192 | bytes 110346 | tf_op jit(solution)/shard_map/ffn_back_1/pallas_call | solution.py:537
  96.5 6.1 %ffn_back_30.1 = (bf16[768,768]{1,0:T(8,128)(2,1)S(1)}, bf16[768,768]{1,0:T(8,128)(2,1)S(1)}, bf16[1536,768]{1,0:T(8,128)(2,1)S(1)}, f32[512,768]{1,0:T(8,128)S(1)}, f32[8,768]{1,0:T(8,128)S(1)}) custom-call(bf16[512,768]{1,0:T(8,128)(2,1)S(1)} %get-tuple-element.297.grad_low, bf16[512,768]{1,0:T(8,128)(2,1)S(1)} %get-tuple-element.276.normed, ...), custom_call_target="tpu_custom_call" | custom-call | flops 48318384 | bytes 173260 | tf_op jit(solution)/shard_map/ffn_back_30/pallas_call | solution.py:537
  102.6 3.3 %collective-permute-done.23.refs_2_.refs_3_ = bf16[384,768]{1,0:T(8,128)(2,1)S(1)} collective-permute-done((bf16[384,768]{1,0:T(8,128)(2,1)S(1)}, bf16[384,768]{1,0:T(8,128)(2,1)S(1)}, u32[]{:S(2)}, u32[]{:S(2)}) %collective-permute-start.23) | collective-permute-done | bytes 589856 | tf_op jit(solution)/shard_map/ppermute | solution.py:30
  108.0 6.9 %attn_back_23.1 = (bf16[384,768]{1,0:T(8,128)(2,1)S(1)}, bf16[384,768]{1,0:T(8,128)(2,1)S(1)}, bf16[768,768]{1,0:T(8,128)(2,1)S(1)}, f32[512,768]{1,0:T(8,128)S(...) custom-call(bf16[512,768]{1,0:T(8,128)(2,1)S(1)} %get-tuple-element.249.mixed, ...), custom_call_target="tpu_custom_call" | custom-call | flops 24159192 | bytes 137052 | tf_op jit(solution)/shard_map/attn_back_23/pallas_call | solution.py:537
  125.6 4.6 %collective-permute-done.28.refs_2_ = bf16[192,768]{1,0:T(8,128)(2,1)S(1)} collective-permute-done((bf16[192,768]{1,0:T(8,128)(2,1)S(1)}, bf16[192,768]{1,0:T(8,128)(2,1)S(1)}, u32[]{:S(2)}, u32[]{:S(2)}) %collective-permute-start.28) | collective-permute-done | bytes 294944 | tf_op jit(solution)/shard_map/ppermute | solution.py:30
  136.5 4.3 %attn_back_0.1 = (bf16[384,768]{1,0:T(8,128)(2,1)S(1)}, bf16[384,768]{1,0:T(8,128)(2,1)S(1)}, bf16[512,768]{1,0:T(8,128)(2,1)}, f32[8,768]{1,0:T(8,128)S(1)}) custom-call(bf16[512,768]{1,0:T(8,128)(2,1)S(1)} %get-tuple-element.249.mixed, f32[512,768]{1,0:T(8,128)S(1)} %get-tuple-element.382.part, bf16[512,768]{1,0:T(8,128)(2,1)S(1)} %get-tuple-element.359.refs_0_, ...), custom_call_target="tpu_custom_call" | custom-call | flops 12079595 | bytes 74958 | tf_op jit(solution)/shard_map/attn_back_0/pallas_call | solution.py:537
  140.8 3.1 %collective-permute-done.32.refs_2_ = bf16[192,768]{1,0:T(8,128)(2,1)S(1)} collective-permute-done((bf16[192,768]{1,0:T(8,128)(2,1)S(1)}, bf16[192,768]{1,0:T(8,128)(2,1)S(1)}, u32[]{:S(2)}, u32[]{:S(2)}) %collective-permute-start.32) | collective-permute-done | bytes 294944 | tf_op jit(solution)/shard_map/ppermute | solution.py:30
  152.1 4.9 %collective-permute-done.36.refs_5_ = bf16[192,768]{1,0:T(8,128)(2,1)S(1)} collective-permute-done((bf16[192,768]{1,0:T(8,128)(2,1)S(1)}, bf16[192,768]{1,0:T(8,128)(2,1)S(1)}, u32[]{:S(2)}, u32[]{:S(2)}) %collective-permute-start.36) | collective-permute-done | bytes 294944 | tf_op jit(solution)/shard_map/ppermute | solution.py:30
  164.4 7.6 %collective-permute-done.44 = f32[16,768]{1,0:T(8,128)S(1)} collective-permute-done((f32[16,768]{1,0:T(8,128)S(1)}, f32[16,768]{1,0:T(8,128)S(1)}, u32[]{:S(2)}, u32[]{:S(2)}) %collective-permute-start.44) | collective-permute-done | bytes 49184 | tf_op jit(solution)/shard_map/ppermute | solution.py:30
  177.9 7.2 %collective-permute-done.48 = f32[16,768]{1,0:T(8,128)S(1)} collective-permute-done((f32[16,768]{1,0:T(8,128)S(1)}, f32[16,768]{1,0:T(8,128)S(1)}, u32[]{:S(2)}, u32[]{:S(2)}) %collective-permute-start.48) | collective-permute-done | bytes 49184 | tf_op jit(solution)/shard_map/ppermute | solution.py:30
  188.2 3.6 %collective-permute-done.51 = f32[16,768]{1,0:T(8,128)S(1)} collective-permute-done((f32[16,768]{1,0:T(8,128)S(1)}, f32[16,768]{1,0:T(8,128)S(1)}, u32[]{:S(2)}, u32[]{:S(2)}) %collective-permute-start.51) | collective-permute-done | bytes 49184 | tf_op jit(solution)/shard_map/ppermute | solution.py:30
  191.8 3.5 %collective-permute-done.50.refs_4_ = bf16[96,768]{1,0:T(8,128)(2,1)S(1)} collective-permute-done((bf16[96,768]{1,0:T(8,128)(2,1)S(1)}, bf16[96,768]{1,0:T(8,128)(2,1)S(1)}, u32[]{:S(2)}, u32[]{:S(2)}) %collective-permute-start.50) | collective-permute-done | bytes 147488 | tf_op jit(solution)/shard_map/ppermute | solution.py:30
  198.5 3.9 %collective-permute-done.55 = f32[16,768]{1,0:T(8,128)S(1)} collective-permute-done((f32[16,768]{1,0:T(8,128)S(1)}, f32[16,768]{1,0:T(8,128)S(1)}, u32[]{:S(2)}, u32[]{:S(2)}) %collective-permute-start.55) | collective-permute-done | bytes 49184 | tf_op jit(solution)/shard_map/ppermute | solution.py:30
  (171 shorter events, 97.6 us)
Async XLA Ops:
  3.5 10.2 %collective-permute-start = (bf16[112,768]{1,0:T(8,128)(2,1)}, bf16[112,768]{1,0:T(8,128)(2,1)S(1)}, u32[]{:S(2)}, u32[]{:S(2)}) collective-permute-start(bf16[112,768]{1,0:T(8,128)(2,1)} %get-tuple-element.244), channel_id=1, source_target_pairs={{1,0},{2,1},{3,2},{0,3},{5,4},{6,5},{7,6},{4,7},{9,8},{10,9},{11,1... | collective-permute-start | bytes 516104 | tf_op jit(solution)/shard_map/ppermute | solution.py:30
  36.5 11.6 %collective-permute-start.11 = (bf16[768,768]{1,0:T(8,128)(2,1)S(1)}, bf16[768,768]{1,0:T(8,128)(2,1)S(1)}, u32[]{:S(2)}, u32[]{:S(2)}) collective-permute-start(bf16[768,768]{1,0:T(8,128)(2,1)S(1)} %get-tuple-element.264), channel_id=1, source_target_pairs={{4,0},{5,1},{6,2},{7,3},{0,4},{1,5},{2,6},{3,7},{12,8},{13,9},{14,... | collective-permute-start | bytes 3538952 | tf_op jit(solution)/shard_map/ppermute | solution.py:30
  36.6 11.5 %collective-permute-start.10 = (bf16[288,768]{1,0:T(8,128)(2,1)S(1)}, bf16[288,768]{1,0:T(8,128)(2,1)S(1)}, u32[]{:S(2)}, u32[]{:S(2)}) collective-permute-start(bf16[288,768]{1,0:T(8,128)(2,1)S(1)} %get-tuple-element.263), channel_id=1, source_target_pairs={{16,0},{17,1},{18,2},{19,3},{12,4},{13,5},{14,6},{15,7},{24,8},{25... | collective-permute-start | bytes 1327112 | tf_op jit(solution)/shard_map/ppermute | solution.py:30
  36.9 11.1 %collective-permute-start.8 = (bf16[192,768]{1,0:T(8,128)(2,1)S(1)}, bf16[192,768]{1,0:T(8,128)(2,1)S(1)}, u32[]{:S(2)}, u32[]{:S(2)}) collective-permute-start(bf16[192,768]{1,0:T(8,128)(2,1)S(1)} %copy-done.15), channel_id=1, source_target_pairs={{3,0},{0,1},{1,2},{2,3},{7,4},{4,5},{5,6},{6,7},{11,8},{8,9},{9,10... | collective-permute-start | bytes 884744 | tf_op jit(solution)/shard_map/ppermute | solution.py:30
  48.2 13.1 %collective-permute-start.14 = (bf16[384,768]{1,0:T(8,128)(2,1)S(1)}, bf16[384,768]{1,0:T(8,128)(2,1)S(1)}, u32[]{:S(2)}, u32[]{:S(2)}) collective-permute-start(bf16[384,768]{1,0:T(8,128)(2,1)S(1)} %get-tuple-element.268), channel_id=1, source_target_pairs={{16,0},{17,1},{18,2},{19,3},{12,4},{13,5},{14,6},{15,7},{24,8},{25... | collective-permute-start | bytes 1769480 | tf_op jit(solution)/shard_map/ppermute | solution.py:30
  48.7 12.6 %collective-permute-start.15 = (bf16[384,768]{1,0:T(8,128)(2,1)S(1)}, bf16[384,768]{1,0:T(8,128)(2,1)S(1)}, u32[]{:S(2)}, u32[]{:S(2)}) collective-permute-start(bf16[384,768]{1,0:T(8,128)(2,1)S(1)} %get-tuple-element.269), channel_id=1, source_target_pairs={{4,0},{5,1},{6,2},{7,3},{0,4},{1,5},{2,6},{3,7},{12,8},{13,9},{14,... | collective-permute-start | bytes 1769480 | tf_op jit(solution)/shard_map/ppermute | solution.py:30
  49.2 11.2 %collective-permute-start.12 = (bf16[192,768]{1,0:T(8,128)(2,1)S(1)}, bf16[192,768]{1,0:T(8,128)(2,1)S(1)}, u32[]{:S(2)}, u32[]{:S(2)}) collective-permute-start(bf16[192,768]{1,0:T(8,128)(2,1)S(1)} %pick.3), channel_id=1, source_target_pairs={{1,0},{2,1},{3,2},{0,3},{7,4},{4,5},{5,6},{6,7},{9,8},{10,9},{11,1... | collective-permute-start | bytes 884744 | tf_op jit(solution)/shard_map/ppermute | solution.py:30
  61.4 13.2 %collective-permute-start.18 = (bf16[768,768]{1,0:T(8,128)(2,1)S(1)}, bf16[768,768]{1,0:T(8,128)(2,1)S(1)}, u32[]{:S(2)}, u32[]{:S(2)}) collective-permute-start(bf16[768,768]{1,0:T(8,128)(2,1)S(1)} %get-tuple-element.281), channel_id=1, source_target_pairs={{4,0},{5,1},{6,2},{7,3},{0,4},{1,5},{2,6},{3,7},{12,8},{13,9},{14,... | collective-permute-start | bytes 3538952 | tf_op jit(solution)/shard_map/ppermute | solution.py:30
  61.6 13.1 %collective-permute-start.17 = (bf16[384,768]{1,0:T(8,128)(2,1)S(1)}, bf16[384,768]{1,0:T(8,128)(2,1)S(1)}, u32[]{:S(2)}, u32[]{:S(2)}) collective-permute-start(bf16[384,768]{1,0:T(8,128)(2,1)S(1)} %get-tuple-element.280), channel_id=1, source_target_pairs={{16,0},{17,1},{18,2},{19,3},{12,4},{13,5},{14,6},{15,7},{24,8},{25... | collective-permute-start | bytes 1769480 | tf_op jit(solution)/shard_map/ppermute | solution.py:30
  95.7 10.2 %collective-permute-start.24 = (bf16[768,768]{1,0:T(8,128)(2,1)S(1)}, bf16[768,768]{1,0:T(8,128)(2,1)S(1)}, u32[]{:S(2)}, u32[]{:S(2)}) collective-permute-start(bf16[768,768]{1,0:T(8,128)(2,1)S(1)} %get-tuple-element.315), channel_id=1, source_target_pairs={{4,0},{5,1},{6,2},{7,3},{0,4},{1,5},{2,6},{3,7},{12,8},{13,9},{14,... | collective-permute-start | bytes 3538952 | tf_op jit(solution)/shard_map/ppermute | solution.py:30
  106.2 13.2 %collective-permute-start.27 = (bf16[1536,768]{1,0:T(8,128)(2,1)S(1)}, bf16[1536,768]{1,0:T(8,128)(2,1)S(1)}, u32[]{:S(2)}, u32[]{:S(2)}) collective-permute-start(bf16[1536,768]{1,0:T(8,128)(2,1)S(1)} %get-tuple-element.332), channel_id=1, source_target_pairs={{4,0},{5,1},{6,2},{7,3},{0,4},{1,5},{2,6},{3,7},{12,8},{13,9},{14,... | collective-permute-start | bytes 7077896 | tf_op jit(solution)/shard_map/ppermute | solution.py:30
  106.2 13.1 %collective-permute-start.26 = (bf16[384,768]{1,0:T(8,128)(2,1)S(1)}, bf16[384,768]{1,0:T(8,128)(2,1)S(1)}, u32[]{:S(2)}, u32[]{:S(2)}) collective-permute-start(bf16[384,768]{1,0:T(8,128)(2,1)S(1)} %get-tuple-element.331), channel_id=1, source_target_pairs={{16,0},{17,1},{18,2},{19,3},{12,4},{13,5},{14,6},{15,7},{24,8},{25... | collective-permute-start | bytes 1769480 | tf_op jit(solution)/shard_map/ppermute | solution.py:30
  119.7 13.2 %collective-permute-start.30 = (bf16[768,768]{1,0:T(8,128)(2,1)S(1)}, bf16[768,768]{1,0:T(8,128)(2,1)S(1)}, u32[]{:S(2)}, u32[]{:S(2)}) collective-permute-start(bf16[768,768]{1,0:T(8,128)(2,1)S(1)} %get-tuple-element.356), channel_id=1, source_target_pairs={{4,0},{5,1},{6,2},{7,3},{0,4},{1,5},{2,6},{3,7},{12,8},{13,9},{14,... | collective-permute-start | bytes 3538952 | tf_op jit(solution)/shard_map/ppermute | solution.py:30
  119.8 13.1 %collective-permute-start.29 = (bf16[384,768]{1,0:T(8,128)(2,1)S(1)}, bf16[384,768]{1,0:T(8,128)(2,1)S(1)}, u32[]{:S(2)}, u32[]{:S(2)}) collective-permute-start(bf16[384,768]{1,0:T(8,128)(2,1)S(1)} %get-tuple-element.355), channel_id=1, source_target_pairs={{16,0},{17,1},{18,2},{19,3},{12,4},{13,5},{14,6},{15,7},{24,8},{25... | collective-permute-start | bytes 1769480 | tf_op jit(solution)/shard_map/ppermute | solution.py:30
  133.4 13.2 %collective-permute-start.33 = (bf16[384,768]{1,0:T(8,128)(2,1)S(1)}, bf16[384,768]{1,0:T(8,128)(2,1)S(1)}, u32[]{:S(2)}, u32[]{:S(2)}) collective-permute-start(bf16[384,768]{1,0:T(8,128)(2,1)S(1)} %get-tuple-element.379), channel_id=1, source_target_pairs={{16,0},{17,1},{18,2},{19,3},{12,4},{13,5},{14,6},{15,7},{24,8},{25... | collective-permute-start | bytes 1769480 | tf_op jit(solution)/shard_map/ppermute | solution.py:30
  133.9 12.7 %collective-permute-start.34 = (bf16[384,768]{1,0:T(8,128)(2,1)S(1)}, bf16[384,768]{1,0:T(8,128)(2,1)S(1)}, u32[]{:S(2)}, u32[]{:S(2)}) collective-permute-start(bf16[384,768]{1,0:T(8,128)(2,1)S(1)} %get-tuple-element.380), channel_id=1, source_target_pairs={{4,0},{5,1},{6,2},{7,3},{0,4},{1,5},{2,6},{3,7},{12,8},{13,9},{14,... | collective-permute-start | bytes 1769480 | tf_op jit(solution)/shard_map/ppermute | solution.py:30
  135.1 11.5 %collective-permute-start.35 = (bf16[192,768]{1,0:T(8,128)(2,1)S(1)}, bf16[192,768]{1,0:T(8,128)(2,1)S(1)}, u32[]{:S(2)}, u32[]{:S(2)}) collective-permute-start(bf16[192,768]{1,0:T(8,128)(2,1)S(1)} %get-tuple-element.381), channel_id=1, source_target_pairs={{3,0},{0,1},{1,2},{2,3},{7,4},{4,5},{5,6},{6,7},{11,8},{8,9},{9,10... | collective-permute-start | bytes 884744 | tf_op jit(solution)/shard_map/ppermute | solution.py:30
  147.1 13.1 %collective-permute-start.38 = (bf16[384,768]{1,0:T(8,128)(2,1)S(1)}, bf16[384,768]{1,0:T(8,128)(2,1)S(1)}, u32[]{:S(2)}, u32[]{:S(2)}) collective-permute-start(bf16[384,768]{1,0:T(8,128)(2,1)S(1)} %get-tuple-element.409), channel_id=1, source_target_pairs={{16,0},{17,1},{18,2},{19,3},{12,4},{13,5},{14,6},{15,7},{24,8},{25... | collective-permute-start | bytes 1769480 | tf_op jit(solution)/shard_map/ppermute | solution.py:30
  147.6 12.6 %collective-permute-start.39 = (bf16[384,768]{1,0:T(8,128)(2,1)S(1)}, bf16[384,768]{1,0:T(8,128)(2,1)S(1)}, u32[]{:S(2)}, u32[]{:S(2)}) collective-permute-start(bf16[384,768]{1,0:T(8,128)(2,1)S(1)} %get-tuple-element.410), channel_id=1, source_target_pairs={{4,0},{5,1},{6,2},{7,3},{0,4},{1,5},{2,6},{3,7},{12,8},{13,9},{14,... | collective-permute-start | bytes 1769480 | tf_op jit(solution)/shard_map/ppermute | solution.py:30
  160.5 11.9 %collective-permute-start.43 = (bf16[384,768]{1,0:T(8,128)(2,1)S(1)}, bf16[384,768]{1,0:T(8,128)(2,1)S(1)}, u32[]{:S(2)}, u32[]{:S(2)}) collective-permute-start(bf16[384,768]{1,0:T(8,128)(2,1)S(1)} %get-tuple-element.423), channel_id=1, source_target_pairs={{16,0},{17,1},{18,2},{19,3},{12,4},{13,5},{14,6},{15,7},{24,8},{25... | collective-permute-start | bytes 1769480 | tf_op jit(solution)/shard_map/ppermute | solution.py:30
  161.0 11.0 %collective-permute-start.42 = (bf16[192,768]{1,0:T(8,128)(2,1)S(1)}, bf16[192,768]{1,0:T(8,128)(2,1)S(1)}, u32[]{:S(2)}, u32[]{:S(2)}) collective-permute-start(bf16[192,768]{1,0:T(8,128)(2,1)S(1)} %get-tuple-element.422), channel_id=1, source_target_pairs={{8,0},{9,1},{10,2},{11,3},{20,4},{21,5},{22,6},{23,7},{0,8},{1,9},... | collective-permute-start | bytes 884744 | tf_op jit(solution)/shard_map/ppermute | solution.py:30
  172.9 12.8 %collective-permute-start.45 = (bf16[384,768]{1,0:T(8,128)(2,1)S(1)}, bf16[384,768]{1,0:T(8,128)(2,1)S(1)}, u32[]{:S(2)}, u32[]{:S(2)}) collective-permute-start(bf16[384,768]{1,0:T(8,128)(2,1)S(1)} %get-tuple-element.434), channel_id=1, source_target_pairs={{8,0},{9,1},{10,2},{11,3},{20,4},{21,5},{22,6},{23,7},{0,8},{1,9},... | collective-permute-start | bytes 1769480 | tf_op jit(solution)/shard_map/ppermute | solution.py:30
  174.1 11.0 %collective-permute-start.46 = (bf16[192,768]{1,0:T(8,128)(2,1)S(1)}, bf16[192,768]{1,0:T(8,128)(2,1)S(1)}, u32[]{:S(2)}, u32[]{:S(2)}) collective-permute-start(bf16[192,768]{1,0:T(8,128)(2,1)S(1)} %mix_14.1.refs_10_.refs_6_.refs_0_), channel_id=1, source_target_pairs={{16,0},{17,1},{18,2},{19,3},{12,4},{13,5},{14,6},{15,7},{24,8},{25... | collective-permute-start | bytes 884744 | tf_op jit(solution)/shard_map/ppermute | solution.py:30
  174.6 10.5 %collective-permute-start.47 = (bf16[96,768]{1,0:T(8,128)(2,1)S(1)}, bf16[96,768]{1,0:T(8,128)(2,1)S(1)}, u32[]{:S(2)}, u32[]{:S(2)}) collective-permute-start(bf16[96,768]{1,0:T(8,128)(2,1)S(1)} %get-tuple-element.436), channel_id=1, source_target_pairs={{1,0},{2,1},{3,2},{0,3},{5,4},{6,5},{7,6},{4,7},{9,8},{10,9},{11,1... | collective-permute-start | bytes 442376 | tf_op jit(solution)/shard_map/ppermute | solution.py:30
  (50 other events, 358.9 us)

commit v4 on v3

--- a/solution.py
+++ b/solution.py
@@ -206,37 +206,36 @@
 EMBED, B_OUT, G_ATTN, S_ATTN, B_BACK, G_FFN, S_FFN = range(7)
 
 
-def prep_kernel(
-    width, half, piece, b_in, b_query, b_value, *refs
-):
-    vectors, refs = refs[:7], refs[7:]
-    wq, wk, wv, wo, w_in, w_back, attn_mine, ffn_mine, bias, vecs, rows, sems = refs
+def prep_kernel(width, half, b_in, b_query, b_value, wq, wk, wv, wo, attn_mine, bias, rows, sems):
     core, chip = where_am_i()
-    copies = []
     for index, ref in enumerate((wq, wk, wv, wo)):
         start = pl.multiple_of(core * half, half)
         copy = pltpu.make_async_copy(
             ref.at[pl.ds(start, half)], attn_mine.at[pl.ds(0, half)], sems.at[0]
         )
         pl.when(chip == index)(copy.start)
-    copies.append(copy)
-    for index, ref in enumerate((w_in, w_back)):
-        start = pl.multiple_of(chip * piece, piece)
-        copy = pltpu.make_async_copy(ref.at[pl.ds(start, piece)], ffn_mine, sems.at[1])
-        pl.when(core == index)(copy.start)
-    copies.append(copy)
     as_row = lambda ref: ref[...].astype(F32).reshape(1, -1)
     rows[...] = jnp.zeros_like(rows)
     rows[0:1, :] = as_row(b_in)
     rows[1:2, :width] = as_row(b_query)
     rows[1:2, 2 * width : 3 * width] = as_row(b_value)
     bias[...] = rows[...].astype(BF)
+    copy.wait()
+    attn_mine[half : half + BIAS_ROWS, :] = rows[...].astype(BF)
+
+
+def more_kernel(piece, *refs):
+    vectors = refs[:7]
+    w_in, w_back, ffn_mine, vecs, sems = refs[7:]
+    core, chip = where_am_i()
+    for index, ref in enumerate((w_in, w_back)):
+        start = pl.multiple_of(chip * piece, piece)
+        copy = pltpu.make_async_copy(ref.at[pl.ds(start, piece)], ffn_mine, sems.at[0])
+        pl.when(core == index)(copy.start)
     for index, ref in enumerate(vectors):
-        vecs[index : index + 1, :] = as_row(ref)
-    vecs[7:8, :] = rows[2:3, :]
-    for copy in copies:
-        copy.wait()
-    attn_mine[half : half + BIAS_ROWS, :] = rows[...].astype(BF)
+        vecs[index : index + 1, :] = ref[...].astype(F32).reshape(1, -1)
+    vecs[7:8, :] = jnp.zeros((1, vecs.shape[1]), F32)
+    copy.wait()
 
 
 def pick_kernel(own, other, out):
@@ -269,24 +268,31 @@
     return [mats[i * width : (i + 1) * width, :] for i in range(4)]
 
 
-def attn_turn_kernel(
-    width, seq, layout, last, part_rows, count, lengths, mixed, part, vecs, first, *refs
-):
+def attn_turn_kernel(width, seq, layouts, last, part_rows, count, lengths, mixed, part, vecs, *refs):
+    turns = len(layouts)
+    firsts, refs = refs[:turns], refs[turns:]
     pieces, refs = refs[:count], refs[count:]
-    qkv, soft, ctx, bias_in, mats = refs[:5]
-    sems = refs[-1]
-    copies = copy_in(pieces, layout, part_rows, mats, sems, attn_place(part_rows))
-    bias_in[...] = jnp.broadcast_to(first[part_rows : part_rows + 1, :].astype(F32), bias_in.shape)
-    for copy in copies:
-        copy.wait()
-    bias = first[part_rows + 1 : part_rows + 2, :].astype(F32)
-    total = part[...] + attend(
-        width, seq, lengths, mixed[...], attn_mats(mats, width), bias, qkv, soft, ctx
-    )
+    results, refs = refs[: 5 * turns], refs[5 * turns :]
+    all_sems = refs[-turns:]
+    started = [
+        copy_in(pieces, layouts[turn], part_rows, results[5 * turn + 4], all_sems[turn], attn_place(part_rows))
+        for turn in range(turns)
+    ]
+    total = part[...]
+    for turn in range(turns):
+        qkv, soft, ctx, bias_in, mats = results[5 * turn : 5 * turn + 5]
+        first = firsts[turn]
+        bias_in[...] = jnp.broadcast_to(first[part_rows : part_rows + 1, :].astype(F32), bias_in.shape)
+        for copy in started[turn]:
+            copy.wait()
+        bias = first[part_rows + 1 : part_rows + 2, :].astype(F32)
+        total = total + attend(
+            width, seq, lengths, mixed[...], attn_mats(mats, width), bias, qkv, soft, ctx
+        )
     if not last:
-        refs[5][...] = total
+        refs[0][...] = total
         return
-    hat, inv, normed = refs[5:8]
+    hat, inv, normed = refs[:3]
     ahat, ainv = norm_parts(total + mixed[...].astype(F32) + vecs[B_OUT : B_OUT + 1, :])
     hat[...] = ahat
     inv[...] = jnp.broadcast_to(ainv, inv.shape)
@@ -632,20 +638,22 @@
     own_mats = (w_query.T, w_key.T, w_value.T, w_out)
     dma = lambda n: pltpu.SemaphoreType.DMA((8 * n,))
 
-    attn_mine, ffn_mine, bias_pack, vecs = call(
-        functools.partial(prep_kernel, width, half, piece),
-        [(v, VMEM) for v in (b_in, b_query, b_value)]
-        + [(v, VMEM) for v in (mask_embed, b_out, g_attn, s_attn, b_back, g_ffn, s_ffn)]
-        + [(v, ANY) for v in (*own_mats, w_in, w_back)],
-        [
-            shape(half + BIAS_ROWS, model, BF),
-            shape(piece, model, BF),
-            shape(BIAS_ROWS, model, BF),
-            shape(8, model),
-        ],
-        [pltpu.VMEM((BIAS_ROWS, model), F32), pltpu.SemaphoreType.DMA((2,))],
+    attn_mine, bias_pack = call(
+        functools.partial(prep_kernel, width, half),
+        [(v, VMEM) for v in (b_in, b_query, b_value)] + [(v, ANY) for v in own_mats],
+        [shape(half + BIAS_ROWS, model, BF), shape(BIAS_ROWS, model, BF)],
+        [pltpu.VMEM((BIAS_ROWS, model), F32), pltpu.SemaphoreType.DMA((1,))],
         vmem=60,
         name="prep",
+    )
+    ffn_mine, vecs = call(
+        functools.partial(more_kernel, piece),
+        [(v, VMEM) for v in (mask_embed, after(b_out, attn_mine), g_attn, s_attn, b_back, g_ffn, s_ffn)]
+        + [(v, ANY) for v in (w_in, w_back)],
+        [shape(piece, model, BF), shape(8, model)],
+        [pltpu.SemaphoreType.DMA((1,))],
+        vmem=60,
+        name="more",
     )
     first1, first3 = (moves.fetch(attn_mine, turn) for turn in turns[:2])
 
@@ -694,31 +702,43 @@
         return blocks + [Block(other, (i * count_turns + turn) * rows, rows) for i in range(4)]
 
     qkvs, softs, ctxs, bias_ins, attn_wholes = [], [], [], [], []
-    for index, first in enumerate((first1, first3, first2)):
-        last = index == count - 1
+    for last, firsts in ((False, (first1, first3)), (True, (first2,))):
         if last:
             ffn2, near_f3, far_f1_f3, other2, attn_part = sync(ffn2, near_f3, far_f1_f3, other2, attn_part)
             own_f1 = (Block(ffn1), Block(near_f1), Block(far2_f1, half, piece), Block(far_f1_f3, 0, piece))
             far, other_f1 = mix([Block(near_f3), Block(ffn2)], own_f1, name="mix_5")
             near_f2, far_f3_f2, other_f1 = moves.near(ffn2), moves.far(far), moves.core(other_f1)
-        blocks = parts(own2, other2) if last else parts(own13, other13, index, half)
         refs = Refs()
-        layout = tuple(refs.add(block) for block in blocks)
-        outs = [shape(3 * width, rows, BF), soft_shape, shape(width, rows, BF), shape(8, model)]
-        outs += [shape(model, model, BF), shape(rows, model)]
+        layouts = []
+        for index in range(len(firsts)):
+            blocks = parts(own2, other2) if last else parts(own13, other13, index, half)
+            layouts.append(tuple(refs.add(block) for block in blocks))
+        outs = [
+            shape(3 * width, rows, BF),
+            soft_shape,
+            shape(width, rows, BF),
+            shape(8, model),
+            shape(model, model, BF),
+        ] * len(firsts)
+        outs += [shape(rows, model)]
         if last:
             outs += [shape(rows, 128), shape(rows, model, BF)]
-        qkv, soft, ctx, bias_in, whole, *others = call(
-            functools.partial(attn_turn_kernel, width, seq, layout, last, half, len(refs.arrays)),
-            [(lengths, SMEM), (mixed, VMEM), (attn_part, VMEM), (vecs, VMEM), (first, VMEM)]
+        results = call(
+            functools.partial(attn_turn_kernel, width, seq, tuple(layouts), last, half, len(refs.arrays)),
+            [(lengths, SMEM), (mixed, VMEM), (attn_part, VMEM), (vecs, VMEM)]
+            + [(first, VMEM) for first in firsts]
             + [(array, ANY) for array in refs.arrays],
             outs,
-            [dma(1)],
-            flops=turn_flops,
-            name=f"attn_{turns[index]}",
+            [dma(1)] * len(firsts),
+            flops=len(firsts) * turn_flops,
+            name="attn_2" if last else "attn_13",
         )
-        for values, value in zip((qkvs, softs, ctxs, bias_ins, attn_wholes), (qkv, soft, ctx, bias_in, whole)):
-            values.append(value)
+        for index in range(len(firsts)):
+            for values, value in zip(
+                (qkvs, softs, ctxs, bias_ins, attn_wholes), results[5 * index : 5 * index + 5]
+            ):
+                values.append(value)
+        others = results[5 * len(firsts) :]
         attn_part = others[0]
     hat1, inv1, normed = others
 
@@ -878,10 +898,12 @@
         near_f3, far_a23, a_come1, done1, a_given0, grad_input, a_bias0
     )
 
+    a1 = Slots(a_kept1, a_come1)
+    wide = piece + half
     done3, near, far = mix(
         f3.passed(3, (near_f3, 0), (far_f3, piece), (for_three, 0)),
         a2.passed(0, (far_a23, 0)) + a3.passed(0, (far_a23, half)),
-        [f0.slot(2), f0.slot(1)],
+        [f0.slot(2), a1.slot(2), f0.slot(1), a1.slot(1)],
         name="mix_12",
     )
     biases = (bias30, bias1, bias2, a_bias0, a_bias1, a_bias23)
@@ -900,59 +922,56 @@
         return value + moves.flip(value, *flips.pop(0))
 
     done3, near, far, a_given0, small = sync(done3, near, far, a_given0, small)
-    done3, near_a23, far_f0 = moves.give(done3, 3), moves.near(near), moves.far(far)
+    done3, near_a23, far_f0_a1 = moves.give(done3, 3), moves.near(near), moves.far(far)
     a_come0 = moves.core(a_given0)
-    small = small_step(small)
-    done3, near_a23, far_f0, a_come0, small = sync(done3, near_a23, far_f0, a_come0, small)
-
-    a1, a0 = Slots(a_kept1, a_come1), Slots(a_kept0, a_come0)
+    small = small_step(small_step(small))
+    done3, near_a23, far_f0_a1, a_come0, small = sync(done3, near_a23, far_f0_a1, a_come0, small)
+
+    a0 = Slots(a_kept0, a_come0)
     a_done2, near, far = mix(
         a2.passed(3, (near_a23, 0), (far_a23, 2 * half)),
-        f0.passed(0, (far_f0, 0)),
-        [a1.slot(2), a0.slot(2), a1.slot(1), a0.slot(1)],
+        f0.passed(0, (far_f0_a1, 0)) + a1.passed(0, (far_f0_a1, piece)),
+        [a0.slot(2), a0.slot(1)],
         name="mix_13",
     )
     a_done2, near, far, small = sync(a_done2, near, far, small)
-    a_done2, near_f0, far_a10 = moves.hand_on(a_done2), moves.near(near), moves.far(far)
+    a_done2, near_f0_a1, far_a0 = moves.hand_on(a_done2), moves.near(near), moves.far(far)
     small = small_step(small)
-    a_done2, near_f0, far_a10, small = sync(a_done2, near_f0, far_a10, small)
+    a_done2, near_f0_a1, far_a0, small = sync(a_done2, near_f0_a1, far_a0, small)
 
     a_for_one, a_for_three = split(a_done2)
-    arrived = ((near_f0, 0), (far_f0, piece), (done1, 0), (done3, 0))
+    arrived = ((near_f0_a1, 0), (far_f0_a1, wide), (done1, 0), (done3, 0))
     (ffn_final,) = mix(f0.passed(3, *arrived), name="mix_14")
     if dp_size > 8:
         ffn_final = over_rest(ffn_final, dp_size)
-    a_done3, near = mix(
+    a_done3, a_done1, near = mix(
         a3.passed(3, (near_a23, half), (far_a23, 3 * half), (a_for_three, 0)),
-        a1.passed(0, (far_a10, 0)) + a0.passed(0, (far_a10, half)) + [Block(ffn_final)],
+        a1.passed(3, (near_f0_a1, piece), (far_f0_a1, wide + piece), (a_for_one, 0)),
+        a0.passed(0, (far_a0, 0)) + [Block(ffn_final)],
         name="mix_15",
     )
-    ffn_final, near, a_done3, small = sync(ffn_final, near, a_done3, small)
-    near_a10_f, ffn_over, a_done3 = moves.near(near), moves.far(ffn_final), moves.give(a_done3, 3)
+    ffn_final, near, a_done3, a_done1, small = sync(ffn_final, near, a_done3, a_done1, small)
+    near_a0_f, ffn_over = moves.near(near), moves.far(ffn_final)
+    a_done3, a_done1 = moves.give(a_done3, 3), moves.give(a_done1, 1)
     small = small_step(small)
-    near_a10_f, ffn_over, a_done3, small = sync(near_a10_f, ffn_over, a_done3, small)
-
-    a_done1, far = mix(
-        a1.passed(3, (near_a10_f, 0), (far_a10, 2 * half), (a_for_one, 0)),
-        [Block(near_a10_f, 2 * half, piece)],
-        name="mix_16",
-    )
-    a_done1, far, small = sync(a_done1, far, small)
-    ffn_corner, a_done1 = moves.far(far), moves.give(a_done1, 1)
-    small = small_step(small)
-    ffn_corner, a_done1, small = sync(ffn_corner, a_done1, small)
-
-    own_ffn = (Block(ffn_final), Block(near_a10_f, 2 * half, piece), Block(ffn_over), Block(ffn_corner))
-    arrived = ((near_a10_f, half), (far_a10, 3 * half), (a_done1, 0), (a_done3, 0))
-    attn_final, other_ffn = mix(a0.passed(3, *arrived), own_ffn, name="mix_18")
+    near_a0_f, ffn_over, a_done3, a_done1, small = sync(near_a0_f, ffn_over, a_done3, a_done1, small)
+
+    arrived = ((near_a0_f, 0), (far_a0, half), (a_done1, 0), (a_done3, 0))
+    (attn_final,) = mix(a0.passed(3, *arrived), name="mix_16")
     if dp_size > 8:
         attn_final = over_rest(attn_final, dp_size)
-    attn_final, other_ffn, small = sync(attn_final, other_ffn, small)
-    attn_near, attn_over, other_ffn = moves.near(attn_final), moves.far(attn_final), moves.core(other_ffn)
+    (far,) = mix([Block(near_a0_f, half, piece), Block(attn_final)], name="mix_17")
+    attn_final, far, small = sync(attn_final, far, small)
+    attn_near, far_f_a = moves.near(attn_final), moves.far(far)
+    small = small_step(small)
+    attn_near, far_f_a, small = sync(attn_near, far_f_a, small)
+
+    own_ffn = (Block(ffn_final), Block(near_a0_f, half, piece), Block(ffn_over), Block(far_f_a, 0, piece))
+    (other_ffn,) = mix(own_ffn, name="mix_18")
+    attn_near, other_ffn, small = sync(attn_near, other_ffn, small)
+    other_ffn = moves.core(other_ffn)
     while flips:
         small = small_step(small)
-    attn_near, attn_over, other_ffn, small = sync(attn_near, attn_over, other_ffn, small)
-
     attn_corner = moves.far(attn_near)
 
     def out(kernel, rows_in, own, other, outs, name):
@@ -968,7 +987,7 @@
     outs = [shape(model, hidden), shape(hidden, model)]
     grad_w_in, grad_w_back = out(ffn_out_kernel, piece, own_ffn, other_ffn, outs, "ffn_out")
     attn_corner, grad_w_in, grad_w_back, small = sync(attn_corner, grad_w_in, grad_w_back, small)
-    own_attn = tuple(map(Block, (attn_final, attn_near, attn_over, attn_corner)))
+    own_attn = (Block(attn_final), Block(attn_near), Block(far_f_a, piece, half), Block(attn_corner))
     (other_attn,) = mix(own_attn, name="mix_17")
     other_attn = moves.core(other_attn)
     attn_grads = out(attn_out_kernel, half, own_attn, other_attn, [shape(width, model)] * 4, "attn_out")

time: 215 us -> 208 us (0.967)
  waiting for transfers between devices: 93.1 us -> 87.7 us
  starting transfers between devices: 51.4 us -> 48.6 us
    ppermute x58 -> x57, waiting for transfers between devices: 93.1 us -> 87.7 us  [build(): return lax.ppermute(value, AXES, pairs)]
    ppermute x58 -> x57, starting transfers between devices: 51.4 us -> 48.6 us  [build(): return lax.ppermute(value, AXES, pairs)]
    pallas_call x40 -> x41, Pallas kernels: 62.8 us -> 64.6 us  [call(): pl.pallas_call(kernel, in_specs=[spec for _, spec in ins], out_specs=[VME...]
  transfers between devices with their start and end apart: 58 -> 57, of which waited for: 32 -> 32; matrix products, arithmetic and copies ran while one was open for 1% -> 1% of each run, Pallas kernels for 22% -> 24%
where the time goes in v4:
time: 208 us; the launch traced here: 204 us
  waiting for transfers between devices  87.7 us (42%)
  Pallas kernels  64.6 us (31%)
  starting transfers between devices  48.6 us (23%)
  local copies, waits for them, and re-layouts  2.12 us (1%)
    ppermute x57, waiting for transfers between devices, build(): return lax.ppermute(value, AXES, pairs)  87.7 us
    pallas_call x41, Pallas kernels, call(): pl.pallas_call(kernel, in_specs=[spec for _, spec in ins], out_specs=[VME...  64.6 us
    ppermute x57, starting transfers between devices, build(): return lax.ppermute(value, AXES, pairs)  48.6 us
  transfers between devices with their start and end apart: 57, of which 32 were waited for; matrix products, arithmetic and copies ran while one was open for 1% of the time, Pallas kernels for 24%

profile of v4, /device:TPU:0, one launch (start us, length us, event | category | flops | bytes accessed | tf_op | source)
XLA Modules:
  0.0 204.5 jit_solution(3613519176293747976)
XLA Ops:
  3.1 5.1 %collective-permute-start = (bf16[112,768]{1,0:T(8,128)(2,1)}, bf16[112,768]{1,0:T(8,128)(2,1)S(1)}, u32[]{:S(2)}, u32[]{:S(2)}) collective-permute-start(bf16[112,768]{1,0:T(8,128)(2,1)} %get-tuple-element.239), channel_id=1, source_target_pairs={{1,0},{2,1},{3,2},{0,3},{5,4},{6,5},{7,6},{4,7},{9,8},{10,9},{11,1... | collective-permute-start | bytes 516104 | tf_op jit(solution)/shard_map/ppermute | solution.py:30
  21.5 5.0 %collective-permute-done.2.refs_0_ = bf16[112,768]{1,0:T(8,128)(2,1)S(1)} collective-permute-done((bf16[112,768]{1,0:T(8,128)(2,1)S(1)}, bf16[112,768]{1,0:T(8,128)(2,1)S(1)}, u32[]{:S(2)}, u32[]{:S(2)}) %collective-permute-start.2) | collective-permute-done | bytes 172064 | tf_op jit(solution)/shard_map/ppermute | solution.py:30
  29.9 4.9 %collective-permute-done.6.refs_0_.refs_3_.refs_2_ = bf16[96,768]{1,0:T(8,128)(2,1)S(1)} collective-permute-done((bf16[96,768]{1,0:T(8,128)(2,1)S(1)}, bf16[96,768]{1,0:T(8,128)(2,1)S(1)}, u32[]{:S(2)}, u32[]{:S(2)}) %collective-permute-start.6) | collective-permute-done | bytes 147488 | tf_op jit(solution)/shard_map/ppermute | solution.py:30
  39.0 8.9 %collective-permute-done.8.other.refs_1_.refs_0_ = bf16[192,768]{1,0:T(8,128)(2,1)S(1)} collective-permute-done((bf16[192,768]{1,0:T(8,128)(2,1)S(1)}, bf16[192,768]{1,0:T(8,128)(2,1)S(1)}, u32[]{:S(2)}, u32[]{:S(2)}) %collective-permute-start.8) | collective-permute-done | bytes 294944 | tf_op jit(solution)/shard_map/ppermute | solution.py:30
  48.7 2.9 %collective-permute-start.12 = (bf16[192,768]{1,0:T(8,128)(2,1)S(1)}, bf16[192,768]{1,0:T(8,128)(2,1)S(1)}, u32[]{:S(2)}, u32[]{:S(2)}) collective-permute-start(bf16[192,768]{1,0:T(8,128)(2,1)S(1)} %pick.3), channel_id=1, source_target_pairs={{1,0},{2,1},{3,2},{0,3},{7,4},{4,5},{5,6},{6,7},{9,8},{10,9},{11,1... | collective-permute-start | bytes 884744 | tf_op jit(solution)/shard_map/ppermute | solution.py:30
  52.1 7.4 %attn_13.1 = (bf16[576,512]{1,0:T(8,128)(2,1)S(1)}, bf16[12,128,128]{2,1,0:T(8,128)(2,1)S(1)}, bf16[192,512]{1,0:T(8,128)(2,1)S(1)}, f32[8,768]{1,0:T(8,128)S(1)...) custom-call(s32[16]{0:T(128)S(1)} %copy-done.11, ...), custom_call_target="tpu_custom_call" | custom-call | flops 12079595 | bytes 115753 | tf_op jit(solution)/shard_map/attn_13/pallas_call | solution.py:543
  63.1 4.5 %attn_2.1 = (bf16[576,512]{1,0:T(8,128)(2,1)S(1)}, bf16[12,128,128]{2,1,0:T(8,128)(2,1)S(1)}, bf16[192,512]{1,0:T(8,128)(2,1)S(1)}, f32[8,768]{1,0:T(8,128)S(1)}...) custom-call(s32[16]{0:T(128)S(1)} %copy-done.11, ...), custom_call_target="tpu_custom_call" | custom-call | flops 6039797 | bytes 93307 | tf_op jit(solution)/shard_map/attn_2/pallas_call | solution.py:543
  71.6 2.8 %collective-permute-done.17.refs_3_.refs_2_.refs_5_ = bf16[384,768]{1,0:T(8,128)(2,1)S(1)} collective-permute-done((bf16[384,768]{1,0:T(8,128)(2,1)S(1)}, bf16[384,768]{1,0:T(8,128)(2,1)S(1)}, u32[]{:S(2)}, u32[]{:S(2)}) %collective-permute-start.17) | collective-permute-done | bytes 589856 | tf_op jit(solution)/shard_map/ppermute | solution.py:30
  77.5 3.8 %collective-permute-done.19.refs_3_.refs_6_ = bf16[192,768]{1,0:T(8,128)(2,1)S(1)} collective-permute-done((bf16[192,768]{1,0:T(8,128)(2,1)S(1)}, bf16[192,768]{1,0:T(8,128)(2,1)S(1)}, u32[]{:S(2)}, u32[]{:S(2)}) %collective-permute-start.19) | collective-permute-done | bytes 294944 | tf_op jit(solution)/shard_map/ppermute | solution.py:30
  84.3 4.6 %ffn_2.1 = (bf16[512,768]{1,0:T(8,128)(2,1)S(1)}, bf16[512,768]{1,0:T(8,128)(2,1)S(1)}, bf16[1536,768]{1,0:T(8,128)(2,1)S(1)}, bf16[512,768]{1,0:T(8,128)(2,1)},...) custom-call(bf16[512,768]{1,0:T(8,128)(2,1)S(1)} %get-tuple-element.271.normed, ...), custom_call_target="tpu_custom_call" | custom-call | flops 12079595 | bytes 145244 | tf_op jit(solution)/shard_map/ffn_2/pallas_call | solution.py:543
  89.0 3.0 %ffn_back_2.1 = (bf16[768,768]{1,0:T(8,128)(2,1)S(1)}, bf16[768,768]{1,0:T(8,128)(2,1)S(1)}, f32[512,768]{1,0:T(8,128)S(1)}, f32[8,768]{1,0:T(8,128)S(1)}) custom-call(bf16[512,768]{1,0:T(8,128)(2,1)S(1)} %get-tuple-element.292.grad_low, bf16[512,768]{1,0:T(8,128)(2,1)S(1)} %get-tuple-element.271.normed, f32[512,768]{1,0:T(8,128)S(1)} %get-tuple-element.293.part, ...), custom_call_target="tpu_custom_call" | custom-call | flops 24159192 | bytes 110346 | tf_op jit(solution)/shard_map/ffn_back_2/pallas_call | solution.py:543
  92.3 3.0 %ffn_back_1.1 = (bf16[768,768]{1,0:T(8,128)(2,1)S(1)}, bf16[768,768]{1,0:T(8,128)(2,1)S(1)}, f32[512,768]{1,0:T(8,128)S(1)}, f32[8,768]{1,0:T(8,128)S(1)}) custom-call(bf16[512,768]{1,0:T(8,128)(2,1)S(1)} %get-tuple-element.292.grad_low, bf16[512,768]{1,0:T(8,128)(2,1)S(1)} %get-tuple-element.271.normed, f32[512,768]{1,0:T(8,128)S(1)} %get-tuple-element.297.part, ...), custom_call_target="tpu_custom_call" | custom-call | flops 24159192 | bytes 110346 | tf_op jit(solution)/shard_map/ffn_back_1/pallas_call | solution.py:543
  96.1 6.1 %ffn_back_30.1 = (bf16[768,768]{1,0:T(8,128)(2,1)S(1)}, bf16[768,768]{1,0:T(8,128)(2,1)S(1)}, bf16[1536,768]{1,0:T(8,128)(2,1)S(1)}, f32[512,768]{1,0:T(8,128)S(1)}, f32[8,768]{1,0:T(8,128)S(1)}) custom-call(bf16[512,768]{1,0:T(8,128)(2,1)S(1)} %get-tuple-element.292.grad_low, bf16[512,768]{1,0:T(8,128)(2,1)S(1)} %get-tuple-element.271.normed, ...), custom_call_target="tpu_custom_call" | custom-call | flops 48318384 | bytes 173260 | tf_op jit(solution)/shard_map/ffn_back_30/pallas_call | solution.py:543
  102.3 3.4 %collective-permute-done.23.refs_2_.refs_3_ = bf16[384,768]{1,0:T(8,128)(2,1)S(1)} collective-permute-done((bf16[384,768]{1,0:T(8,128)(2,1)S(1)}, bf16[384,768]{1,0:T(8,128)(2,1)S(1)}, u32[]{:S(2)}, u32[]{:S(2)}) %collective-permute-start.23) | collective-permute-done | bytes 589856 | tf_op jit(solution)/shard_map/ppermute | solution.py:30
  107.6 6.9 %attn_back_23.1 = (bf16[384,768]{1,0:T(8,128)(2,1)S(1)}, bf16[384,768]{1,0:T(8,128)(2,1)S(1)}, bf16[768,768]{1,0:T(8,128)(2,1)S(1)}, f32[512,768]{1,0:T(8,128)S(...) custom-call(bf16[512,768]{1,0:T(8,128)(2,1)S(1)} %get-tuple-element.245.mixed, ...), custom_call_target="tpu_custom_call" | custom-call | flops 24159192 | bytes 137052 | tf_op jit(solution)/shard_map/attn_back_23/pallas_call | solution.py:543
  116.3 2.8 %collective-permute-done.26.refs_6_.refs_3_ = bf16[384,768]{1,0:T(8,128)(2,1)S(1)} collective-permute-done((bf16[384,768]{1,0:T(8,128)(2,1)S(1)}, bf16[384,768]{1,0:T(8,128)(2,1)S(1)}, u32[]{:S(2)}, u32[]{:S(2)}) %collective-permute-start.26) | collective-permute-done | bytes 589856 | tf_op jit(solution)/shard_map/ppermute | solution.py:30
  122.3 2.9 %attn_back_1.1 = (bf16[384,768]{1,0:T(8,128)(2,1)S(1)}, bf16[384,768]{1,0:T(8,128)(2,1)S(1)}, f32[512,768]{1,0:T(8,128)S(1)}, f32[8,768]{1,0:T(8,128)S(1)}) custom-call(bf16[512,768]{1,0:T(8,128)(2,1)S(1)} %get-tuple-element.245.mixed, f32[512,768]{1,0:T(8,128)S(1)} %get-tuple-element.353.part, bf16[512,768]{1,0:T(8,128)(2,1)S(1)} %get-tuple-element.354.refs_0_, ...), custom_call_target="tpu_custom_call" | custom-call | flops 12079595 | bytes 82821 | tf_op jit(solution)/shard_map/attn_back_1/pallas_call | solution.py:543
  125.2 4.7 %collective-permute-done.28.refs_2_ = bf16[192,768]{1,0:T(8,128)(2,1)S(1)} collective-permute-done((bf16[192,768]{1,0:T(8,128)(2,1)S(1)}, bf16[192,768]{1,0:T(8,128)(2,1)S(1)}, u32[]{:S(2)}, u32[]{:S(2)}) %collective-permute-start.28) | collective-permute-done | bytes 294944 | tf_op jit(solution)/shard_map/ppermute | solution.py:30
  136.1 4.3 %attn_back_0.1 = (bf16[384,768]{1,0:T(8,128)(2,1)S(1)}, bf16[384,768]{1,0:T(8,128)(2,1)S(1)}, bf16[512,768]{1,0:T(8,128)(2,1)}, f32[8,768]{1,0:T(8,128)S(1)}) custom-call(bf16[512,768]{1,0:T(8,128)(2,1)S(1)} %get-tuple-element.245.mixed, f32[512,768]{1,0:T(8,128)S(1)} %get-tuple-element.377.part, bf16[512,768]{1,0:T(8,128)(2,1)S(1)} %get-tuple-element.354.refs_0_, ...), custom_call_target="tpu_custom_call" | custom-call | flops 12079595 | bytes 74958 | tf_op jit(solution)/shard_map/attn_back_0/pallas_call | solution.py:543
  140.4 3.1 %collective-permute-done.32.refs_2_ = bf16[192,768]{1,0:T(8,128)(2,1)S(1)} collective-permute-done((bf16[192,768]{1,0:T(8,128)(2,1)S(1)}, bf16[192,768]{1,0:T(8,128)(2,1)S(1)}, u32[]{:S(2)}, u32[]{:S(2)}) %collective-permute-start.32) | collective-permute-done | bytes 294944 | tf_op jit(solution)/shard_map/ppermute | solution.py:30
  153.1 7.7 %collective-permute-done.41 = f32[16,768]{1,0:T(8,128)S(1)} collective-permute-done((f32[16,768]{1,0:T(8,128)S(1)}, f32[16,768]{1,0:T(8,128)S(1)}, u32[]{:S(2)}, u32[]{:S(2)}) %collective-permute-start.41) | collective-permute-done | bytes 49184 | tf_op jit(solution)/shard_map/ppermute | solution.py:30
  167.6 7.5 %collective-permute-done.45 = f32[16,768]{1,0:T(8,128)S(1)} collective-permute-done((f32[16,768]{1,0:T(8,128)S(1)}, f32[16,768]{1,0:T(8,128)S(1)}, u32[]{:S(2)}, u32[]{:S(2)}) %collective-permute-start.45) | collective-permute-done | bytes 49184 | tf_op jit(solution)/shard_map/ppermute | solution.py:30
  179.4 6.5 %collective-permute-done.50 = f32[16,768]{1,0:T(8,128)S(1)} collective-permute-done((f32[16,768]{1,0:T(8,128)S(1)}, f32[16,768]{1,0:T(8,128)S(1)}, u32[]{:S(2)}, u32[]{:S(2)}) %collective-permute-start.50) | collective-permute-done | bytes 49184 | tf_op jit(solution)/shard_map/ppermute | solution.py:30
  189.4 5.2 %collective-permute-done.53 = f32[16,768]{1,0:T(8,128)S(1)} collective-permute-done((f32[16,768]{1,0:T(8,128)S(1)}, f32[16,768]{1,0:T(8,128)S(1)}, u32[]{:S(2)}, u32[]{:S(2)}) %collective-permute-start.53) | collective-permute-done | bytes 49184 | tf_op jit(solution)/shard_map/ppermute | solution.py:30
  (168 shorter events, 86.2 us)
Async XLA Ops:
  3.1 10.8 %collective-permute-start = (bf16[112,768]{1,0:T(8,128)(2,1)}, bf16[112,768]{1,0:T(8,128)(2,1)S(1)}, u32[]{:S(2)}, u32[]{:S(2)}) collective-permute-start(bf16[112,768]{1,0:T(8,128)(2,1)} %get-tuple-element.239), channel_id=1, source_target_pairs={{1,0},{2,1},{3,2},{0,3},{5,4},{6,5},{7,6},{4,7},{9,8},{10,9},{11,1... | collective-permute-start | bytes 516104 | tf_op jit(solution)/shard_map/ppermute | solution.py:30
  36.3 11.6 %collective-permute-start.11 = (bf16[768,768]{1,0:T(8,128)(2,1)S(1)}, bf16[768,768]{1,0:T(8,128)(2,1)S(1)}, u32[]{:S(2)}, u32[]{:S(2)}) collective-permute-start(bf16[768,768]{1,0:T(8,128)(2,1)S(1)} %get-tuple-element.260), channel_id=1, source_target_pairs={{4,0},{5,1},{6,2},{7,3},{0,4},{1,5},{2,6},{3,7},{12,8},{13,9},{14,... | collective-permute-start | bytes 3538952 | tf_op jit(solution)/shard_map/ppermute | solution.py:30
  36.4 11.5 %collective-permute-start.10 = (bf16[288,768]{1,0:T(8,128)(2,1)S(1)}, bf16[288,768]{1,0:T(8,128)(2,1)S(1)}, u32[]{:S(2)}, u32[]{:S(2)}) collective-permute-start(bf16[288,768]{1,0:T(8,128)(2,1)S(1)} %get-tuple-element.259), channel_id=1, source_target_pairs={{16,0},{17,1},{18,2},{19,3},{12,4},{13,5},{14,6},{15,7},{24,8},{25... | collective-permute-start | bytes 1327112 | tf_op jit(solution)/shard_map/ppermute | solution.py:30
  36.7 11.1 %collective-permute-start.8 = (bf16[192,768]{1,0:T(8,128)(2,1)S(1)}, bf16[192,768]{1,0:T(8,128)(2,1)S(1)}, u32[]{:S(2)}, u32[]{:S(2)}) collective-permute-start(bf16[192,768]{1,0:T(8,128)(2,1)S(1)} %copy-done.14), channel_id=1, source_target_pairs={{3,0},{0,1},{1,2},{2,3},{7,4},{4,5},{5,6},{6,7},{11,8},{8,9},{9,10... | collective-permute-start | bytes 884744 | tf_op jit(solution)/shard_map/ppermute | solution.py:30
  48.0 13.1 %collective-permute-start.14 = (bf16[384,768]{1,0:T(8,128)(2,1)S(1)}, bf16[384,768]{1,0:T(8,128)(2,1)S(1)}, u32[]{:S(2)}, u32[]{:S(2)}) collective-permute-start(bf16[384,768]{1,0:T(8,128)(2,1)S(1)} %get-tuple-element.264), channel_id=1, source_target_pairs={{16,0},{17,1},{18,2},{19,3},{12,4},{13,5},{14,6},{15,7},{24,8},{25... | collective-permute-start | bytes 1769480 | tf_op jit(solution)/shard_map/ppermute | solution.py:30
  48.4 12.8 %collective-permute-start.15 = (bf16[384,768]{1,0:T(8,128)(2,1)S(1)}, bf16[384,768]{1,0:T(8,128)(2,1)S(1)}, u32[]{:S(2)}, u32[]{:S(2)}) collective-permute-start(bf16[384,768]{1,0:T(8,128)(2,1)S(1)} %get-tuple-element.265), channel_id=1, source_target_pairs={{4,0},{5,1},{6,2},{7,3},{0,4},{1,5},{2,6},{3,7},{12,8},{13,9},{14,... | collective-permute-start | bytes 1769480 | tf_op jit(solution)/shard_map/ppermute | solution.py:30
  48.7 10.8 %collective-permute-start.12 = (bf16[192,768]{1,0:T(8,128)(2,1)S(1)}, bf16[192,768]{1,0:T(8,128)(2,1)S(1)}, u32[]{:S(2)}, u32[]{:S(2)}) collective-permute-start(bf16[192,768]{1,0:T(8,128)(2,1)S(1)} %pick.3), channel_id=1, source_target_pairs={{1,0},{2,1},{3,2},{0,3},{7,4},{4,5},{5,6},{6,7},{9,8},{10,9},{11,1... | collective-permute-start | bytes 884744 | tf_op jit(solution)/shard_map/ppermute | solution.py:30
  61.2 13.1 %collective-permute-start.18 = (bf16[768,768]{1,0:T(8,128)(2,1)S(1)}, bf16[768,768]{1,0:T(8,128)(2,1)S(1)}, u32[]{:S(2)}, u32[]{:S(2)}) collective-permute-start(bf16[768,768]{1,0:T(8,128)(2,1)S(1)} %get-tuple-element.276), channel_id=1, source_target_pairs={{4,0},{5,1},{6,2},{7,3},{0,4},{1,5},{2,6},{3,7},{12,8},{13,9},{14,... | collective-permute-start | bytes 3538952 | tf_op jit(solution)/shard_map/ppermute | solution.py:30
  61.3 13.0 %collective-permute-start.17 = (bf16[384,768]{1,0:T(8,128)(2,1)S(1)}, bf16[384,768]{1,0:T(8,128)(2,1)S(1)}, u32[]{:S(2)}, u32[]{:S(2)}) collective-permute-start(bf16[384,768]{1,0:T(8,128)(2,1)S(1)} %get-tuple-element.275), channel_id=1, source_target_pairs={{16,0},{17,1},{18,2},{19,3},{12,4},{13,5},{14,6},{15,7},{24,8},{25... | collective-permute-start | bytes 1769480 | tf_op jit(solution)/shard_map/ppermute | solution.py:30
  95.4 10.2 %collective-permute-start.24 = (bf16[768,768]{1,0:T(8,128)(2,1)S(1)}, bf16[768,768]{1,0:T(8,128)(2,1)S(1)}, u32[]{:S(2)}, u32[]{:S(2)}) collective-permute-start(bf16[768,768]{1,0:T(8,128)(2,1)S(1)} %get-tuple-element.310), channel_id=1, source_target_pairs={{4,0},{5,1},{6,2},{7,3},{0,4},{1,5},{2,6},{3,7},{12,8},{13,9},{14,... | collective-permute-start | bytes 3538952 | tf_op jit(solution)/shard_map/ppermute | solution.py:30
  105.9 13.2 %collective-permute-start.27 = (bf16[1536,768]{1,0:T(8,128)(2,1)S(1)}, bf16[1536,768]{1,0:T(8,128)(2,1)S(1)}, u32[]{:S(2)}, u32[]{:S(2)}) collective-permute-start(bf16[1536,768]{1,0:T(8,128)(2,1)S(1)} %get-tuple-element.327), channel_id=1, source_target_pairs={{4,0},{5,1},{6,2},{7,3},{0,4},{1,5},{2,6},{3,7},{12,8},{13,9},{14,... | collective-permute-start | bytes 7077896 | tf_op jit(solution)/shard_map/ppermute | solution.py:30
  106.0 13.1 %collective-permute-start.26 = (bf16[384,768]{1,0:T(8,128)(2,1)S(1)}, bf16[384,768]{1,0:T(8,128)(2,1)S(1)}, u32[]{:S(2)}, u32[]{:S(2)}) collective-permute-start(bf16[384,768]{1,0:T(8,128)(2,1)S(1)} %get-tuple-element.326), channel_id=1, source_target_pairs={{16,0},{17,1},{18,2},{19,3},{12,4},{13,5},{14,6},{15,7},{24,8},{25... | collective-permute-start | bytes 1769480 | tf_op jit(solution)/shard_map/ppermute | solution.py:30
  119.5 13.2 %collective-permute-start.30 = (bf16[768,768]{1,0:T(8,128)(2,1)S(1)}, bf16[768,768]{1,0:T(8,128)(2,1)S(1)}, u32[]{:S(2)}, u32[]{:S(2)}) collective-permute-start(bf16[768,768]{1,0:T(8,128)(2,1)S(1)} %get-tuple-element.351), channel_id=1, source_target_pairs={{4,0},{5,1},{6,2},{7,3},{0,4},{1,5},{2,6},{3,7},{12,8},{13,9},{14,... | collective-permute-start | bytes 3538952 | tf_op jit(solution)/shard_map/ppermute | solution.py:30
  119.5 13.1 %collective-permute-start.29 = (bf16[384,768]{1,0:T(8,128)(2,1)S(1)}, bf16[384,768]{1,0:T(8,128)(2,1)S(1)}, u32[]{:S(2)}, u32[]{:S(2)}) collective-permute-start(bf16[384,768]{1,0:T(8,128)(2,1)S(1)} %get-tuple-element.350), channel_id=1, source_target_pairs={{16,0},{17,1},{18,2},{19,3},{12,4},{13,5},{14,6},{15,7},{24,8},{25... | collective-permute-start | bytes 1769480 | tf_op jit(solution)/shard_map/ppermute | solution.py:30
  133.1 13.2 %collective-permute-start.33 = (bf16[384,768]{1,0:T(8,128)(2,1)S(1)}, bf16[384,768]{1,0:T(8,128)(2,1)S(1)}, u32[]{:S(2)}, u32[]{:S(2)}) collective-permute-start(bf16[384,768]{1,0:T(8,128)(2,1)S(1)} %get-tuple-element.374), channel_id=1, source_target_pairs={{16,0},{17,1},{18,2},{19,3},{12,4},{13,5},{14,6},{15,7},{24,8},{25... | collective-permute-start | bytes 1769480 | tf_op jit(solution)/shard_map/ppermute | solution.py:30
  133.6 12.7 %collective-permute-start.34 = (bf16[384,768]{1,0:T(8,128)(2,1)S(1)}, bf16[384,768]{1,0:T(8,128)(2,1)S(1)}, u32[]{:S(2)}, u32[]{:S(2)}) collective-permute-start(bf16[384,768]{1,0:T(8,128)(2,1)S(1)} %get-tuple-element.375), channel_id=1, source_target_pairs={{4,0},{5,1},{6,2},{7,3},{0,4},{1,5},{2,6},{3,7},{12,8},{13,9},{14,... | collective-permute-start | bytes 1769480 | tf_op jit(solution)/shard_map/ppermute | solution.py:30
  134.8 11.5 %collective-permute-start.35 = (bf16[192,768]{1,0:T(8,128)(2,1)S(1)}, bf16[192,768]{1,0:T(8,128)(2,1)S(1)}, u32[]{:S(2)}, u32[]{:S(2)}) collective-permute-start(bf16[192,768]{1,0:T(8,128)(2,1)S(1)} %get-tuple-element.376), channel_id=1, source_target_pairs={{3,0},{0,1},{1,2},{2,3},{7,4},{4,5},{5,6},{6,7},{11,8},{8,9},{9,10... | collective-permute-start | bytes 884744 | tf_op jit(solution)/shard_map/ppermute | solution.py:30
  146.9 16.3 %collective-permute-start.38 = (bf16[576,768]{1,0:T(8,128)(2,1)S(1)}, bf16[576,768]{1,0:T(8,128)(2,1)S(1)}, u32[]{:S(2)}, u32[]{:S(2)}) collective-permute-start(bf16[576,768]{1,0:T(8,128)(2,1)S(1)} %get-tuple-element.406), channel_id=1, source_target_pairs={{16,0},{17,1},{18,2},{19,3},{12,4},{13,5},{14,6},{15,7},{24,8},{25... | collective-permute-start | bytes 2654216 | tf_op jit(solution)/shard_map/ppermute | solution.py:30
  147.3 13.5 %collective-permute-start.39 = (bf16[384,768]{1,0:T(8,128)(2,1)S(1)}, bf16[384,768]{1,0:T(8,128)(2,1)S(1)}, u32[]{:S(2)}, u32[]{:S(2)}) collective-permute-start(bf16[384,768]{1,0:T(8,128)(2,1)S(1)} %get-tuple-element.407), channel_id=1, source_target_pairs={{4,0},{5,1},{6,2},{7,3},{0,4},{1,5},{2,6},{3,7},{12,8},{13,9},{14,... | collective-permute-start | bytes 1769480 | tf_op jit(solution)/shard_map/ppermute | solution.py:30
  147.3 13.5 %collective-permute-start.36 = (bf16[192,768]{1,0:T(8,128)(2,1)S(1)}, bf16[192,768]{1,0:T(8,128)(2,1)S(1)}, u32[]{:S(2)}, u32[]{:S(2)}) collective-permute-start(bf16[192,768]{1,0:T(8,128)(2,1)S(1)} %get-tuple-element.404), channel_id=1, source_target_pairs={{1,0},{2,1},{3,2},{0,3},{5,4},{6,5},{7,6},{4,7},{9,8},{10,9},{11,1... | collective-permute-start | bytes 884744 | tf_op jit(solution)/shard_map/ppermute | solution.py:30
  149.8 11.0 %collective-permute-start.37 = (bf16[192,768]{1,0:T(8,128)(2,1)S(1)}, bf16[192,768]{1,0:T(8,128)(2,1)S(1)}, u32[]{:S(2)}, u32[]{:S(2)}) collective-permute-start(bf16[192,768]{1,0:T(8,128)(2,1)S(1)} %get-tuple-element.405), channel_id=1, source_target_pairs={{8,0},{9,1},{10,2},{11,3},{20,4},{21,5},{22,6},{23,7},{0,8},{1,9},... | collective-permute-start | bytes 884744 | tf_op jit(solution)/shard_map/ppermute | solution.py:30
  163.4 11.7 %collective-permute-start.43 = (bf16[288,768]{1,0:T(8,128)(2,1)S(1)}, bf16[288,768]{1,0:T(8,128)(2,1)S(1)}, u32[]{:S(2)}, u32[]{:S(2)}) collective-permute-start(bf16[288,768]{1,0:T(8,128)(2,1)S(1)} %get-tuple-element.417), channel_id=1, source_target_pairs={{8,0},{9,1},{10,2},{11,3},{20,4},{21,5},{22,6},{23,7},{0,8},{1,9},... | collective-permute-start | bytes 1327112 | tf_op jit(solution)/shard_map/ppermute | solution.py:30
  164.3 10.8 %collective-permute-start.44 = (bf16[192,768]{1,0:T(8,128)(2,1)S(1)}, bf16[192,768]{1,0:T(8,128)(2,1)S(1)}, u32[]{:S(2)}, u32[]{:S(2)}) collective-permute-start(bf16[192,768]{1,0:T(8,128)(2,1)S(1)} %get-tuple-element.418), channel_id=1, source_target_pairs={{16,0},{17,1},{18,2},{19,3},{12,4},{13,5},{14,6},{15,7},{24,8},{25... | collective-permute-start | bytes 884744 | tf_op jit(solution)/shard_map/ppermute | solution.py:30
  175.7 10.5 %collective-permute-start.46 = (bf16[288,768]{1,0:T(8,128)(2,1)S(1)}, bf16[288,768]{1,0:T(8,128)(2,1)S(1)}, u32[]{:S(2)}, u32[]{:S(2)}) collective-permute-start(bf16[288,768]{1,0:T(8,128)(2,1)S(1)} %get-tuple-element.431), channel_id=1, source_target_pairs={{8,0},{9,1},{10,2},{11,3},{20,4},{21,5},{22,6},{23,7},{0,8},{1,9},... | collective-permute-start | bytes 1327112 | tf_op jit(solution)/shard_map/ppermute | solution.py:30
  (48 other events, 348.2 us)

commit v5 on v4

--- a/solution.py
+++ b/solution.py
@@ -350,7 +350,10 @@
     small[3:, :] = jnp.zeros_like(small[3:, :])
 
 
-def ffn_back_kernel(counts, part_rows, grad_low, normed, part, *refs):
+def ffn_back_kernel(counts, late, part_rows, grad_low, normed, *refs):
+    if late is not None:
+        part, refs = refs[0], refs[1:]
+        earlier, refs = refs[: 2 * late], refs[2 * late :]
     turns = []
     for count in counts:
         act, slope, *mats = refs[: 2 + count]
@@ -359,7 +362,10 @@
     kepts, refs = refs[: len(turns)], refs[len(turns) :]
     given, total, bias_grad, whole = refs
     height = 4 * part_rows
-    value = part[...]
+    if late is not None:
+        value = part[...]
+        for index in range(late):
+            value = value + dot_nt(earlier[2 * index][...], earlier[2 * index + 1][:height, :])
     bias_grad[...] = jnp.zeros_like(bias_grad)
     for index, (act, slope, mats) in enumerate(turns):
         if len(mats) == 2:
@@ -371,10 +377,14 @@
         grad_pre = (grad_act * slope[...].astype(F32)).astype(BF)
         bias_grad[index : index + 1, :] = row_sum(grad_pre.astype(F32))
         whole[:height, :] = dot_tn(normed[...], grad_pre).astype(BF)
-        value = value + dot_nt(grad_pre, mat_in)
+        if late is None:
+            total[...] = grad_pre
+        else:
+            value = value + dot_nt(grad_pre, mat_in)
         base = index * 4 * part_rows
         scatter_out(whole, part_rows, kepts[index], given, base, ffn_place(part_rows))
-    total[...] = value
+    if late is not None:
+        total[...] = value
 
 
 def attend_back(width, seq, grad_low, mats, mixed, qkv, soft, ctx, grad_qkv, whole):
@@ -791,18 +801,27 @@
         else:
             (ffn_part,) = others
 
-    def ffn_back(part, *turns_in, name):
+    def ffn_back(*turns_in, part=None, earlier=(), after_this=None, name):
         kinds = tuple(len(turn) - 2 for turn in turns_in)
-        *kepts, given, part, bias = call(
-            functools.partial(ffn_back_kernel, kinds, piece),
-            [(v, VMEM) for v in (grad_low, normed, part)] + [(v, VMEM) for turn in turns_in for v in turn],
+        late = None if part is None else len(earlier)
+        first = grad_low if after_this is None else after(grad_low, after_this)
+        ins = [first, normed]
+        if part is not None:
+            ins += [part] + [v for pair in earlier for v in pair]
+        *kepts, given, total, bias = call(
+            functools.partial(ffn_back_kernel, kinds, late, piece),
+            [(v, VMEM) for v in ins] + [(v, VMEM) for turn in turns_in for v in turn],
             [shape(4 * piece, model, BF)] * len(kinds)
-            + [shape(4 * len(kinds) * piece, model, BF), shape(rows, model), shape(8, model)],
+            + [
+                shape(4 * len(kinds) * piece, model, BF),
+                shape(rows, model, BF if part is None else F32),
+                shape(8, model),
+            ],
             [pltpu.VMEM((2 * model, model), BF)],
             flops=2 * len(kinds) * ffn_flops,
             name=name,
         )
-        return kepts, given, part, bias
+        return kepts, given, total, bias
 
     def attn_back(part, grad_low, *turns_in, own=False, name):
         first = grad_low is None
@@ -844,17 +863,21 @@
         def passed(self, index, *arrived):
             return [self.slot(index) + [Block(array, row, self.rows) for array, row in arrived]]
 
-    (kept2,), given2, part, bias2 = ffn_back(grad_second, ffn_turn(2), name="ffn_back_2")
+    (kept2,), given2, pre2, bias2 = ffn_back(ffn_turn(2), name="ffn_back_2")
     come2 = moves.core(given2)
-    (kept1,), given1, part, bias1 = ffn_back(part, ffn_turn(0), name="ffn_back_1")
-    come2, given1, part = sync(come2, given1, part)
+    (kept1,), given1, pre1, bias1 = ffn_back(ffn_turn(0), after_this=pre2, name="ffn_back_1")
+    come2, given1, pre1 = sync(come2, given1, pre1)
 
     f2 = Slots(kept2, come2)
     (far,) = mix([f2.slot(2), f2.slot(1)], name="mix_8")
-    far, part, given1 = sync(far, part, given1)
+    far, pre1, given1 = sync(far, pre1, given1)
     far_f2, come1 = moves.far(far), moves.core(given1)
     (kept3, kept0), given30, part, bias30 = ffn_back(
-        part, ffn_turn(1), (act_own, slope_own, w_in, w_back), name="ffn_back_30"
+        ffn_turn(1),
+        (act_own, slope_own, w_in, w_back),
+        part=grad_second,
+        earlier=((pre2, ffn_wholes[2]), (pre1, ffn_wholes[0])),
+        name="ffn_back_30",
     )
     far_f2, come1, given30, part = sync(far_f2, come1, given30, part)
 

time: 208 us -> 207 us (level)
  transfers between devices with their start and end apart: 57 -> 57, of which waited for: 32 -> 32; matrix products, arithmetic and copies ran while one was open for 1% -> 1% of each run, Pallas kernels for 24% -> 25%
where the time goes in v5:
time: 207 us; the launch traced here: 204 us
  waiting for transfers between devices  87 us (42%)
  Pallas kernels  64.7 us (31%)
  starting transfers between devices  48.2 us (23%)
  local copies, waits for them, and re-layouts  2.17 us (1%)
    ppermute x57, waiting for transfers between devices, build(): return lax.ppermute(value, AXES, pairs)  87 us
    pallas_call x41, Pallas kernels, call(): pl.pallas_call(kernel, in_specs=[spec for _, spec in ins], out_specs=[VME...  64.7 us
    ppermute x57, starting transfers between devices, build(): return lax.ppermute(value, AXES, pairs)  48.2 us
  transfers between devices with their start and end apart: 57, of which 32 were waited for; matrix products, arithmetic and copies ran while one was open for 1% of the time, Pallas kernels for 25%

profile of v5, /device:TPU:0, one launch (start us, length us, event | category | flops | bytes accessed | tf_op | source)
XLA Modules:
  0.0 203.6 jit_solution(11782093855796228469)
XLA Ops:
  3.1 5.1 %collective-permute-start = (bf16[112,768]{1,0:T(8,128)(2,1)}, bf16[112,768]{1,0:T(8,128)(2,1)S(1)}, u32[]{:S(2)}, u32[]{:S(2)}) collective-permute-start(bf16[112,768]{1,0:T(8,128)(2,1)} %get-tuple-element.240), channel_id=1, source_target_pairs={{1,0},{2,1},{3,2},{0,3},{5,4},{6,5},{7,6},{4,7},{9,8},{10,9},{11,1... | collective-permute-start | bytes 516104 | tf_op jit(solution)/shard_map/ppermute | solution.py:30
  13.9 2.7 %collective-permute-done.1.other.refs_1_ = bf16[112,768]{1,0:T(8,128)(2,1)S(1)} collective-permute-done((bf16[112,768]{1,0:T(8,128)(2,1)}, bf16[112,768]{1,0:T(8,128)(2,1)S(1)}, u32[]{:S(2)}, u32[]{:S(2)}) %collective-permute-start.1) | collective-permute-done | bytes 172064 | tf_op jit(solution)/shard_map/ppermute | solution.py:30
  21.5 5.0 %collective-permute-done.2.refs_0_ = bf16[112,768]{1,0:T(8,128)(2,1)S(1)} collective-permute-done((bf16[112,768]{1,0:T(8,128)(2,1)S(1)}, bf16[112,768]{1,0:T(8,128)(2,1)S(1)}, u32[]{:S(2)}, u32[]{:S(2)}) %collective-permute-start.2) | collective-permute-done | bytes 172064 | tf_op jit(solution)/shard_map/ppermute | solution.py:30
  29.9 4.9 %collective-permute-done.6.refs_0_.refs_3_.refs_2_ = bf16[96,768]{1,0:T(8,128)(2,1)S(1)} collective-permute-done((bf16[96,768]{1,0:T(8,128)(2,1)S(1)}, bf16[96,768]{1,0:T(8,128)(2,1)S(1)}, u32[]{:S(2)}, u32[]{:S(2)}) %collective-permute-start.6) | collective-permute-done | bytes 147488 | tf_op jit(solution)/shard_map/ppermute | solution.py:30
  39.0 8.9 %collective-permute-done.8.other.refs_1_.refs_0_ = bf16[192,768]{1,0:T(8,128)(2,1)S(1)} collective-permute-done((bf16[192,768]{1,0:T(8,128)(2,1)S(1)}, bf16[192,768]{1,0:T(8,128)(2,1)S(1)}, u32[]{:S(2)}, u32[]{:S(2)}) %collective-permute-start.8) | collective-permute-done | bytes 294944 | tf_op jit(solution)/shard_map/ppermute | solution.py:30
  48.7 2.8 %collective-permute-start.12 = (bf16[192,768]{1,0:T(8,128)(2,1)S(1)}, bf16[192,768]{1,0:T(8,128)(2,1)S(1)}, u32[]{:S(2)}, u32[]{:S(2)}) collective-permute-start(bf16[192,768]{1,0:T(8,128)(2,1)S(1)} %pick.3), channel_id=1, source_target_pairs={{1,0},{2,1},{3,2},{0,3},{7,4},{4,5},{5,6},{6,7},{9,8},{10,9},{11,1... | collective-permute-start | bytes 884744 | tf_op jit(solution)/shard_map/ppermute | solution.py:30
  52.1 7.4 %attn_13.1 = (bf16[576,512]{1,0:T(8,128)(2,1)S(1)}, bf16[12,128,128]{2,1,0:T(8,128)(2,1)S(1)}, bf16[192,512]{1,0:T(8,128)(2,1)S(1)}, f32[8,768]{1,0:T(8,128)S(1)...) custom-call(s32[16]{0:T(128)S(1)} %copy-done.21, ...), custom_call_target="tpu_custom_call" | custom-call | flops 12079595 | bytes 115753 | tf_op jit(solution)/shard_map/attn_13/pallas_call | solution.py:553
  63.2 4.5 %attn_2.1 = (bf16[576,512]{1,0:T(8,128)(2,1)S(1)}, bf16[12,128,128]{2,1,0:T(8,128)(2,1)S(1)}, bf16[192,512]{1,0:T(8,128)(2,1)S(1)}, f32[8,768]{1,0:T(8,128)S(1)}...) custom-call(s32[16]{0:T(128)S(1)} %copy-done.21, ...), custom_call_target="tpu_custom_call" | custom-call | flops 6039797 | bytes 93307 | tf_op jit(solution)/shard_map/attn_2/pallas_call | solution.py:553
  71.6 2.9 %collective-permute-done.17.refs_3_.refs_2_.refs_5_ = bf16[384,768]{1,0:T(8,128)(2,1)S(1)} collective-permute-done((bf16[384,768]{1,0:T(8,128)(2,1)S(1)}, bf16[384,768]{1,0:T(8,128)(2,1)S(1)}, u32[]{:S(2)}, u32[]{:S(2)}) %collective-permute-start.17) | collective-permute-done | bytes 589856 | tf_op jit(solution)/shard_map/ppermute | solution.py:30
  77.6 3.8 %collective-permute-done.19.refs_3_.refs_6_ = bf16[192,768]{1,0:T(8,128)(2,1)S(1)} collective-permute-done((bf16[192,768]{1,0:T(8,128)(2,1)S(1)}, bf16[192,768]{1,0:T(8,128)(2,1)S(1)}, u32[]{:S(2)}, u32[]{:S(2)}) %collective-permute-start.19) | collective-permute-done | bytes 294944 | tf_op jit(solution)/shard_map/ppermute | solution.py:30
  81.6 2.6 %ffn_3.1 = (bf16[512,768]{1,0:T(8,128)(2,1)S(1)}, bf16[512,768]{1,0:T(8,128)(2,1)S(1)}, bf16[1536,768]{1,0:T(8,128)(2,1)S(1)}, f32[512,768]{1,0:T(8,128)S(1)}) custom-call(bf16[512,768]{1,0:T(8,128)(2,1)S(1)} %get-tuple-element.272.normed, f32[512,768]{1,0:T(8,128)S(1)} %get-tuple-element.285.part, f32[8,768]{1,0:T(8,128)S(1)} %get-tuple-element.286.bias_in, ...), custom_call_target="tpu_custom_call" | custom-call | flops 12079595 | bytes 108380 | tf_op jit(solution)/shard_map/ffn_3/pallas_call | solution.py:553
  84.4 4.7 %ffn_2.1 = (bf16[512,768]{1,0:T(8,128)(2,1)S(1)}, bf16[512,768]{1,0:T(8,128)(2,1)S(1)}, bf16[1536,768]{1,0:T(8,128)(2,1)S(1)}, bf16[512,768]{1,0:T(8,128)(2,1)},...) custom-call(bf16[512,768]{1,0:T(8,128)(2,1)S(1)} %get-tuple-element.272.normed, ...), custom_call_target="tpu_custom_call" | custom-call | flops 12079595 | bytes 145244 | tf_op jit(solution)/shard_map/ffn_2/pallas_call | solution.py:553
  95.1 7.7 %ffn_back_30.1 = (bf16[768,768]{1,0:T(8,128)(2,1)S(1)}, bf16[768,768]{1,0:T(8,128)(2,1)S(1)}, bf16[1536,768]{1,0:T(8,128)(2,1)S(1)}, f32[512,768]{1,0:T(8,128)S(1)}, f32[8,768]{1,0:T(8,128)S(1)}) custom-call(bf16[512,768]{1,0:T(8,128)(2,1)S(1)} %get-tuple-element.298.grad_low, bf16[512,768]{1,0:T(8,128)(2,1)S(1)} %get-tuple-element.272.normed, ...), custom_call_target="tpu_custom_call" | custom-call | flops 48318384 | bytes 236175 | tf_op jit(solution)/shard_map/ffn_back_30/pallas_call | solution.py:553
  106.6 6.9 %attn_back_23.1 = (bf16[384,768]{1,0:T(8,128)(2,1)S(1)}, bf16[384,768]{1,0:T(8,128)(2,1)S(1)}, bf16[768,768]{1,0:T(8,128)(2,1)S(1)}, f32[512,768]{1,0:T(8,128)S(...) custom-call(bf16[512,768]{1,0:T(8,128)(2,1)S(1)} %get-tuple-element.246.mixed, ...), custom_call_target="tpu_custom_call" | custom-call | flops 24159192 | bytes 137052 | tf_op jit(solution)/shard_map/attn_back_23/pallas_call | solution.py:553
  115.2 2.8 %collective-permute-done.26.refs_6_.refs_3_ = bf16[384,768]{1,0:T(8,128)(2,1)S(1)} collective-permute-done((bf16[384,768]{1,0:T(8,128)(2,1)S(1)}, bf16[384,768]{1,0:T(8,128)(2,1)S(1)}, u32[]{:S(2)}, u32[]{:S(2)}) %collective-permute-start.26) | collective-permute-done | bytes 589856 | tf_op jit(solution)/shard_map/ppermute | solution.py:30
  121.2 2.9 %attn_back_1.1 = (bf16[384,768]{1,0:T(8,128)(2,1)S(1)}, bf16[384,768]{1,0:T(8,128)(2,1)S(1)}, f32[512,768]{1,0:T(8,128)S(1)}, f32[8,768]{1,0:T(8,128)S(1)}) custom-call(bf16[512,768]{1,0:T(8,128)(2,1)S(1)} %get-tuple-element.246.mixed, f32[512,768]{1,0:T(8,128)S(1)} %get-tuple-element.355.part, bf16[512,768]{1,0:T(8,128)(2,1)S(1)} %get-tuple-element.356.refs_0_, ...), custom_call_target="tpu_custom_call" | custom-call | flops 12079595 | bytes 82821 | tf_op jit(solution)/shard_map/attn_back_1/pallas_call | solution.py:553
  124.1 4.7 %collective-permute-done.28.refs_2_ = bf16[192,768]{1,0:T(8,128)(2,1)S(1)} collective-permute-done((bf16[192,768]{1,0:T(8,128)(2,1)S(1)}, bf16[192,768]{1,0:T(8,128)(2,1)S(1)}, u32[]{:S(2)}, u32[]{:S(2)}) %collective-permute-start.28) | collective-permute-done | bytes 294944 | tf_op jit(solution)/shard_map/ppermute | solution.py:30
  135.0 4.3 %attn_back_0.1 = (bf16[384,768]{1,0:T(8,128)(2,1)S(1)}, bf16[384,768]{1,0:T(8,128)(2,1)S(1)}, bf16[512,768]{1,0:T(8,128)(2,1)}, f32[8,768]{1,0:T(8,128)S(1)}) custom-call(bf16[512,768]{1,0:T(8,128)(2,1)S(1)} %get-tuple-element.246.mixed, f32[512,768]{1,0:T(8,128)S(1)} %get-tuple-element.379.part, bf16[512,768]{1,0:T(8,128)(2,1)S(1)} %get-tuple-element.356.refs_0_, ...), custom_call_target="tpu_custom_call" | custom-call | flops 12079595 | bytes 74958 | tf_op jit(solution)/shard_map/attn_back_0/pallas_call | solution.py:553
  139.3 3.2 %collective-permute-done.32.refs_2_ = bf16[192,768]{1,0:T(8,128)(2,1)S(1)} collective-permute-done((bf16[192,768]{1,0:T(8,128)(2,1)S(1)}, bf16[192,768]{1,0:T(8,128)(2,1)S(1)}, u32[]{:S(2)}, u32[]{:S(2)}) %collective-permute-start.32) | collective-permute-done | bytes 294944 | tf_op jit(solution)/shard_map/ppermute | solution.py:30
  142.5 2.8 %collective-permute-done.35.refs_4_ = bf16[192,768]{1,0:T(8,128)(2,1)S(1)} collective-permute-done((bf16[192,768]{1,0:T(8,128)(2,1)S(1)}, bf16[192,768]{1,0:T(8,128)(2,1)S(1)}, u32[]{:S(2)}, u32[]{:S(2)}) %collective-permute-start.35) | collective-permute-done | bytes 294944 | tf_op jit(solution)/shard_map/ppermute | solution.py:30
  152.1 7.7 %collective-permute-done.41 = f32[16,768]{1,0:T(8,128)S(1)} collective-permute-done((f32[16,768]{1,0:T(8,128)S(1)}, f32[16,768]{1,0:T(8,128)S(1)}, u32[]{:S(2)}, u32[]{:S(2)}) %collective-permute-start.41) | collective-permute-done | bytes 49184 | tf_op jit(solution)/shard_map/ppermute | solution.py:30
  166.6 7.5 %collective-permute-done.45 = f32[16,768]{1,0:T(8,128)S(1)} collective-permute-done((f32[16,768]{1,0:T(8,128)S(1)}, f32[16,768]{1,0:T(8,128)S(1)}, u32[]{:S(2)}, u32[]{:S(2)}) %collective-permute-start.45) | collective-permute-done | bytes 49184 | tf_op jit(solution)/shard_map/ppermute | solution.py:30
  178.4 6.5 %collective-permute-done.50 = f32[16,768]{1,0:T(8,128)S(1)} collective-permute-done((f32[16,768]{1,0:T(8,128)S(1)}, f32[16,768]{1,0:T(8,128)S(1)}, u32[]{:S(2)}, u32[]{:S(2)}) %collective-permute-start.50) | collective-permute-done | bytes 49184 | tf_op jit(solution)/shard_map/ppermute | solution.py:30
  188.4 5.2 %collective-permute-done.53 = f32[16,768]{1,0:T(8,128)S(1)} collective-permute-done((f32[16,768]{1,0:T(8,128)S(1)}, f32[16,768]{1,0:T(8,128)S(1)}, u32[]{:S(2)}, u32[]{:S(2)}) %collective-permute-start.53) | collective-permute-done | bytes 49184 | tf_op jit(solution)/shard_map/ppermute | solution.py:30
  (188 shorter events, 84.7 us)
Async XLA Ops:
  3.1 10.8 %collective-permute-start = (bf16[112,768]{1,0:T(8,128)(2,1)}, bf16[112,768]{1,0:T(8,128)(2,1)S(1)}, u32[]{:S(2)}, u32[]{:S(2)}) collective-permute-start(bf16[112,768]{1,0:T(8,128)(2,1)} %get-tuple-element.240), channel_id=1, source_target_pairs={{1,0},{2,1},{3,2},{0,3},{5,4},{6,5},{7,6},{4,7},{9,8},{10,9},{11,1... | collective-permute-start | bytes 516104 | tf_op jit(solution)/shard_map/ppermute | solution.py:30
  36.3 11.6 %collective-permute-start.11 = (bf16[768,768]{1,0:T(8,128)(2,1)S(1)}, bf16[768,768]{1,0:T(8,128)(2,1)S(1)}, u32[]{:S(2)}, u32[]{:S(2)}) collective-permute-start(bf16[768,768]{1,0:T(8,128)(2,1)S(1)} %get-tuple-element.261), channel_id=1, source_target_pairs={{4,0},{5,1},{6,2},{7,3},{0,4},{1,5},{2,6},{3,7},{12,8},{13,9},{14,... | collective-permute-start | bytes 3538952 | tf_op jit(solution)/shard_map/ppermute | solution.py:30
  36.4 11.5 %collective-permute-start.10 = (bf16[288,768]{1,0:T(8,128)(2,1)S(1)}, bf16[288,768]{1,0:T(8,128)(2,1)S(1)}, u32[]{:S(2)}, u32[]{:S(2)}) collective-permute-start(bf16[288,768]{1,0:T(8,128)(2,1)S(1)} %get-tuple-element.260), channel_id=1, source_target_pairs={{16,0},{17,1},{18,2},{19,3},{12,4},{13,5},{14,6},{15,7},{24,8},{25... | collective-permute-start | bytes 1327112 | tf_op jit(solution)/shard_map/ppermute | solution.py:30
  36.8 11.1 %collective-permute-start.8 = (bf16[192,768]{1,0:T(8,128)(2,1)S(1)}, bf16[192,768]{1,0:T(8,128)(2,1)S(1)}, u32[]{:S(2)}, u32[]{:S(2)}) collective-permute-start(bf16[192,768]{1,0:T(8,128)(2,1)S(1)} %copy-done.24), channel_id=1, source_target_pairs={{3,0},{0,1},{1,2},{2,3},{7,4},{4,5},{5,6},{6,7},{11,8},{8,9},{9,10... | collective-permute-start | bytes 884744 | tf_op jit(solution)/shard_map/ppermute | solution.py:30
  48.0 13.1 %collective-permute-start.14 = (bf16[384,768]{1,0:T(8,128)(2,1)S(1)}, bf16[384,768]{1,0:T(8,128)(2,1)S(1)}, u32[]{:S(2)}, u32[]{:S(2)}) collective-permute-start(bf16[384,768]{1,0:T(8,128)(2,1)S(1)} %get-tuple-element.265), channel_id=1, source_target_pairs={{16,0},{17,1},{18,2},{19,3},{12,4},{13,5},{14,6},{15,7},{24,8},{25... | collective-permute-start | bytes 1769480 | tf_op jit(solution)/shard_map/ppermute | solution.py:30
  48.4 12.8 %collective-permute-start.15 = (bf16[384,768]{1,0:T(8,128)(2,1)S(1)}, bf16[384,768]{1,0:T(8,128)(2,1)S(1)}, u32[]{:S(2)}, u32[]{:S(2)}) collective-permute-start(bf16[384,768]{1,0:T(8,128)(2,1)S(1)} %get-tuple-element.266), channel_id=1, source_target_pairs={{4,0},{5,1},{6,2},{7,3},{0,4},{1,5},{2,6},{3,7},{12,8},{13,9},{14,... | collective-permute-start | bytes 1769480 | tf_op jit(solution)/shard_map/ppermute | solution.py:30
  48.7 10.8 %collective-permute-start.12 = (bf16[192,768]{1,0:T(8,128)(2,1)S(1)}, bf16[192,768]{1,0:T(8,128)(2,1)S(1)}, u32[]{:S(2)}, u32[]{:S(2)}) collective-permute-start(bf16[192,768]{1,0:T(8,128)(2,1)S(1)} %pick.3), channel_id=1, source_target_pairs={{1,0},{2,1},{3,2},{0,3},{7,4},{4,5},{5,6},{6,7},{9,8},{10,9},{11,1... | collective-permute-start | bytes 884744 | tf_op jit(solution)/shard_map/ppermute | solution.py:30
  61.3 13.2 %collective-permute-start.18 = (bf16[768,768]{1,0:T(8,128)(2,1)S(1)}, bf16[768,768]{1,0:T(8,128)(2,1)S(1)}, u32[]{:S(2)}, u32[]{:S(2)}) collective-permute-start(bf16[768,768]{1,0:T(8,128)(2,1)S(1)} %get-tuple-element.277), channel_id=1, source_target_pairs={{4,0},{5,1},{6,2},{7,3},{0,4},{1,5},{2,6},{3,7},{12,8},{13,9},{14,... | collective-permute-start | bytes 3538952 | tf_op jit(solution)/shard_map/ppermute | solution.py:30
  61.4 13.1 %collective-permute-start.17 = (bf16[384,768]{1,0:T(8,128)(2,1)S(1)}, bf16[384,768]{1,0:T(8,128)(2,1)S(1)}, u32[]{:S(2)}, u32[]{:S(2)}) collective-permute-start(bf16[384,768]{1,0:T(8,128)(2,1)S(1)} %get-tuple-element.276), channel_id=1, source_target_pairs={{16,0},{17,1},{18,2},{19,3},{12,4},{13,5},{14,6},{15,7},{24,8},{25... | collective-permute-start | bytes 1769480 | tf_op jit(solution)/shard_map/ppermute | solution.py:30
  94.4 10.2 %collective-permute-start.24 = (bf16[768,768]{1,0:T(8,128)(2,1)S(1)}, bf16[768,768]{1,0:T(8,128)(2,1)S(1)}, u32[]{:S(2)}, u32[]{:S(2)}) collective-permute-start(bf16[768,768]{1,0:T(8,128)(2,1)S(1)} %get-tuple-element.311), channel_id=1, source_target_pairs={{4,0},{5,1},{6,2},{7,3},{0,4},{1,5},{2,6},{3,7},{12,8},{13,9},{14,... | collective-permute-start | bytes 3538952 | tf_op jit(solution)/shard_map/ppermute | solution.py:30
  104.9 13.2 %collective-permute-start.27 = (bf16[1536,768]{1,0:T(8,128)(2,1)S(1)}, bf16[1536,768]{1,0:T(8,128)(2,1)S(1)}, u32[]{:S(2)}, u32[]{:S(2)}) collective-permute-start(bf16[1536,768]{1,0:T(8,128)(2,1)S(1)} %get-tuple-element.329), channel_id=1, source_target_pairs={{4,0},{5,1},{6,2},{7,3},{0,4},{1,5},{2,6},{3,7},{12,8},{13,9},{14,... | collective-permute-start | bytes 7077896 | tf_op jit(solution)/shard_map/ppermute | solution.py:30
  104.9 13.1 %collective-permute-start.26 = (bf16[384,768]{1,0:T(8,128)(2,1)S(1)}, bf16[384,768]{1,0:T(8,128)(2,1)S(1)}, u32[]{:S(2)}, u32[]{:S(2)}) collective-permute-start(bf16[384,768]{1,0:T(8,128)(2,1)S(1)} %get-tuple-element.328), channel_id=1, source_target_pairs={{16,0},{17,1},{18,2},{19,3},{12,4},{13,5},{14,6},{15,7},{24,8},{25... | collective-permute-start | bytes 1769480 | tf_op jit(solution)/shard_map/ppermute | solution.py:30
  118.4 13.2 %collective-permute-start.30 = (bf16[768,768]{1,0:T(8,128)(2,1)S(1)}, bf16[768,768]{1,0:T(8,128)(2,1)S(1)}, u32[]{:S(2)}, u32[]{:S(2)}) collective-permute-start(bf16[768,768]{1,0:T(8,128)(2,1)S(1)} %get-tuple-element.353), channel_id=1, source_target_pairs={{4,0},{5,1},{6,2},{7,3},{0,4},{1,5},{2,6},{3,7},{12,8},{13,9},{14,... | collective-permute-start | bytes 3538952 | tf_op jit(solution)/shard_map/ppermute | solution.py:30
  118.5 13.1 %collective-permute-start.29 = (bf16[384,768]{1,0:T(8,128)(2,1)S(1)}, bf16[384,768]{1,0:T(8,128)(2,1)S(1)}, u32[]{:S(2)}, u32[]{:S(2)}) collective-permute-start(bf16[384,768]{1,0:T(8,128)(2,1)S(1)} %get-tuple-element.352), channel_id=1, source_target_pairs={{16,0},{17,1},{18,2},{19,3},{12,4},{13,5},{14,6},{15,7},{24,8},{25... | collective-permute-start | bytes 1769480 | tf_op jit(solution)/shard_map/ppermute | solution.py:30
  132.1 13.2 %collective-permute-start.33 = (bf16[384,768]{1,0:T(8,128)(2,1)S(1)}, bf16[384,768]{1,0:T(8,128)(2,1)S(1)}, u32[]{:S(2)}, u32[]{:S(2)}) collective-permute-start(bf16[384,768]{1,0:T(8,128)(2,1)S(1)} %get-tuple-element.376), channel_id=1, source_target_pairs={{16,0},{17,1},{18,2},{19,3},{12,4},{13,5},{14,6},{15,7},{24,8},{25... | collective-permute-start | bytes 1769480 | tf_op jit(solution)/shard_map/ppermute | solution.py:30
  132.5 12.7 %collective-permute-start.34 = (bf16[384,768]{1,0:T(8,128)(2,1)S(1)}, bf16[384,768]{1,0:T(8,128)(2,1)S(1)}, u32[]{:S(2)}, u32[]{:S(2)}) collective-permute-start(bf16[384,768]{1,0:T(8,128)(2,1)S(1)} %get-tuple-element.377), channel_id=1, source_target_pairs={{4,0},{5,1},{6,2},{7,3},{0,4},{1,5},{2,6},{3,7},{12,8},{13,9},{14,... | collective-permute-start | bytes 1769480 | tf_op jit(solution)/shard_map/ppermute | solution.py:30
  133.8 11.5 %collective-permute-start.35 = (bf16[192,768]{1,0:T(8,128)(2,1)S(1)}, bf16[192,768]{1,0:T(8,128)(2,1)S(1)}, u32[]{:S(2)}, u32[]{:S(2)}) collective-permute-start(bf16[192,768]{1,0:T(8,128)(2,1)S(1)} %get-tuple-element.378), channel_id=1, source_target_pairs={{3,0},{0,1},{1,2},{2,3},{7,4},{4,5},{5,6},{6,7},{11,8},{8,9},{9,10... | collective-permute-start | bytes 884744 | tf_op jit(solution)/shard_map/ppermute | solution.py:30
  145.8 16.3 %collective-permute-start.38 = (bf16[576,768]{1,0:T(8,128)(2,1)S(1)}, bf16[576,768]{1,0:T(8,128)(2,1)S(1)}, u32[]{:S(2)}, u32[]{:S(2)}) collective-permute-start(bf16[576,768]{1,0:T(8,128)(2,1)S(1)} %get-tuple-element.408), channel_id=1, source_target_pairs={{16,0},{17,1},{18,2},{19,3},{12,4},{13,5},{14,6},{15,7},{24,8},{25... | collective-permute-start | bytes 2654216 | tf_op jit(solution)/shard_map/ppermute | solution.py:30
  146.3 13.5 %collective-permute-start.39 = (bf16[384,768]{1,0:T(8,128)(2,1)S(1)}, bf16[384,768]{1,0:T(8,128)(2,1)S(1)}, u32[]{:S(2)}, u32[]{:S(2)}) collective-permute-start(bf16[384,768]{1,0:T(8,128)(2,1)S(1)} %get-tuple-element.409), channel_id=1, source_target_pairs={{4,0},{5,1},{6,2},{7,3},{0,4},{1,5},{2,6},{3,7},{12,8},{13,9},{14,... | collective-permute-start | bytes 1769480 | tf_op jit(solution)/shard_map/ppermute | solution.py:30
  146.3 13.5 %collective-permute-start.36 = (bf16[192,768]{1,0:T(8,128)(2,1)S(1)}, bf16[192,768]{1,0:T(8,128)(2,1)S(1)}, u32[]{:S(2)}, u32[]{:S(2)}) collective-permute-start(bf16[192,768]{1,0:T(8,128)(2,1)S(1)} %get-tuple-element.406), channel_id=1, source_target_pairs={{1,0},{2,1},{3,2},{0,3},{5,4},{6,5},{7,6},{4,7},{9,8},{10,9},{11,1... | collective-permute-start | bytes 884744 | tf_op jit(solution)/shard_map/ppermute | solution.py:30
  148.7 11.0 %collective-permute-start.37 = (bf16[192,768]{1,0:T(8,128)(2,1)S(1)}, bf16[192,768]{1,0:T(8,128)(2,1)S(1)}, u32[]{:S(2)}, u32[]{:S(2)}) collective-permute-start(bf16[192,768]{1,0:T(8,128)(2,1)S(1)} %get-tuple-element.407), channel_id=1, source_target_pairs={{8,0},{9,1},{10,2},{11,3},{20,4},{21,5},{22,6},{23,7},{0,8},{1,9},... | collective-permute-start | bytes 884744 | tf_op jit(solution)/shard_map/ppermute | solution.py:30
  162.4 11.7 %collective-permute-start.43 = (bf16[288,768]{1,0:T(8,128)(2,1)S(1)}, bf16[288,768]{1,0:T(8,128)(2,1)S(1)}, u32[]{:S(2)}, u32[]{:S(2)}) collective-permute-start(bf16[288,768]{1,0:T(8,128)(2,1)S(1)} %get-tuple-element.419), channel_id=1, source_target_pairs={{8,0},{9,1},{10,2},{11,3},{20,4},{21,5},{22,6},{23,7},{0,8},{1,9},... | collective-permute-start | bytes 1327112 | tf_op jit(solution)/shard_map/ppermute | solution.py:30
  163.3 10.8 %collective-permute-start.44 = (bf16[192,768]{1,0:T(8,128)(2,1)S(1)}, bf16[192,768]{1,0:T(8,128)(2,1)S(1)}, u32[]{:S(2)}, u32[]{:S(2)}) collective-permute-start(bf16[192,768]{1,0:T(8,128)(2,1)S(1)} %get-tuple-element.420), channel_id=1, source_target_pairs={{16,0},{17,1},{18,2},{19,3},{12,4},{13,5},{14,6},{15,7},{24,8},{25... | collective-permute-start | bytes 884744 | tf_op jit(solution)/shard_map/ppermute | solution.py:30
  174.6 10.5 %collective-permute-start.46 = (bf16[288,768]{1,0:T(8,128)(2,1)S(1)}, bf16[288,768]{1,0:T(8,128)(2,1)S(1)}, u32[]{:S(2)}, u32[]{:S(2)}) collective-permute-start(bf16[288,768]{1,0:T(8,128)(2,1)S(1)} %get-tuple-element.433), channel_id=1, source_target_pairs={{8,0},{9,1},{10,2},{11,3},{20,4},{21,5},{22,6},{23,7},{0,8},{1,9},... | collective-permute-start | bytes 1327112 | tf_op jit(solution)/shard_map/ppermute | solution.py:30
  (58 other events, 381.5 us)
